TPU v7x, 32 devices: a whole 2x2x4 slice. The times are simulated.
32 devices in a mesh: gx: 8 (over z, x), gy: 4 (over y, core).
Axes of the slice: x: 2, y: 2, z: 4, core: 2. Of those that a mesh axis runs over, the one named last changes fastest.
Arguments:
- inputs: float32 [64, 32, 16, 256], P('gx', 'gy'), may hold values from -6 to 6
- cotangent: float32 [64, 32, 16, 256], P('gx', 'gy'), may hold values from -6 to 6
- weight: float32 [6912, 256], replicated, may hold values from -0.125 to 0.125
- occupancy: int32 [64, 32, 16], P('gx', 'gy'), may hold values from 0 to 1, as said below
Outputs:
- input_grad: float32 [64, 32, 16, 256], P('gx', 'gy')
- weight_grad: float32 [6912, 256], P('gx', 'gy')
Inputs may be any that keep to these rules, and one draw needn't show every extreme that they name: `occupancy`: occupied voxels lie in bricks of 8 x 8 x min(8, 16) voxels aligned to each device's block; some bricks are empty.
All inputs are finite; a program needn't handle non-finite values.
Results may differ from a plain program's by a relative error of at most 0.0001.
Values sent between devices are 32-bit elements; how exact they have to be, the bound alone decides.
No kernel may reach another device: no remote copies, remote signals or barrier semaphores. Data moves between devices by JAX's collectives and lax.ppermute only.
A program may use at most 192 MiB of HBM per device.

v0:
```python
import jax
import jax.numpy as jnp
from jax import lax
from jax.sharding import PartitionSpec as P


def with_halo(array, sides, width):
    for axis, dim in sides:
        devices, length = (lax.axis_size(axis), array.shape[dim])
        up = [(i, (i + 1) % devices) for i in range(devices - 1)]
        down = [(j, i) for i, j in up]
        last = lax.slice_in_dim(array, length - width, length, axis=dim)
        first = lax.slice_in_dim(array, 0, width, axis=dim)
        before = lax.ppermute(last, axis, up)
        after = lax.ppermute(first, axis, down)
        array = jnp.concatenate([before, array, after], axis=dim)
    return array


def offsets():
    return [
        (first, second, third) for first in range(3) for second in range(3) for third in range(3)
    ]


def body(inputs, cotangent, weight, occupancy):
    span_x, span_y, depth, channels = inputs.shape
    count = span_x * span_y * depth
    filled = occupancy.astype(jnp.float32)[..., None]
    masked = inputs * filled
    bordered = with_halo(masked, (("gx", 0), ("gy", 1)), 1)
    padded = jnp.pad(bordered, ((0, 0), (0, 0), (1, 1), (0, 0)))
    preact = jnp.zeros((count, channels), jnp.float32)
    for index, (first, second, third) in enumerate(offsets()):
        piece = padded[
            first : first + span_x, second : second + span_y, third : third + depth
        ].reshape(count, channels)
        preact = preact + jnp.dot(
            piece,
            weight[index * channels : (index + 1) * channels],
            precision=lax.Precision.HIGHEST,
            preferred_element_type=jnp.float32,
        )
    sigma = jax.nn.sigmoid(preact)
    upstream = (
        cotangent.reshape(count, channels)
        * sigma
        * (1.0 + preact * (1.0 - sigma))
        * filled.reshape(count, 1)
    )
    grid_up = upstream.reshape(span_x, span_y, depth, channels)
    border_up = with_halo(grid_up, (("gx", 0), ("gy", 1)), 1)
    border_up = jnp.pad(border_up, ((0, 0), (0, 0), (1, 1), (0, 0)))
    result = jnp.zeros((count, channels), jnp.float32)
    for index, (first, second, third) in enumerate(offsets()):
        kernel = weight[index * channels : (index + 1) * channels]
        back = border_up[
            2 - first : 2 - first + span_x,
            2 - second : 2 - second + span_y,
            2 - third : 2 - third + depth,
        ].reshape(count, channels)
        result = result + jnp.dot(
            back, kernel.T, precision=lax.Precision.HIGHEST, preferred_element_type=jnp.float32
        )
    result = result.reshape(span_x, span_y, depth, channels)
    input_grad = result * filled
    blocks = []
    for index, (first, second, third) in enumerate(offsets()):
        piece = padded[
            first : first + span_x, second : second + span_y, third : third + depth
        ].reshape(count, channels)
        blocks.append(
            jnp.dot(
                piece.T,
                upstream,
                precision=lax.Precision.HIGHEST,
                preferred_element_type=jnp.float32,
            )
        )
    term = jnp.concatenate(blocks, axis=0)
    row_sums = lax.psum_scatter(term, "gx", scatter_dimension=0, tiled=True)
    weight_grad = lax.psum_scatter(row_sums, "gy", scatter_dimension=1, tiled=True)
    return (input_grad, weight_grad)


def solution(mesh):
    in_specs = (P("gx", "gy", None, None), P("gx", "gy", None, None), P(), P("gx", "gy", None))
    out_specs = (P("gx", "gy", None, None), P("gx", "gy"))
    return jax.shard_map(body, mesh=mesh, in_specs=in_specs, out_specs=out_specs, check_vma=False)
```

profile of v0, /device:TPU:0, one launch (start us, length us, event | category | flops | bytes accessed | tf_op | source)
XLA Modules:
  0.0 350.4 jit_solution(3534970052594225115)
XLA Ops:
  9.4 4.8 %collective-permute-start = (f32[1,8,16,256]{3,2,1,0:T(8,128)S(1)}, f32[1,8,16,256]{3,2,1,0:T(8,128)S(1)}, u32[]{:S(2)}, u32[]{:S(2)}) collective-permute-start(f32[1,8,16,256]{3,2,1,0:T(8,128)S(1)} %get-tuple-element.68), channel_id=1, source_target_pairs={{0,4},{4,8},{8,12},{12,16},{16,20},{20,24},{24,28},{1,5},{5,9},{9,... | collective-permute-start | bytes 393224 | tf_op jit(solution)/shard_map/ppermute | solution.py:14
  15.6 2.9 fusion.79
  24.1 3.1 fusion.45
  43.1 6.4 %fusion.134 = (f32[8,8,16,256]{3,2,1,0:T(8,128)}, f32[8,8,16,256]{3,2,1,0:T(8,128)}, f32[8,8,16,256]{3,2,1,0:T(8,128)}, f32[8,8,16,256]{3,2,1,0:T(8,128)}, f32[8...) fusion(f32[10,10,18,256]{3,2,1,0:T(8,128)S(1)} %select_maximum_, ...), kind=kLoop, calls=%fused_computation.190 | loop fusion | bytes 37748736 | tf_op jit(solution)/shard_map/slice | solution.py:35
  49.6 3.6 %fusion.37 = f32[1024,256]{1,0:T(8,128)} fusion(f32[1024,256]{1,0:T(8,128)} %bitcast.191, f32[6912,256]{1,0:T(8,128)S(1)} %copy-done), kind=kOutput, calls=%fused_computation.87 | convolution fusion | flops 805306368 | bytes 2359296 | tf_op jit(solution)/shard_map/dot_general | solution.py:38
  53.1 3.3 fusion.131
  56.5 3.3 fusion.41
  75.6 15.0 %fusion.99 = f32[1024,256]{1,0:T(8,128)} fusion(f32[1024,256]{1,0:T(8,128)S(1)} %bitcast.217, f32[6912,256]{1,0:T(8,128)S(1)} %copy-done), kind=kOutput, calls=%fused_computation.149 | convolution fusion | flops 805306368 | bytes 2359296 | tf_op jit(solution)/shard_map/dot_general | solution.py:38
  100.5 10.3 %fusion.26 = f32[1024,256]{1,0:T(8,128)S(1)} fusion(f32[8,8,16,256]{3,2,1,0:T(8,128)} %param.5, f32[1024,256]{1,0:T(8,128)} %fusion.29, f32[1024,256]{1,0:T(8,128)} %fusion.33, f32[1024,256]{1,0:T(8,128)} %fusion.37, f32[1024,256]{1,0:T(8,128)} %fusion.41, f32[1024,256]{1,0:T(8,128)} %fusion.45, f32[1024,256]{1,0:T(8,128)} %fusion.49, ...), kind=kOutput, calls=%fused_computation.74 | convolution fusion | flops 814481408 | bytes 30674944 | tf_op jit(solution)/shard_map/dot_general | solution.py:38
  110.9 2.6 convolution_dynamic-update-slice_fusion.26
  116.1 3.8 %convolution_dynamic-update-slice_fusion.24 = f32[6912,256]{1,0:T(8,128)} fusion(f32[6912,256]{1,0:T(8,128)} %convolution_dynamic-update-slice_fusion.25, f32[1024,256]{1,0:T(8,128)} %bitcast.225, f32[1024,256]{1,0:T(8,128)S(1)} %fusion.26), kind=kOutput, calls=%fused_computation.65 | convolution fusion | flops 805306368 | bytes 2359296 | tf_op jit(solution)/shard_map/dot_general | solution.py:73
  127.5 2.9 convolution_dynamic-update-slice_fusion.20
  130.5 2.6 convolution_dynamic-update-slice_fusion.19
  145.9 2.7 convolution_dynamic-update-slice_fusion.13
  151.1 2.6 convolution_dynamic-update-slice_fusion.11
  156.3 2.6 convolution_dynamic-update-slice_fusion.9
  158.9 2.6 convolution_dynamic-update-slice_fusion.8
  164.0 2.8 convolution_dynamic-update-slice_fusion.6
  166.8 2.6 convolution_dynamic-update-slice_fusion.5
  169.4 2.6 convolution_dynamic-update-slice_fusion.4
  183.9 5.0 %collective-permute-start.4 = (f32[1,8,16,256]{3,2,1,0:T(8,128)S(1)}, f32[1,8,16,256]{3,2,1,0:T(8,128)S(1)}, u32[]{:S(2)}, u32[]{:S(2)}) collective-permute-start(f32[1,8,16,256]{3,2,1,0:T(8,128)S(1)} %bitcast.261), channel_id=1, source_target_pairs={{0,4},{4,8},{8,12},{12,16},{16,20},{20,24},{24,28},{1,5},{5,9},{9,... | collective-permute-start | bytes 393224 | tf_op jit(solution)/shard_map/ppermute | solution.py:14
  190.9 3.3 collective-permute-done.4
  194.3 4.0 %collective-permute-start.6 = (f32[10,1,16,256]{3,2,1,0:T(8,128)S(1)}, f32[10,1,16,256]{3,2,1,0:T(8,128)S(1)}, u32[]{:S(2)}, u32[]{:S(2)}) collective-permute-start(f32[10,1,16,256]{3,2,1,0:T(8,128)S(1)} %get-tuple-element.56), channel_id=1, source_target_pairs={{0,1},{1,2},{2,3},{4,5},{5,6},{6,7},{8,9},{9,10},{10,11},{12,13},{... | collective-permute-start | bytes 491528 | tf_op jit(solution)/shard_map/ppermute | solution.py:14
  199.9 3.0 fusion.113
  202.8 3.1 fusion.43
  220.8 6.0 %fusion.133 = (f32[8,8,16,256]{3,2,1,0:T(8,128)}, f32[8,8,16,256]{3,2,1,0:T(8,128)}, f32[8,8,16,256]{3,2,1,0:T(8,128)}, f32[8,8,16,256]{3,2,1,0:T(8,128)}, f32[8...) fusion(f32[10,10,18,256]{3,2,1,0:T(8,128)S(1)} %select_maximum_, ...), kind=kLoop, calls=%fused_computation.189 | loop fusion | bytes 37748736 | tf_op jit(solution)/shard_map/slice | solution.py:57
  226.8 3.4 fusion.129
  230.2 3.3 fusion.35
  233.5 3.4 fusion.39
  261.3 55.6 %reduce-scatter.5.cloned.1.call-done = f32[864,256]{1,0:T(8,128)} async-done(((f32[6912,256]{1,0:T(8,128)}), f32[864,256]{1,0:T(8,128)}) %reduce-scatter.5.cloned.1.call-update) | async-done | bytes 884752 | tf_op jit(solution)/shard_map/reduce_scatter | solution.py:81
  323.9 10.0 %fusion.23 = f32[1024,256]{1,0:T(8,128)S(1)} fusion(f32[1024,256]{1,0:T(8,128)S(1)} %fusion.27, f32[1024,256]{1,0:T(8,128)} %fusion.31, f32[1024,256]{1,0:T(8,128)} %fusion.35, f32[1024,256]{1,0:T(8,128)} %fusion.39, f32[1024,256]{1,0:T(8,128)} %fusion.43, f32[1024,256]{1,0:T(8,128)} %fusion.47, f32[1024,256]{1,0:T(8,128)} %fusion.51, ...), kind=kOutput, calls=%fused_computation.39 | convolution fusion | flops 812122112 | bytes 29622272 | tf_op jit(solution)/shard_map/dot_general | solution.py:62
  335.1 8.2 %reduce-scatter.7.cloned.1.call-done = f32[64,864]{1,0:T(8,128)} async-done(((f32[256,864]{1,0:T(8,128)}), f32[64,864]{1,0:T(8,128)}) %reduce-scatter.7.cloned.1.call-update) | async-done | bytes 221200
  (200 shorter events, 144.0 us)
Async XLA Ops:
  7.2 309.7 %reduce-scatter.5.cloned.1.call-start = ((), (), s32[]{:S(2)}) async-start(), calls=%async_computation.2 | async-start | bytes 7962624 | tf_op jit(solution)/shard_map/reduce_scatter | solution.py:81
  9.4 9.2 %collective-permute-start = (f32[1,8,16,256]{3,2,1,0:T(8,128)S(1)}, f32[1,8,16,256]{3,2,1,0:T(8,128)S(1)}, u32[]{:S(2)}, u32[]{:S(2)}) collective-permute-start(f32[1,8,16,256]{3,2,1,0:T(8,128)S(1)} %get-tuple-element.68), channel_id=1, source_target_pairs={{0,4},{4,8},{8,12},{12,16},{16,20},{20,24},{24,28},{1,5},{5,9},{9,... | collective-permute-start | bytes 393224 | tf_op jit(solution)/shard_map/ppermute | solution.py:14
  14.3 6.9 %collective-permute-start.1 = (f32[1,8,16,256]{3,2,1,0:T(8,128)S(1)}, f32[1,8,16,256]{3,2,1,0:T(8,128)S(1)}, u32[]{:S(2)}, u32[]{:S(2)}) collective-permute-start(f32[1,8,16,256]{3,2,1,0:T(8,128)S(1)} %get-tuple-element.69), channel_id=1, source_target_pairs={{4,0},{8,4},{12,8},{16,12},{20,16},{24,20},{28,24},{5,1},{9,5},{13... | collective-permute-start | bytes 393224 | tf_op jit(solution)/shard_map/ppermute | solution.py:15
  21.2 8.0 %collective-permute-start.2 = (f32[10,1,16,256]{3,2,1,0:T(8,128)S(1)}, f32[10,1,16,256]{3,2,1,0:T(8,128)S(1)}, u32[]{:S(2)}, u32[]{:S(2)}) collective-permute-start(f32[10,1,16,256]{3,2,1,0:T(8,128)S(1)} %get-tuple-element.60), channel_id=1, source_target_pairs={{0,1},{1,2},{2,3},{4,5},{5,6},{6,7},{8,9},{9,10},{10,11},{12,13},{... | collective-permute-start | bytes 491528 | tf_op jit(solution)/shard_map/ppermute | solution.py:14
  22.5 6.7 %collective-permute-start.3 = (f32[10,1,16,256]{3,2,1,0:T(8,128)S(1)}, f32[10,1,16,256]{3,2,1,0:T(8,128)S(1)}, u32[]{:S(2)}, u32[]{:S(2)}) collective-permute-start(f32[10,1,16,256]{3,2,1,0:T(8,128)S(1)} %get-tuple-element.61), channel_id=1, source_target_pairs={{1,0},{2,1},{3,2},{5,4},{6,5},{7,6},{9,8},{10,9},{11,10},{13,12},{... | collective-permute-start | bytes 491528 | tf_op jit(solution)/shard_map/ppermute | solution.py:15
  49.5 49.0 %copy-start.5 = (f32[8,8,16,256]{3,2,1,0:T(8,128)}, f32[8,8,16,256]{3,2,1,0:T(8,128)S(1)}, u32[]{:S(2)}) copy-start(f32[8,8,16,256]{3,2,1,0:T(8,128)S(1)} %get-tuple-element.41) | copy-start | bytes 3145732
  49.5 14.2 %copy-start.13 = (f32[8,8,16,256]{3,2,1,0:T(8,128)S(1)}, f32[8,8,16,256]{3,2,1,0:T(8,128)}, u32[]{:S(2)}) copy-start(f32[8,8,16,256]{3,2,1,0:T(8,128)} %get-tuple-element.29) | copy-start | bytes 3145732
  49.5 16.2 %copy-start.16 = (f32[8,8,16,256]{3,2,1,0:T(8,128)S(1)}, f32[8,8,16,256]{3,2,1,0:T(8,128)}, u32[]{:S(2)}) copy-start(f32[8,8,16,256]{3,2,1,0:T(8,128)} %get-tuple-element.30) | copy-start | bytes 3145732
  53.1 14.5 %copy-start.17 = (f32[8,8,16,256]{3,2,1,0:T(8,128)S(1)}, f32[8,8,16,256]{3,2,1,0:T(8,128)}, u32[]{:S(2)}) copy-start(f32[8,8,16,256]{3,2,1,0:T(8,128)} %get-tuple-element.31) | copy-start | bytes 3145732
  65.7 24.9 %copy-start.25 = (f32[8,8,16,256]{3,2,1,0:T(8,128)S(1)}, f32[8,8,16,256]{3,2,1,0:T(8,128)}, u32[]{:S(2)}) copy-start(f32[8,8,16,256]{3,2,1,0:T(8,128)} %get-tuple-element.37) | copy-start | bytes 3145732
  67.7 24.9 %copy-start.27 = (f32[8,8,16,256]{3,2,1,0:T(8,128)S(1)}, f32[8,8,16,256]{3,2,1,0:T(8,128)}, u32[]{:S(2)}) copy-start(f32[8,8,16,256]{3,2,1,0:T(8,128)} %get-tuple-element.38) | copy-start | bytes 3145732
  69.7 24.9 %copy-start.29 = (f32[8,8,16,256]{3,2,1,0:T(8,128)S(1)}, f32[8,8,16,256]{3,2,1,0:T(8,128)}, u32[]{:S(2)}) copy-start(f32[8,8,16,256]{3,2,1,0:T(8,128)} %get-tuple-element.39) | copy-start | bytes 3145732
  71.6 24.9 %copy-start.31 = (f32[8,8,16,256]{3,2,1,0:T(8,128)S(1)}, f32[8,8,16,256]{3,2,1,0:T(8,128)}, u32[]{:S(2)}) copy-start(f32[8,8,16,256]{3,2,1,0:T(8,128)} %get-tuple-element.40) | copy-start | bytes 3145732
  110.9 14.1 %copy-start.28 = (f32[8,8,16,256]{3,2,1,0:T(8,128)S(1)}, f32[8,8,16,256]{3,2,1,0:T(8,128)}, u32[]{:S(2)}) copy-start(f32[8,8,16,256]{3,2,1,0:T(8,128)} %get-tuple-element.38) | copy-start | bytes 3145732
  110.9 16.7 %copy-start.26 = (f32[8,8,16,256]{3,2,1,0:T(8,128)S(1)}, f32[8,8,16,256]{3,2,1,0:T(8,128)}, u32[]{:S(2)}) copy-start(f32[8,8,16,256]{3,2,1,0:T(8,128)} %get-tuple-element.37) | copy-start | bytes 3145732
  113.5 17.0 %copy-start.15 = (f32[8,8,16,256]{3,2,1,0:T(8,128)S(1)}, f32[8,8,16,256]{3,2,1,0:T(8,128)}, u32[]{:S(2)}) copy-start(f32[8,8,16,256]{3,2,1,0:T(8,128)} %copy-done.14) | copy-start | bytes 3145732
  116.1 17.0 %copy-start.24 = (f32[8,8,16,256]{3,2,1,0:T(8,128)S(1)}, f32[8,8,16,256]{3,2,1,0:T(8,128)}, u32[]{:S(2)}) copy-start(f32[8,8,16,256]{3,2,1,0:T(8,128)} %get-tuple-element.36) | copy-start | bytes 3145732
  122.5 15.7 %copy-start.10 = (f32[8,8,16,256]{3,2,1,0:T(8,128)S(1)}, f32[8,8,16,256]{3,2,1,0:T(8,128)}, u32[]{:S(2)}) copy-start(f32[8,8,16,256]{3,2,1,0:T(8,128)} %copy-done.9) | copy-start | bytes 3145732
  138.2 15.5 %copy-start.4 = (f32[8,8,16,256]{3,2,1,0:T(8,128)S(1)}, f32[8,8,16,256]{3,2,1,0:T(8,128)}, u32[]{:S(2)}) copy-start(f32[8,8,16,256]{3,2,1,0:T(8,128)} %copy-done.3) | copy-start | bytes 3145732
  145.9 15.6 %copy-start.2 = (f32[8,8,16,256]{3,2,1,0:T(8,128)S(1)}, f32[8,8,16,256]{3,2,1,0:T(8,128)}, u32[]{:S(2)}) copy-start(f32[8,8,16,256]{3,2,1,0:T(8,128)} %copy-done.1) | copy-start | bytes 3145732
  153.7 15.7 %copy-start.34 = (f32[8,8,16,256]{3,2,1,0:T(8,128)S(1)}, f32[8,8,16,256]{3,2,1,0:T(8,128)}, u32[]{:S(2)}) copy-start(f32[8,8,16,256]{3,2,1,0:T(8,128)} %copy-done.33) | copy-start | bytes 3145732
  156.3 15.7 %copy-start.8 = (f32[8,8,16,256]{3,2,1,0:T(8,128)S(1)}, f32[8,8,16,256]{3,2,1,0:T(8,128)}, u32[]{:S(2)}) copy-start(f32[8,8,16,256]{3,2,1,0:T(8,128)} %get-tuple-element.26) | copy-start | bytes 3145732
  158.9 15.7 %copy-start.7 = (f32[8,8,16,256]{3,2,1,0:T(8,128)S(1)}, f32[8,8,16,256]{3,2,1,0:T(8,128)}, u32[]{:S(2)}) copy-start(f32[8,8,16,256]{3,2,1,0:T(8,128)} %get-tuple-element.25) | copy-start | bytes 3145732
  164.0 15.6 %copy-start.6 = (f32[8,8,16,256]{3,2,1,0:T(8,128)S(1)}, f32[8,8,16,256]{3,2,1,0:T(8,128)}, u32[]{:S(2)}) copy-start(f32[8,8,16,256]{3,2,1,0:T(8,128)} %copy-done.5) | copy-start | bytes 3145732
  182.2 161.2 %reduce-scatter.7.cloned.1.call-start = ((), (), s32[]{:S(2)}) async-start(), calls=%async_computation.3 | async-start | bytes 1146880
  182.6 8.3 %collective-permute-start.5 = (f32[1,8,16,256]{3,2,1,0:T(8,128)S(1)}, f32[1,8,16,256]{3,2,1,0:T(8,128)S(1)}, u32[]{:S(2)}, u32[]{:S(2)}) collective-permute-start(f32[1,8,16,256]{3,2,1,0:T(8,128)S(1)} %bitcast.262), channel_id=1, source_target_pairs={{4,0},{8,4},{12,8},{16,12},{20,16},{24,20},{28,24},{5,1},{9,5},{13... | collective-permute-start | bytes 393224 | tf_op jit(solution)/shard_map/ppermute | solution.py:15
  183.9 10.3 %collective-permute-start.4 = (f32[1,8,16,256]{3,2,1,0:T(8,128)S(1)}, f32[1,8,16,256]{3,2,1,0:T(8,128)S(1)}, u32[]{:S(2)}, u32[]{:S(2)}) collective-permute-start(f32[1,8,16,256]{3,2,1,0:T(8,128)S(1)} %bitcast.261), channel_id=1, source_target_pairs={{0,4},{4,8},{8,12},{12,16},{16,20},{20,24},{24,28},{1,5},{5,9},{9,... | collective-permute-start | bytes 393224 | tf_op jit(solution)/shard_map/ppermute | solution.py:14
  194.3 11.7 %collective-permute-start.6 = (f32[10,1,16,256]{3,2,1,0:T(8,128)S(1)}, f32[10,1,16,256]{3,2,1,0:T(8,128)S(1)}, u32[]{:S(2)}, u32[]{:S(2)}) collective-permute-start(f32[10,1,16,256]{3,2,1,0:T(8,128)S(1)} %get-tuple-element.56), channel_id=1, source_target_pairs={{0,1},{1,2},{2,3},{4,5},{5,6},{6,7},{8,9},{9,10},{10,11},{12,13},{... | collective-permute-start | bytes 491528 | tf_op jit(solution)/shard_map/ppermute | solution.py:14
  198.3 7.6 %collective-permute-start.7 = (f32[10,1,16,256]{3,2,1,0:T(8,128)S(1)}, f32[10,1,16,256]{3,2,1,0:T(8,128)S(1)}, u32[]{:S(2)}, u32[]{:S(2)}) collective-permute-start(f32[10,1,16,256]{3,2,1,0:T(8,128)S(1)} %get-tuple-element.57), channel_id=1, source_target_pairs={{1,0},{2,1},{3,2},{5,4},{6,5},{7,6},{9,8},{10,9},{11,10},{13,12},{... | collective-permute-start | bytes 491528 | tf_op jit(solution)/shard_map/ppermute | solution.py:15
  226.8 16.1 %copy-start.44 = (f32[8,8,16,256]{3,2,1,0:T(8,128)S(1)}, f32[8,8,16,256]{3,2,1,0:T(8,128)}, u32[]{:S(2)}) copy-start(f32[8,8,16,256]{3,2,1,0:T(8,128)} %get-tuple-element.12) | copy-start | bytes 3145732
  230.2 14.7 %copy-start.43 = (f32[8,8,16,256]{3,2,1,0:T(8,128)S(1)}, f32[8,8,16,256]{3,2,1,0:T(8,128)}, u32[]{:S(2)}) copy-start(f32[8,8,16,256]{3,2,1,0:T(8,128)} %get-tuple-element.13) | copy-start | bytes 3145732
  255.3 68.7 %copy-start.37 = (f32[1024,256]{1,0:T(8,128)S(1)}, f32[1024,256]{1,0:T(8,128)}, u32[]{:S(2)}) copy-start(f32[1024,256]{1,0:T(8,128)} %fusion.113) | copy-start | bytes 3145732
  (32 other events, 345.4 us)
Sparse Core Ops, SparseCore 0:
  182.3 134.5 reduce-scatter.4
  320.2 23.1 reduce-scatter.6
where the time goes:
time: 354 us; the launch traced here: 350 us
  matrix products  222 us (63%)
  waiting for transfers between devices  69.7 us (20%)
  starting transfers between devices  20.8 us (6%)
  local copies, waits for them, and re-layouts  17.5 us (5%)
  between operations  14.8 us (4%)
  other arithmetic  5.64 us (2%)
    dot_general x27, matrix products, body(): jnp.dot(piece, weight[index * channels:(index + 1) * channels], precision...  81.6 us
    dot_general x27, matrix products, body(): jnp.dot(piece.T, upstream, precision=lax.Precision.HIGHEST, preferred_ele...  71.2 us
    dot_general x27, matrix products, body(): jnp.dot(back, kernel.T, precision=lax.Precision.HIGHEST, preferred_elemen...  69.2 us
    reduce_scatter x1, waiting for transfers between devices, body(): row_sums = lax.psum_scatter(term, 'gx', scatter_dimension=0, tiled=True)  55.6 us
    ppermute x4, starting transfers between devices, with_halo(): before = lax.ppermute(last, axis, up)  15.2 us
    unnamed x3, waiting for transfers between devices  8.28 us
  transfers between devices with their start and end apart: 10, of which 4 were waited for; matrix products, arithmetic and copies ran while one was open for 25% of the time, Pallas kernels for 0%

commit v1 on v0

v1 whole, which is shorter than its diff:
```python
import jax
import jax.numpy as jnp
from jax import lax
from jax.experimental import pallas as pl
from jax.experimental.pallas import tpu as pltpu
from jax.sharding import PartitionSpec as P

F32 = jnp.float32
BF16 = jnp.bfloat16
VMEM_BYTES = 40 * 1024 * 1024
LANES = 128


def split(value):
    high = value.astype(BF16)
    low = (value - high.astype(F32)).astype(BF16)
    return high, low


def with_halo(array, sides, width):
    for axis, dim in sides:
        devices, length = (lax.axis_size(axis), array.shape[dim])
        up = [(i, (i + 1) % devices) for i in range(devices - 1)]
        down = [(j, i) for i, j in up]
        last = lax.slice_in_dim(array, length - width, length, axis=dim)
        first = lax.slice_in_dim(array, 0, width, axis=dim)
        before = lax.ppermute(last, axis, up)
        after = lax.ppermute(first, axis, down)
        array = jnp.concatenate([before, array, after], axis=dim)
    return array


def shift_rows(value, step, depth):
    rows = value.shape[0]
    place = lax.broadcasted_iota(jnp.int32, value.shape, 0) % depth
    moved = pltpu.roll(value, (-step) % rows, 0)
    inside = (place + step >= 0) & (place + step < depth)
    return jnp.where(inside, moved, 0.0)


def stack_terms(value):
    high, low = split(value)
    return jnp.concatenate([high, low, high], axis=-1)


def forward_kernel(span_x, span_y, depth, padded_ref, cot_ref, weight_ref, up_ref, stack_ref, acc_ref):
    step = pl.program_id(0)
    count = span_x * span_y * depth
    channels = weight_ref.shape[-1]

    @pl.when(step == 0)
    def _():
        for i in range(span_x + 2):
            stack_ref[i] = stack_terms(padded_ref[i])
        acc_ref[...] = jnp.zeros_like(acc_ref)

    first, second = step // 3, step % 3
    piece = stack_ref[pl.ds(first, span_x), pl.ds(second, span_y)].reshape(count, 3 * channels)
    for third in range(3):
        high, low = split(weight_ref[third])
        acc_ref[third] += jnp.dot(
            piece, jnp.concatenate([high, high, low], axis=0), preferred_element_type=F32
        )

    @pl.when(step == 8)
    def _():
        preact = (
            acc_ref[1] + shift_rows(acc_ref[0], -1, depth) + shift_rows(acc_ref[2], 1, depth)
        )
        sigma = jax.nn.sigmoid(preact)
        up_ref[...] = cot_ref[...] * sigma * (1.0 + preact * (1.0 - sigma))


def forward(padded, cot, weight, span_x, span_y, depth):
    channels = padded.shape[-1]
    count = span_x * span_y * depth

    def kernel(*refs):
        forward_kernel(span_x, span_y, depth, *refs)

    return pl.pallas_call(
        kernel,
        grid=(9,),
        in_specs=[
            pl.BlockSpec(padded.shape, lambda s: (0, 0, 0, 0)),
            pl.BlockSpec((count, channels), lambda s: (0, 0)),
            pl.BlockSpec((3, channels, channels), lambda s: (s, 0, 0)),
        ],
        out_specs=pl.BlockSpec((count, channels), lambda s: (0, 0)),
        out_shape=jax.ShapeDtypeStruct((count, channels), F32),
        scratch_shapes=[
            pltpu.VMEM((span_x + 2, span_y + 2, depth, 3 * channels), BF16),
            pltpu.VMEM((3, count, channels), F32),
        ],
        compiler_params=pltpu.CompilerParams(vmem_limit_bytes=VMEM_BYTES),
        cost_estimate=pl.CostEstimate(
            flops=2 * 81 * count * channels * channels,
            bytes_accessed=4 * (padded.size + 2 * cot.size + weight.size),
            transcendentals=count * channels,
        ),
    )(padded, cot, weight)


def data_kernel(span_x, span_y, depth, padded_ref, filled_ref, weight_ref, out_ref, stack_ref, acc_ref):
    step = pl.program_id(0)
    count = span_x * span_y * depth
    channels = weight_ref.shape[-1]

    @pl.when(step == 0)
    def _():
        for i in range(span_x + 2):
            stack_ref[i] = stack_terms(padded_ref[i])
        acc_ref[...] = jnp.zeros_like(acc_ref)

    first, second = step // 3, step % 3
    piece = stack_ref[pl.ds(2 - first, span_x), pl.ds(2 - second, span_y)].reshape(
        count, 3 * channels
    )
    for third in range(3):
        high, low = split(weight_ref[third])
        acc_ref[third] += lax.dot_general(
            piece,
            jnp.concatenate([high, high, low], axis=1),
            (((1,), (1,)), ((), ())),
            preferred_element_type=F32,
        )

    @pl.when(step == 8)
    def _():
        total = acc_ref[1] + shift_rows(acc_ref[0], 1, depth) + shift_rows(acc_ref[2], -1, depth)
        out_ref[...] = total * filled_ref[...]


def data_grad(padded, filled, weight, span_x, span_y, depth):
    channels = padded.shape[-1]
    count = span_x * span_y * depth

    def kernel(*refs):
        data_kernel(span_x, span_y, depth, *refs)

    return pl.pallas_call(
        kernel,
        grid=(9,),
        in_specs=[
            pl.BlockSpec(padded.shape, lambda s: (0, 0, 0, 0)),
            pl.BlockSpec((count, 1), lambda s: (0, 0)),
            pl.BlockSpec((3, channels, channels), lambda s: (s, 0, 0)),
        ],
        out_specs=pl.BlockSpec((count, channels), lambda s: (0, 0)),
        out_shape=jax.ShapeDtypeStruct((count, channels), F32),
        scratch_shapes=[
            pltpu.VMEM((span_x + 2, span_y + 2, depth, 3 * channels), BF16),
            pltpu.VMEM((3, count, channels), F32),
        ],
        compiler_params=pltpu.CompilerParams(vmem_limit_bytes=VMEM_BYTES),
        cost_estimate=pl.CostEstimate(
            flops=2 * 81 * count * channels * channels,
            bytes_accessed=4 * (padded.size + count * channels + weight.size),
            transcendentals=0,
        ),
    )(padded, filled, weight)


def filter_kernel(span_x, span_y, depth, parts, place_ref, padded_ref, up_ref, *refs):
    outs, (turned_ref, left_ref, right_ref, acc_ref) = refs[: 2 * parts], refs[2 * parts :]
    channels = padded_ref.shape[-1]
    count = span_x * span_y * depth
    slab = span_y * depth
    groups = channels // (16 * parts)
    rows = groups * 16

    left, right = up_ref[:, :LANES], up_ref[:, LANES:]
    swap_high, swap_low = place_ref[0, 0] > 0, place_ref[0, 1] > 0
    left, right = jnp.where(swap_high, right, left), jnp.where(swap_high, left, right)
    left = jnp.where(swap_low, pltpu.roll(left, 64, 1), left)
    right = jnp.where(swap_low, pltpu.roll(right, 64, 1), right)
    upstream = jnp.concatenate([left, right], axis=1)
    for third in range(3):
        high, low = split(shift_rows(upstream, 1 - third, depth))
        right_ref[third, :count] = high
        right_ref[third, count : 2 * count] = high
        right_ref[third, 2 * count :] = low

    for second in range(3):
        for i in range(span_x + 2):
            piece = padded_ref[i, second : second + span_y].reshape(slab, channels)
            high, low = split(piece.T)
            turned_ref[0, second, :, i * slab : (i + 1) * slab] = high
            turned_ref[1, second, :, i * slab : (i + 1) * slab] = low

    low_lanes = lax.broadcasted_iota(jnp.int32, (8, LANES), 1) < 64
    for part in range(parts):
        for first in range(3):
            for second in range(3):
                tap = first * 3 + second
                lanes = slice(first * slab, first * slab + count)
                for group in range(groups):
                    source = slice((group * parts + part) * 16, (group * parts + part + 1) * 16)
                    target = slice(tap * rows + group * 16, tap * rows + (group + 1) * 16)
                    high = turned_ref[0, second, source, lanes]
                    left_ref[target, :count] = high
                    left_ref[target, count : 2 * count] = turned_ref[1, second, source, lanes]
                    left_ref[target, 2 * count :] = high
        keep_ref, send_ref = outs[2 * part], outs[2 * part + 1]
        jump = place_ref[0, 2 + part]

        def one(third, carry):
            acc_ref[...] = jnp.dot(left_ref[...], right_ref[third], preferred_element_type=F32)
            for tap in range(9):
                for group in range(groups):
                    at = place_ref[1 + part, (tap * 3 + third) * groups + group]
                    start = tap * rows + group * 16
                    for high_half in range(2):
                        columns = slice(high_half * LANES, (high_half + 1) * LANES)
                        upper = acc_ref[start : start + 8, columns]
                        lower = acc_ref[start + 8 : start + 16, columns]
                        keep_ref[at + high_half * jump] = jnp.where(
                            low_lanes, upper, pltpu.roll(lower, 64, 1)
                        )
                        send_ref[at + high_half * jump] = jnp.where(
                            low_lanes, pltpu.roll(upper, 64, 1), lower
                        )
            return carry

        lax.fori_loop(0, 3, one, 0)


def filter_terms(padded, upstream, place, parts, chunks, units, span_x, span_y, depth):
    channels = padded.shape[-1]
    count = span_x * span_y * depth

    def kernel(*refs):
        filter_kernel(span_x, span_y, depth, parts, *refs)

    whole = pl.BlockSpec(memory_space=pltpu.VMEM)
    shape = jax.ShapeDtypeStruct((chunks * units, 8, LANES), F32)
    return pl.pallas_call(
        kernel,
        in_specs=[pl.BlockSpec(memory_space=pltpu.SMEM), whole, whole],
        out_specs=[whole] * (2 * parts),
        out_shape=[shape] * (2 * parts),
        scratch_shapes=[
            pltpu.VMEM((2, 3, channels, (span_x + 2) * span_y * depth), BF16),
            pltpu.VMEM((9 * channels // parts, 3 * count), BF16),
            pltpu.VMEM((3, 3 * count, channels), BF16),
            pltpu.VMEM((9 * channels // parts, channels), F32),
        ],
        compiler_params=pltpu.CompilerParams(vmem_limit_bytes=VMEM_BYTES),
        cost_estimate=pl.CostEstimate(
            flops=2 * 81 * count * channels * channels,
            bytes_accessed=4 * (padded.size + upstream.size + 27 * channels * channels),
            transcendentals=0,
        ),
    )(place, padded, upstream)


def bits_of(size):
    return size.bit_length() - 1


def reduce_part(keep, send, stages, units):
    axis, bit = stages[0]
    for index, (axis, bit) in enumerate(stages):
        pairs = [(i, i ^ (1 << bit)) for i in range(lax.axis_size(axis))]
        got = lax.ppermute(send, axis, pairs)
        if index == len(stages) - 1:
            return keep + got
        middle = keep.shape[0] // 2
        send = keep[middle:] + got[middle:]
        keep = keep[:middle] + got[:middle]


def plain_filter_grad(bordered, upstream, span_x, span_y, depth):
    padded = jnp.pad(bordered, ((0, 0), (0, 0), (1, 1), (0, 0)))
    blocks = []
    for first in range(3):
        for second in range(3):
            for third in range(3):
                piece = padded[
                    first : first + span_x, second : second + span_y, third : third + depth
                ].reshape(upstream.shape)
                blocks.append(
                    jnp.dot(
                        piece.T,
                        upstream,
                        precision=lax.Precision.HIGHEST,
                        preferred_element_type=F32,
                    )
                )
    term = jnp.concatenate(blocks, axis=0)
    row_sums = lax.psum_scatter(term, "gx", scatter_dimension=0, tiled=True)
    return lax.psum_scatter(row_sums, "gy", scatter_dimension=1, tiled=True)


def data_part(upstream, shape, filled, taps, sides):
    span_x, span_y, depth, channels = shape
    border_up = with_halo(upstream.reshape(shape), sides, 1)
    result = data_grad(border_up, filled.reshape(-1, 1), taps, span_x, span_y, depth)
    return result.reshape(shape)


def body(inputs, cotangent, weight, occupancy):
    span_x, span_y, depth, channels = inputs.shape
    count = span_x * span_y * depth
    size_x, size_y = lax.axis_size("gx"), lax.axis_size("gy")
    sides = (("gx", 0), ("gy", 1))
    filled = occupancy.astype(F32)[..., None]
    masked = inputs * filled
    bordered = with_halo(masked, sides, 1)
    cot = (cotangent * filled).reshape(count, channels)
    taps = weight.reshape(27, channels, channels)
    upstream = forward(bordered, cot, taps, span_x, span_y, depth)

    parts, groups = 2, channels // 32
    if channels // size_y != 64 or 27 * groups % size_x or channels != 256:
        weight_grad = plain_filter_grad(bordered, upstream, span_x, span_y, depth)
        return (data_part(upstream, inputs.shape, filled, taps, sides), weight_grad)
    units = 27 * groups // size_x
    me_x, me_y = lax.axis_index("gx"), lax.axis_index("gy")
    bits_x, bits_y = bits_of(size_x), bits_of(size_y)
    order = {
        0: [("gy", 0), ("gx", 0), ("gy", 1)] + [("gx", b) for b in range(1, bits_x)],
        1: [("gy", 0), ("gy", 1)] + [("gx", b) for b in range(bits_x)],
    }
    unit = jnp.arange(27 * groups, dtype=jnp.int32)
    relative = (unit // units) ^ me_x
    rows = []
    jumps = []
    for part in range(parts):
        stages = order[part][1:]
        at = jnp.zeros_like(unit)
        for position, (axis, bit) in enumerate(stages):
            worth = 1 << (len(stages) - 1 - position)
            if axis == "gx":
                at = at + ((relative >> bit) & 1) * worth
            else:
                jumps.append(jnp.int32(worth * units))
        rows.append(at * units + unit % units)
    head = jnp.stack([(me_y >> 1) & 1, me_y & 1] + jumps).astype(jnp.int32)
    head = jnp.pad(head, (0, unit.size - head.size))
    place = jnp.stack([head] + rows)
    chunks = 2 * size_x
    terms = filter_terms(
        bordered, upstream, place, parts, chunks, units, span_x, span_y, depth
    )
    sums = [
        reduce_part(terms[2 * p], terms[2 * p + 1], order[p], units) for p in range(parts)
    ]
    both = jnp.stack([s.reshape(units, 8, 2, 64) for s in sums], axis=1)
    weight_grad = both.transpose(0, 1, 3, 2, 4).reshape(units * 32, 64)

    return (data_part(upstream, inputs.shape, filled, taps, sides), weight_grad)


def solution(mesh):
    in_specs = (P("gx", "gy", None, None), P("gx", "gy", None, None), P(), P("gx", "gy", None))
    out_specs = (P("gx", "gy", None, None), P("gx", "gy"))
    return jax.shard_map(body, mesh=mesh, in_specs=in_specs, out_specs=out_specs, check_vma=False)
```

time: 354 us -> 147 us (0.42)
  matrix products: 222 us -> 0 us
  Pallas kernels: 0 us -> 44.7 us
  waiting for transfers between devices: 69.7 us -> 48.2 us
  starting transfers between devices: 20.8 us -> 35.4 us
  between operations: 14.8 us -> 0.87 us
  local copies, waits for them, and re-layouts: 17.5 us -> 7.65 us
  other arithmetic: 5.64 us -> 9.67 us
    dot_general x81 -> x0, matrix products: 222 us -> none  [the longest x27 81.6 us: body(): jnp.dot(piece, weight[index * channels:(index + 1) * channels], precision...]
    reduce_scatter x1 -> x0, waiting for transfers between devices: 55.6 us -> none  [body(): row_sums = lax.psum_scatter(term, 'gx', scatter_dimension=0, tiled=True)]
    pallas_call x0 -> x3, Pallas kernels: none -> 44.7 us  [the longest x1 16.1 us: filter_terms(): pl.pallas_call(kernel, in_specs=[pl.BlockSpec(memory_space=pltpu.SMEM), w...]
    ppermute x0 -> x10, starting transfers between devices: none -> 18.4 us  [reduce_part(): got = lax.ppermute(send, axis, pairs)]
    ppermute x0 -> x10, waiting for transfers between devices: none -> 17.8 us  [reduce_part(): got = lax.ppermute(send, axis, pairs)]
    ppermute x4, waiting for transfers between devices: 3.32 us -> 20.8 us  [with_halo(): before = lax.ppermute(last, axis, up)]
    slice x5 -> x0, local copies, waits for them, and re-layouts: 13.7 us -> none  [the longest x2 6.95 us: body(): padded[first:first + span_x, second:second + span_y, third:third + depth]]
    unnamed x3 -> x0, waiting for transfers between devices: 8.28 us -> none
  transfers between devices with their start and end apart: 10 -> 18, of which waited for: 4 -> 9; matrix products, arithmetic and copies ran while one was open for 25% -> 5% of each run, Pallas kernels for 0% -> 10%
where the time goes in v1:
time: 147 us; the launch traced here: 146 us
  waiting for transfers between devices  48.2 us (33%)
  Pallas kernels  44.7 us (30%)
  starting transfers between devices  35.4 us (24%)
  other arithmetic  9.67 us (7%)
  local copies, waits for them, and re-layouts  7.65 us (5%)
    ppermute x4, waiting for transfers between devices, with_halo(): before = lax.ppermute(last, axis, up)  20.8 us
    ppermute x10, starting transfers between devices, reduce_part(): got = lax.ppermute(send, axis, pairs)  18.4 us
    ppermute x10, waiting for transfers between devices, reduce_part(): got = lax.ppermute(send, axis, pairs)  17.8 us
    pallas_call x1, Pallas kernels, filter_terms(): pl.pallas_call(kernel, in_specs=[pl.BlockSpec(memory_space=pltpu.SMEM), w...  16.1 us
    pallas_call x1, Pallas kernels, data_grad(): pl.pallas_call(kernel, grid=(9,), in_specs=[pl.BlockSpec(padded.shape, la...  14.8 us
    pallas_call x1, Pallas kernels, forward(): pl.pallas_call(kernel, grid=(9,), in_specs=[pl.BlockSpec(padded.shape, la...  13.8 us
    ppermute x4, starting transfers between devices, with_halo(): before = lax.ppermute(last, axis, up)  11.6 us
    ppermute x4, waiting for transfers between devices, with_halo(): after = lax.ppermute(first, axis, down)  9.6 us
  transfers between devices with their start and end apart: 18, of which 9 were waited for; matrix products, arithmetic and copies ran while one was open for 5% of the time, Pallas kernels for 10%

profile of v1, /device:TPU:0, one launch (start us, length us, event | category | flops | bytes accessed | tf_op | source)
XLA Modules:
  0.0 146.4 jit_solution(5199840120443489366)
XLA Ops:
  1.4 1.8 %broadcast_multiply_fusion = (f32[8,8,16,256]{3,2,1,0:T(8,128)S(1)}, f32[8,8,16,256]{3,2,1,0:T(8,128)S(1)}) fusion(f32[8,8,16,256]{3,2,1,0:T(8,128)} %param.5, f32[8,8,16]{2,1,0:T(8,128)S(1)} %convert_element_type.3, f32[8,8,16,256]{3,2,1,0:T(8,128)} %param.4), kind=kLoop, calls=%fused_computation.6 | loop fusion | flops 524288 | bytes 4198400 | tf_op jit(solution)/shard_map/mul | solution.py:310
  3.3 4.8 %collective-permute-start = (f32[1,8,16,256]{3,2,1,0:T(8,128)S(1)}, f32[1,8,16,256]{3,2,1,0:T(8,128)S(1)}, u32[]{:S(2)}, u32[]{:S(2)}) collective-permute-start(f32[1,8,16,256]{3,2,1,0:T(8,128)S(1)} %get-tuple-element.26), channel_id=1, source_target_pairs={{0,4},{4,8},{8,12},{12,16},{16,20},{20,24},{24,28},{1,5},{5,9},{9,... | collective-permute-start | bytes 393224 | tf_op jit(solution)/shard_map/ppermute | solution.py:27
  8.1 1.3 collective-permute-start.1
  9.5 1.4 collective-permute-done
  10.9 4.1 %collective-permute-done.1 = f32[1,8,16,256]{3,2,1,0:T(8,128)S(1)} collective-permute-done((f32[1,8,16,256]{3,2,1,0:T(8,128)S(1)}, f32[1,8,16,256]{3,2,1,0:T(8,128)S(1)}, u32[]{:S(2)}, u32[]{:S(2)}) %collective-permute-start.1) | collective-permute-done | bytes 131104 | tf_op jit(solution)/shard_map/ppermute | solution.py:28
  15.0 1.3 collective-permute-start.2
  16.3 1.3 collective-permute-start.3
  17.7 3.6 %collective-permute-done.3 = f32[10,1,16,256]{3,2,1,0:T(8,128)S(1)} collective-permute-done((f32[10,1,16,256]{3,2,1,0:T(8,128)S(1)}, f32[10,1,16,256]{3,2,1,0:T(8,128)S(1)}, u32[]{:S(2)}, u32[]{:S(2)}) %collective-permute-start.3) | collective-permute-done | bytes 163872 | tf_op jit(solution)/shard_map/ppermute | solution.py:28
  21.5 3.0 %copy-done = f32[6912,256]{1,0:T(8,128)S(1)} copy-done((f32[6912,256]{1,0:T(8,128)S(1)}, f32[6912,256]{1,0:T(8,128)}, u32[]{:S(2)}) %copy-start) | copy-done | bytes 7077912
  24.5 13.8 %shard_map.59.refs_2_ = f32[1024,256]{1,0:T(8,128)S(1)} custom-call(f32[10,10,16,256]{3,2,1,0:T(8,128)S(1)} %pad_maximum_fusion.refs_0_.refs_1_, f32[1024,256]{1,0:T(8,128)S(1)} %bitcast.14, f32[27,256,256]{2,1,0:T(8,128)S(1)} %bitcast.15), custom_call_target="tpu_custom_call" | custom-call | flops 10871635968 | bytes 10813440 | tf_op jit(solution)/shard_map/pallas_call | solution.py:81
  38.4 16.1 %shard_map.61 = (f32[432,8,128]{2,1,0:T(8,128)S(1)}, f32[432,8,128]{2,1,0:T(8,128)S(1)}, f32[432,8,128]{2,1,0:T(8,128)S(1)}, f32[432,8,128]{2,1,0:T(8,128)S(1)}) custom-call(s32[3,216]{1,0:T(4,128)S(1)} %pad_add_fusion.refs_0_, f32[10,10,16,256]{3,2,1,0:T(8,128)S(1)} %pad_maximum_fusion.refs_0_.refs_1_, f32[1024,256]{1,0:T(8,128)S(1)} %shard_map.59.refs_2_), custom_call_target="tpu_custom_call" | custom-call | flops 10871635968 | bytes 9764864 | tf_op jit(solution)/shard_map/pallas_call | solution.py:237
  54.4 3.9 %collective-permute-start.8 = (f32[432,8,128]{2,1,0:T(8,128)S(1)}, f32[432,8,128]{2,1,0:T(8,128)S(1)}, u32[]{:S(2)}, u32[]{:S(2)}) collective-permute-start(f32[432,8,128]{2,1,0:T(8,128)S(1)} %get-tuple-element.7), channel_id=1, source_target_pairs={{0,1},{1,0},{2,3},{3,2},{4,5},{5,4},{6,7},{7,6},{8,9},{9,8},{10,11... | collective-permute-start | bytes 5308424 | tf_op jit(solution)/shard_map/ppermute | solution.py:265
  58.4 3.2 %collective-permute-done.8 = f32[432,8,128]{2,1,0:T(8,128)S(1)} collective-permute-done((f32[432,8,128]{2,1,0:T(8,128)S(1)}, f32[432,8,128]{2,1,0:T(8,128)S(1)}, u32[]{:S(2)}, u32[]{:S(2)}) %collective-permute-start.8) | collective-permute-done | bytes 1769504 | tf_op jit(solution)/shard_map/ppermute | solution.py:265
  62.7 2.5 %collective-permute-start.9 = (f32[216,8,128]{2,1,0:T(8,128)}, f32[216,8,128]{2,1,0:T(8,128)}, u32[]{:S(2)}, u32[]{:S(2)}) collective-permute-start(f32[216,8,128]{2,1,0:T(8,128)} %get-tuple-element.13), channel_id=1, source_target_pairs={{0,4},{4,0},{8,12},{12,8},{16,20},{20,16},{24,28},{28,24},{1,5},{5... | collective-permute-start | bytes 2654216 | tf_op jit(solution)/shard_map/ppermute | solution.py:265
  66.4 3.3 %collective-permute-start.4 = (f32[1,8,16,256]{3,2,1,0:T(8,128)S(1)}, f32[1,8,16,256]{3,2,1,0:T(8,128)S(1)}, u32[]{:S(2)}, u32[]{:S(2)}) collective-permute-start(f32[1,8,16,256]{3,2,1,0:T(8,128)S(1)} %bitcast.19), channel_id=1, source_target_pairs={{0,4},{4,8},{8,12},{12,16},{16,20},{20,24},{24,28},{1,5},{5,9},{9,... | collective-permute-start | bytes 393224 | tf_op jit(solution)/shard_map/ppermute | solution.py:27
  69.8 1.3 collective-permute-start.5
  71.1 19.4 %collective-permute-done.4 = f32[1,8,16,256]{3,2,1,0:T(8,128)S(1)} collective-permute-done((f32[1,8,16,256]{3,2,1,0:T(8,128)S(1)}, f32[1,8,16,256]{3,2,1,0:T(8,128)S(1)}, u32[]{:S(2)}, u32[]{:S(2)}) %collective-permute-start.4) | collective-permute-done | bytes 131104 | tf_op jit(solution)/shard_map/ppermute | solution.py:27
  91.2 2.1 %collective-permute-start.6 = (f32[10,1,16,256]{3,2,1,0:T(8,128)}, f32[10,1,16,256]{3,2,1,0:T(8,128)}, u32[]{:S(2)}, u32[]{:S(2)}) collective-permute-start(f32[10,1,16,256]{3,2,1,0:T(8,128)} %get-tuple-element.20), channel_id=1, source_target_pairs={{0,1},{1,2},{2,3},{4,5},{5,6},{6,7},{8,9},{9,10},{10,11},{12,13},{... | collective-permute-start | bytes 491528 | tf_op jit(solution)/shard_map/ppermute | solution.py:27
  93.4 1.5 collective-permute-start.7
  95.1 1.8 %collective-permute-done.7 = f32[10,1,16,256]{3,2,1,0:T(8,128)} collective-permute-done((f32[10,1,16,256]{3,2,1,0:T(8,128)}, f32[10,1,16,256]{3,2,1,0:T(8,128)}, u32[]{:S(2)}, u32[]{:S(2)}) %collective-permute-start.7) | collective-permute-done | bytes 163872 | tf_op jit(solution)/shard_map/ppermute | solution.py:28
  98.2 1.2 slice_add_fusion.7
  99.4 2.9 %collective-permute-start.10 = (f32[108,8,128]{2,1,0:T(8,128)S(1)}, f32[108,8,128]{2,1,0:T(8,128)S(1)}, u32[]{:S(2)}, u32[]{:S(2)}) collective-permute-start(f32[108,8,128]{2,1,0:T(8,128)S(1)} %get-tuple-element.17), channel_id=1, source_target_pairs={{0,2},{1,3},{2,0},{3,1},{4,6},{5,7},{6,4},{7,5},{8,10},{9,11},{10,... | collective-permute-start | bytes 1327112 | tf_op jit(solution)/shard_map/ppermute | solution.py:265
  102.3 1.2 slice_add_fusion.5
  103.6 2.5 %collective-permute-start.15 = (f32[108,8,128]{2,1,0:T(8,128)S(1)}, f32[108,8,128]{2,1,0:T(8,128)S(1)}, u32[]{:S(2)}, u32[]{:S(2)}) collective-permute-start(f32[108,8,128]{2,1,0:T(8,128)S(1)} %get-tuple-element.19), channel_id=1, source_target_pairs={{0,4},{4,0},{8,12},{12,8},{16,20},{20,16},{24,28},{28,24},{1,5},{5... | collective-permute-start | bytes 1327112 | tf_op jit(solution)/shard_map/ppermute | solution.py:265
  106.1 3.0 %copy-done.1 = f32[6912,256]{1,0:T(8,128)S(1)} copy-done((f32[6912,256]{1,0:T(8,128)S(1)}, f32[6912,256]{1,0:T(8,128)}, u32[]{:S(2)}) %copy-start.1) | copy-done | bytes 7077912
  109.1 14.8 %shard_map.60 = f32[1024,256]{1,0:T(8,128)} custom-call(f32[10,10,16,256]{3,2,1,0:T(8,128)S(1)} %pad_maximum_fusion.1.refs_0_, f32[1024,1]{1,0:T(8,128)S(1)} %reshape_broadcast_in_dim.4.refs_1_, f32[27,256,256]{2,1,0:T(8,128)S(1)} %bitcast.16), custom_call_target="tpu_custom_call" | custom-call | flops 10871635968 | bytes 9764864 | tf_op jit(solution)/shard_map/pallas_call | solution.py:141
  124.0 1.6 %collective-permute-start.11 = (f32[54,8,128]{2,1,0:T(8,128)S(1)}, f32[54,8,128]{2,1,0:T(8,128)S(1)}, u32[]{:S(2)}, u32[]{:S(2)}) collective-permute-start(f32[54,8,128]{2,1,0:T(8,128)S(1)} %get-tuple-element.29), channel_id=1, source_target_pairs={{0,8},{4,12},{8,0},{12,4},{16,24},{20,28},{24,16},{28,20},{1,9},{5... | collective-permute-start | bytes 663560 | tf_op jit(solution)/shard_map/ppermute | solution.py:265
  126.2 6.1 %collective-permute-done.11 = f32[54,8,128]{2,1,0:T(8,128)S(1)} collective-permute-done((f32[54,8,128]{2,1,0:T(8,128)S(1)}, f32[54,8,128]{2,1,0:T(8,128)S(1)}, u32[]{:S(2)}, u32[]{:S(2)}) %collective-permute-start.11) | collective-permute-done | bytes 221216 | tf_op jit(solution)/shard_map/ppermute | solution.py:265
  132.3 2.7 %collective-permute-start.12 = (f32[27,8,128]{2,1,0:T(8,128)S(1)}, f32[27,8,128]{2,1,0:T(8,128)S(1)}, u32[]{:S(2)}, u32[]{:S(2)}) collective-permute-start(f32[27,8,128]{2,1,0:T(8,128)S(1)} %slice_add_fusion.14), channel_id=1, source_target_pairs={{0,16},{4,20},{8,24},{12,28},{16,0},{20,4},{24,8},{28,12},{1,17},{... | collective-permute-start | bytes 331784 | tf_op jit(solution)/shard_map/ppermute | solution.py:265
  135.0 3.1 %collective-permute-done.16 = f32[54,8,128]{2,1,0:T(8,128)S(1)} collective-permute-done((f32[54,8,128]{2,1,0:T(8,128)S(1)}, f32[54,8,128]{2,1,0:T(8,128)S(1)}, u32[]{:S(2)}, u32[]{:S(2)}) %collective-permute-start.16) | collective-permute-done | bytes 221216 | tf_op jit(solution)/shard_map/ppermute | solution.py:265
  138.1 1.6 %collective-permute-start.17 = (f32[27,8,128]{2,1,0:T(8,128)S(1)}, f32[27,8,128]{2,1,0:T(8,128)S(1)}, u32[]{:S(2)}, u32[]{:S(2)}) collective-permute-start(f32[27,8,128]{2,1,0:T(8,128)S(1)} %slice_add_fusion.12), channel_id=1, source_target_pairs={{0,16},{4,20},{8,24},{12,28},{16,0},{20,4},{24,8},{28,12},{1,17},{... | collective-permute-start | bytes 331784 | tf_op jit(solution)/shard_map/ppermute | solution.py:265
  140.0 5.3 %collective-permute-done.17 = f32[27,8,128]{2,1,0:T(8,128)S(1)} collective-permute-done((f32[27,8,128]{2,1,0:T(8,128)S(1)}, f32[27,8,128]{2,1,0:T(8,128)S(1)}, u32[]{:S(2)}, u32[]{:S(2)}) %collective-permute-start.17) | collective-permute-done | bytes 110624 | tf_op jit(solution)/shard_map/ppermute | solution.py:265
  (42 shorter events, 7.6 us)
Async XLA Ops:
  3.3 7.6 %collective-permute-start = (f32[1,8,16,256]{3,2,1,0:T(8,128)S(1)}, f32[1,8,16,256]{3,2,1,0:T(8,128)S(1)}, u32[]{:S(2)}, u32[]{:S(2)}) collective-permute-start(f32[1,8,16,256]{3,2,1,0:T(8,128)S(1)} %get-tuple-element.26), channel_id=1, source_target_pairs={{0,4},{4,8},{8,12},{12,16},{16,20},{20,24},{24,28},{1,5},{5,9},{9,... | collective-permute-start | bytes 393224 | tf_op jit(solution)/shard_map/ppermute | solution.py:27
  8.1 6.9 %collective-permute-start.1 = (f32[1,8,16,256]{3,2,1,0:T(8,128)S(1)}, f32[1,8,16,256]{3,2,1,0:T(8,128)S(1)}, u32[]{:S(2)}, u32[]{:S(2)}) collective-permute-start(f32[1,8,16,256]{3,2,1,0:T(8,128)S(1)} %get-tuple-element.27), channel_id=1, source_target_pairs={{4,0},{8,4},{12,8},{16,12},{20,16},{24,20},{28,24},{5,1},{9,5},{13... | collective-permute-start | bytes 393224 | tf_op jit(solution)/shard_map/ppermute | solution.py:28
  15.0 2.7 %collective-permute-start.2 = (f32[10,1,16,256]{3,2,1,0:T(8,128)S(1)}, f32[10,1,16,256]{3,2,1,0:T(8,128)S(1)}, u32[]{:S(2)}, u32[]{:S(2)}) collective-permute-start(f32[10,1,16,256]{3,2,1,0:T(8,128)S(1)} %get-tuple-element.22), channel_id=1, source_target_pairs={{0,1},{1,2},{2,3},{4,5},{5,6},{6,7},{8,9},{9,10},{10,11},{12,13},{... | collective-permute-start | bytes 491528 | tf_op jit(solution)/shard_map/ppermute | solution.py:27
  16.3 5.0 %collective-permute-start.3 = (f32[10,1,16,256]{3,2,1,0:T(8,128)S(1)}, f32[10,1,16,256]{3,2,1,0:T(8,128)S(1)}, u32[]{:S(2)}, u32[]{:S(2)}) collective-permute-start(f32[10,1,16,256]{3,2,1,0:T(8,128)S(1)} %get-tuple-element.23), channel_id=1, source_target_pairs={{1,0},{2,1},{3,2},{5,4},{6,5},{7,6},{9,8},{10,9},{11,10},{13,12},{... | collective-permute-start | bytes 491528 | tf_op jit(solution)/shard_map/ppermute | solution.py:28
  21.5 3.0 %copy-start = (f32[6912,256]{1,0:T(8,128)S(1)}, f32[6912,256]{1,0:T(8,128)}, u32[]{:S(2)}) copy-start(f32[6912,256]{1,0:T(8,128)} %param.6) | copy-start | bytes 21233668
  54.4 7.2 %collective-permute-start.8 = (f32[432,8,128]{2,1,0:T(8,128)S(1)}, f32[432,8,128]{2,1,0:T(8,128)S(1)}, u32[]{:S(2)}, u32[]{:S(2)}) collective-permute-start(f32[432,8,128]{2,1,0:T(8,128)S(1)} %get-tuple-element.7), channel_id=1, source_target_pairs={{0,1},{1,0},{2,3},{3,2},{4,5},{5,4},{6,7},{7,6},{8,9},{9,8},{10,11... | collective-permute-start | bytes 5308424 | tf_op jit(solution)/shard_map/ppermute | solution.py:265
  58.3 6.9 %collective-permute-start.13 = (f32[432,8,128]{2,1,0:T(8,128)S(1)}, f32[432,8,128]{2,1,0:T(8,128)S(1)}, u32[]{:S(2)}, u32[]{:S(2)}) collective-permute-start(f32[432,8,128]{2,1,0:T(8,128)S(1)} %get-tuple-element.9), channel_id=1, source_target_pairs={{0,1},{1,0},{2,3},{3,2},{4,5},{5,4},{6,7},{7,6},{8,9},{9,8},{10,11... | collective-permute-start | bytes 5308424 | tf_op jit(solution)/shard_map/ppermute | solution.py:265
  62.7 35.5 %collective-permute-start.9 = (f32[216,8,128]{2,1,0:T(8,128)}, f32[216,8,128]{2,1,0:T(8,128)}, u32[]{:S(2)}, u32[]{:S(2)}) collective-permute-start(f32[216,8,128]{2,1,0:T(8,128)} %get-tuple-element.13), channel_id=1, source_target_pairs={{0,4},{4,0},{8,12},{12,8},{16,20},{20,16},{24,28},{28,24},{1,5},{5... | collective-permute-start | bytes 2654216 | tf_op jit(solution)/shard_map/ppermute | solution.py:265
  66.3 36.0 %collective-permute-start.14 = (f32[216,8,128]{2,1,0:T(8,128)}, f32[216,8,128]{2,1,0:T(8,128)}, u32[]{:S(2)}, u32[]{:S(2)}) collective-permute-start(f32[216,8,128]{2,1,0:T(8,128)} %get-tuple-element.15), channel_id=1, source_target_pairs={{0,2},{1,3},{2,0},{3,1},{4,6},{5,7},{6,4},{7,5},{8,10},{9,11},{10,... | collective-permute-start | bytes 2654216 | tf_op jit(solution)/shard_map/ppermute | solution.py:265
  66.4 24.1 %collective-permute-start.4 = (f32[1,8,16,256]{3,2,1,0:T(8,128)S(1)}, f32[1,8,16,256]{3,2,1,0:T(8,128)S(1)}, u32[]{:S(2)}, u32[]{:S(2)}) collective-permute-start(f32[1,8,16,256]{3,2,1,0:T(8,128)S(1)} %bitcast.19), channel_id=1, source_target_pairs={{0,4},{4,8},{8,12},{12,16},{16,20},{20,24},{24,28},{1,5},{5,9},{9,... | collective-permute-start | bytes 393224 | tf_op jit(solution)/shard_map/ppermute | solution.py:27
  69.8 20.7 %collective-permute-start.5 = (f32[1,8,16,256]{3,2,1,0:T(8,128)S(1)}, f32[1,8,16,256]{3,2,1,0:T(8,128)S(1)}, u32[]{:S(2)}, u32[]{:S(2)}) collective-permute-start(f32[1,8,16,256]{3,2,1,0:T(8,128)S(1)} %bitcast.18), channel_id=1, source_target_pairs={{4,0},{8,4},{12,8},{16,12},{20,16},{24,20},{28,24},{5,1},{9,5},{13... | collective-permute-start | bytes 393224 | tf_op jit(solution)/shard_map/ppermute | solution.py:28
  90.5 2.9 %copy-start.2 = (f32[1,8,16,256]{3,2,1,0:T(8,128)}, f32[1,8,16,256]{3,2,1,0:T(8,128)S(1)}, u32[]{:S(2)}) copy-start(f32[1,8,16,256]{3,2,1,0:T(8,128)S(1)} %collective-permute-done.5) | copy-start | bytes 393220
  91.2 3.9 %collective-permute-start.6 = (f32[10,1,16,256]{3,2,1,0:T(8,128)}, f32[10,1,16,256]{3,2,1,0:T(8,128)}, u32[]{:S(2)}, u32[]{:S(2)}) collective-permute-start(f32[10,1,16,256]{3,2,1,0:T(8,128)} %get-tuple-element.20), channel_id=1, source_target_pairs={{0,1},{1,2},{2,3},{4,5},{5,6},{6,7},{8,9},{9,10},{10,11},{12,13},{... | collective-permute-start | bytes 491528 | tf_op jit(solution)/shard_map/ppermute | solution.py:27
  93.4 3.6 %collective-permute-start.7 = (f32[10,1,16,256]{3,2,1,0:T(8,128)}, f32[10,1,16,256]{3,2,1,0:T(8,128)}, u32[]{:S(2)}, u32[]{:S(2)}) collective-permute-start(f32[10,1,16,256]{3,2,1,0:T(8,128)} %get-tuple-element.21), channel_id=1, source_target_pairs={{1,0},{2,1},{3,2},{5,4},{6,5},{7,6},{9,8},{10,9},{11,10},{13,12},{... | collective-permute-start | bytes 491528 | tf_op jit(solution)/shard_map/ppermute | solution.py:28
  99.4 24.5 %collective-permute-start.10 = (f32[108,8,128]{2,1,0:T(8,128)S(1)}, f32[108,8,128]{2,1,0:T(8,128)S(1)}, u32[]{:S(2)}, u32[]{:S(2)}) collective-permute-start(f32[108,8,128]{2,1,0:T(8,128)S(1)} %get-tuple-element.17), channel_id=1, source_target_pairs={{0,2},{1,3},{2,0},{3,1},{4,6},{5,7},{6,4},{7,5},{8,10},{9,11},{10,... | collective-permute-start | bytes 1327112 | tf_op jit(solution)/shard_map/ppermute | solution.py:265
  103.6 22.0 %collective-permute-start.15 = (f32[108,8,128]{2,1,0:T(8,128)S(1)}, f32[108,8,128]{2,1,0:T(8,128)S(1)}, u32[]{:S(2)}, u32[]{:S(2)}) collective-permute-start(f32[108,8,128]{2,1,0:T(8,128)S(1)} %get-tuple-element.19), channel_id=1, source_target_pairs={{0,4},{4,0},{8,12},{12,8},{16,20},{20,16},{24,28},{28,24},{1,5},{5... | collective-permute-start | bytes 1327112 | tf_op jit(solution)/shard_map/ppermute | solution.py:265
  106.1 3.0 %copy-start.1 = (f32[6912,256]{1,0:T(8,128)S(1)}, f32[6912,256]{1,0:T(8,128)}, u32[]{:S(2)}) copy-start(f32[6912,256]{1,0:T(8,128)} %param.6) | copy-start | bytes 21233668
  124.0 8.4 %collective-permute-start.11 = (f32[54,8,128]{2,1,0:T(8,128)S(1)}, f32[54,8,128]{2,1,0:T(8,128)S(1)}, u32[]{:S(2)}, u32[]{:S(2)}) collective-permute-start(f32[54,8,128]{2,1,0:T(8,128)S(1)} %get-tuple-element.29), channel_id=1, source_target_pairs={{0,8},{4,12},{8,0},{12,4},{16,24},{20,28},{24,16},{28,20},{1,9},{5... | collective-permute-start | bytes 663560 | tf_op jit(solution)/shard_map/ppermute | solution.py:265
  125.7 12.4 %collective-permute-start.16 = (f32[54,8,128]{2,1,0:T(8,128)S(1)}, f32[54,8,128]{2,1,0:T(8,128)S(1)}, u32[]{:S(2)}, u32[]{:S(2)}) collective-permute-start(f32[54,8,128]{2,1,0:T(8,128)S(1)} %get-tuple-element.31), channel_id=1, source_target_pairs={{0,8},{4,12},{8,0},{12,4},{16,24},{20,28},{24,16},{28,20},{1,9},{5... | collective-permute-start | bytes 663560 | tf_op jit(solution)/shard_map/ppermute | solution.py:265
  132.3 7.4 %collective-permute-start.12 = (f32[27,8,128]{2,1,0:T(8,128)S(1)}, f32[27,8,128]{2,1,0:T(8,128)S(1)}, u32[]{:S(2)}, u32[]{:S(2)}) collective-permute-start(f32[27,8,128]{2,1,0:T(8,128)S(1)} %slice_add_fusion.14), channel_id=1, source_target_pairs={{0,16},{4,20},{8,24},{12,28},{16,0},{20,4},{24,8},{28,12},{1,17},{... | collective-permute-start | bytes 331784 | tf_op jit(solution)/shard_map/ppermute | solution.py:265
  138.1 7.1 %collective-permute-start.17 = (f32[27,8,128]{2,1,0:T(8,128)S(1)}, f32[27,8,128]{2,1,0:T(8,128)S(1)}, u32[]{:S(2)}, u32[]{:S(2)}) collective-permute-start(f32[27,8,128]{2,1,0:T(8,128)S(1)} %slice_add_fusion.12), channel_id=1, source_target_pairs={{0,16},{4,20},{8,24},{12,28},{16,0},{20,4},{24,8},{28,12},{1,17},{... | collective-permute-start | bytes 331784 | tf_op jit(solution)/shard_map/ppermute | solution.py:265

commit v2 on v0

v2 whole, which is shorter than its diff:
```python
import jax
import jax.numpy as jnp
import numpy as np
from jax import lax
from jax.experimental import pallas as pl
from jax.experimental.pallas import tpu as pltpu
from jax.sharding import PartitionSpec as P

F32 = jnp.float32
BF16 = jnp.bfloat16
LANES = 128


def split(value):
    high = value.astype(BF16)
    low = (value - high.astype(F32)).astype(BF16)
    return high, low


def shift_rows(value, step, depth):
    rows = value.shape[0]
    place = lax.broadcasted_iota(jnp.int32, value.shape, 0) % depth
    moved = pltpu.roll(value, (-step) % rows, 0)
    inside = (place + step >= 0) & (place + step < depth)
    return jnp.where(inside, moved, 0.0)


def stack_terms(value):
    return jnp.concatenate(split(value), axis=-1)


def products(piece, high, low, dim):
    channels = high.shape[0]

    def dot(left, right):
        return lax.dot_general(
            left, right, (((1,), (dim,)), ((), ())), preferred_element_type=F32
        )

    own_high, own_low = piece[:, :channels], piece[:, channels:]
    return dot(own_high, high) + dot(own_low, high) + dot(own_high, low)


WHOLE = pl.BlockSpec(memory_space=pltpu.VMEM)


def params(mib):
    return pltpu.CompilerParams(vmem_limit_bytes=mib * 1024 * 1024)


def padded_slab(index, span, own, before_x, after_x, before_y, after_y):
    if index == 0:
        middle = before_x[0]
    elif index == span + 1:
        middle = after_x[0]
    else:
        middle = own(index - 1)
    return jnp.concatenate([before_y[index], middle, after_y[index]], axis=0)


def forward_kernel(
    swap_ref,
    inputs_ref,
    filled_ref,
    before_x_ref,
    after_x_ref,
    before_y_ref,
    after_y_ref,
    cot_ref,
    weight_ref,
    up_ref,
    turned_ref,
    right_ref,
    stack_ref,
    acc_ref,
    slab_ref,
):
    step = pl.program_id(0)
    span_x, span_y, depth, channels = inputs_ref.shape
    count, side = span_x * span_y * depth, span_y * depth

    @pl.when(step == 0)
    def _():
        for i in range(span_x + 2):
            slab = padded_slab(
                i,
                span_x,
                lambda x: inputs_ref[x] * filled_ref[x],
                before_x_ref,
                after_x_ref,
                before_y_ref,
                after_y_ref,
            )
            slab_ref[i] = slab
            stack_ref[i] = stack_terms(slab)
        acc_ref[...] = jnp.zeros_like(acc_ref)

    first, second = step // 3, step % 3
    piece = stack_ref[pl.ds(first, span_x), pl.ds(second, span_y)].reshape(count, 2 * channels)
    for third in range(3):
        acc_ref[third] += products(piece, *split(weight_ref[3 * step + third]), 0)

    each = -(-(span_x + 2) // 3)
    groups = channels // 16
    for j in range(each):
        i = jnp.minimum(first * each + j, span_x + 1)
        turn = slab_ref[i, pl.ds(second, span_y)].reshape(side, channels).T
        high, low = split(turn)
        lanes = pl.ds(pl.multiple_of(i * side, LANES), side)
        for m in range(groups):
            at = (m % 2) * 3 * (channels // 2) + 16 * (m // 2)
            rows = pl.ds(pl.multiple_of(at + second * (channels // 2), 16), 16)
            turned_ref[0, rows, lanes] = high[16 * m : 16 * m + 16]
            turned_ref[1, rows, lanes] = low[16 * m : 16 * m + 16]

    @pl.when(step == 8)
    def _():
        preact = (
            acc_ref[1] + shift_rows(acc_ref[0], -1, depth) + shift_rows(acc_ref[2], 1, depth)
        )
        sigma = jax.nn.sigmoid(preact)
        cot = cot_ref[...] * filled_ref[...].reshape(count, 1)
        upstream = cot * sigma * (1.0 + preact * (1.0 - sigma))
        up_ref[...] = upstream

        left, right = upstream[:, :LANES], upstream[:, LANES:]
        swap_high, swap_low = swap_ref[0] > 0, swap_ref[1] > 0
        left, right = jnp.where(swap_high, right, left), jnp.where(swap_high, left, right)
        left = jnp.where(swap_low, pltpu.roll(left, 64, 1), left)
        right = jnp.where(swap_low, pltpu.roll(right, 64, 1), right)
        ordered = jnp.concatenate([left, right], axis=1)
        for third in range(3):
            high, low = split(shift_rows(ordered, 1 - third, depth))
            right_ref[third, 0] = high
            right_ref[third, 1] = low


def forward(swap, inputs, filled, before_x, after_x, before_y, after_y, cot, taps):
    span_x, span_y, depth, channels = inputs.shape
    count = span_x * span_y * depth
    turned = (2, 3 * channels, (span_x + 2) * span_y * depth)
    right = (3, 2, count, channels)
    return pl.pallas_call(
        forward_kernel,
        grid=(9,),
        in_specs=[pl.BlockSpec(memory_space=pltpu.SMEM)]
        + [WHOLE] * 8,
        out_specs=[WHOLE] * 3,
        out_shape=[
            jax.ShapeDtypeStruct((count, channels), F32),
            jax.ShapeDtypeStruct(turned, BF16),
            jax.ShapeDtypeStruct(right, BF16),
        ],
        scratch_shapes=[
            pltpu.VMEM((span_x + 2, span_y + 2, depth, 2 * channels), BF16),
            pltpu.VMEM((3, count, channels), F32),
            pltpu.VMEM((span_x + 2, span_y + 2, depth, channels), F32),
        ],
        compiler_params=params(24),
        cost_estimate=pl.CostEstimate(
            flops=2 * 81 * count * channels * channels,
            bytes_accessed=4 * (8 * inputs.size + taps.size),
            transcendentals=count * channels,
        ),
    )(swap, inputs, filled, before_x, after_x, before_y, after_y, cot, taps)


def filter_kernel(part, side, place_ref, turned_ref, right_ref, keep_ref, send_ref, acc_ref):
    count, channels = right_ref.shape[2:]
    low_lanes = lax.broadcasted_iota(jnp.int32, (8, LANES), 1) < 64
    keep_jump, send_jump = place_ref[0, 0], place_ref[1, 0]
    seen = 0
    rows = 3 * (channels // 2)
    base = part * rows
    for third in range(3):
        for first in range(3):
            lanes = slice(first * side, first * side + count)
            high = turned_ref[0, base : base + rows, lanes]
            low = turned_ref[1, base : base + rows, lanes]
            acc_ref[...] = (
                jnp.dot(high, right_ref[third, 0], preferred_element_type=F32)
                + jnp.dot(low, right_ref[third, 0], preferred_element_type=F32)
                + jnp.dot(high, right_ref[third, 1], preferred_element_type=F32)
            )
            for group in range(rows // 16):
                keep_at, send_at = place_ref[0, 1 + seen], place_ref[1, 1 + seen]
                seen += 1
                start = group * 16
                for high_half in range(2):
                    columns = slice(high_half * LANES, (high_half + 1) * LANES)
                    upper = acc_ref[start : start + 8, columns]
                    lower = acc_ref[start + 8 : start + 16, columns]
                    keep_ref[keep_at + high_half * keep_jump] = jnp.where(
                        low_lanes, upper, pltpu.roll(lower, 64, 1)
                    )
                    send_ref[send_at + high_half * send_jump] = jnp.where(
                        low_lanes, pltpu.roll(upper, 64, 1), lower
                    )


def filter_terms(part, place, turned, right, tiles, side):
    count, channels = right.shape[2:]

    def kernel(*refs):
        filter_kernel(part, side, *refs)

    shape = jax.ShapeDtypeStruct((tiles, 8, LANES), F32)
    return pl.pallas_call(
        kernel,
        in_specs=[pl.BlockSpec(memory_space=pltpu.SMEM), WHOLE, WHOLE],
        out_specs=[WHOLE] * 2,
        out_shape=[shape] * 2,
        scratch_shapes=[pltpu.VMEM((3 * channels // 2, channels), F32)],
        compiler_params=params(12),
        cost_estimate=pl.CostEstimate(
            flops=81 * count * channels * channels,
            bytes_accessed=2 * (turned.size + right.size) + 8 * tiles * 8 * LANES,
            transcendentals=0,
        ),
    )(place, turned, right)


def unit_tables(channels, size_x):
    groups = channels // 16
    units = 27 * groups // size_x
    tables = []
    for part in range(2):
        order = [
            (first * 9 + second * 3 + third) * groups + m
            for third in range(3)
            for first in range(3)
            for second in range(3)
            for m in range(part, groups, 2)
        ]
        unit = np.array(order, np.int32)
        tables.append((unit // units, unit % units // 2))
    return tables


def data_kernel(
    begin,
    end,
    turn_ref,
    up_ref,
    filled_ref,
    before_x_ref,
    after_x_ref,
    before_y_ref,
    after_y_ref,
    weight_ref,
    out_ref,
    stack_ref,
    acc_ref,
):
    step = pl.program_id(0)
    span_x, span_y, depth, channels = up_ref.shape
    width = end - begin
    count = width * span_y * depth

    @pl.when(step == 0)
    def _():
        for i in range(width + 2):
            stack_ref[i] = stack_terms(
                padded_slab(
                    begin + i,
                    span_x,
                    lambda x: up_ref[x],
                    before_x_ref,
                    after_x_ref,
                    before_y_ref,
                    after_y_ref,
                )
            )
        acc_ref[...] = jnp.zeros_like(acc_ref)

    first, second = step // 3, step % 3
    piece = stack_ref[pl.ds(2 - first, width), pl.ds(2 - second, span_y)].reshape(
        count, 2 * channels
    )
    for third in range(3):
        acc_ref[third] += products(piece, *split(weight_ref[3 * step + third]), 1)

    @pl.when(step == 8)
    def _():
        total = acc_ref[1] + shift_rows(acc_ref[0], 1, depth) + shift_rows(acc_ref[2], -1, depth)
        out_ref[...] = total * filled_ref[begin:end].reshape(count, 1)


def data_grad(turn, up, filled, before_x, after_x, before_y, after_y, taps, begin, end):
    span_x, span_y, depth, channels = up.shape
    width = end - begin
    count = width * span_y * depth

    def kernel(*refs):
        data_kernel(begin, end, *refs)

    return pl.pallas_call(
        kernel,
        grid=(9,),
        in_specs=[pl.BlockSpec(memory_space=pltpu.SMEM)] + [WHOLE] * 7,
        out_specs=WHOLE,
        out_shape=jax.ShapeDtypeStruct((count, channels), F32),
        scratch_shapes=[
            pltpu.VMEM((width + 2, span_y + 2, depth, 2 * channels), BF16),
            pltpu.VMEM((3, count, channels), F32),
        ],
        compiler_params=params(16),
        cost_estimate=pl.CostEstimate(
            flops=2 * 81 * count * channels * channels,
            bytes_accessed=4 * (3 * count * channels + taps.size),
            transcendentals=0,
        ),
    )(turn, up, filled, before_x, after_x, before_y, after_y, taps)


def bits_of(size):
    return size.bit_length() - 1


def after(value, *others):
    return lax.optimization_barrier((value, *others))[0]


def neighbours(axis):
    size = lax.axis_size(axis)
    up = [(i, i + 1) for i in range(size - 1)]
    return up, [(j, i) for i, j in up]


def halo_x(first, last):
    up, down = neighbours("gx")
    return lax.ppermute(last, "gx", up), lax.ppermute(first, "gx", down)


def halo_y(first, last, before_x, after_x):
    up, down = neighbours("gy")
    span_y = before_x.shape[1]
    low = jnp.concatenate([before_x[:, 0], first, after_x[:, 0]], axis=0)
    high = jnp.concatenate([before_x[:, span_y - 1], last, after_x[:, span_y - 1]], axis=0)
    got = lax.ppermute(high[:, None], "gy", up), lax.ppermute(low[:, None], "gy", down)
    return got


def flip_pairs(size_x, size_y, flips):
    pairs = []
    for x in range(size_x):
        for y in range(size_y):
            axis, bit = flips[y & 1]
            other = (x ^ (1 << bit), y) if axis == "gx" else (x, y ^ (1 << bit))
            pairs.append((x * size_y + y, other[0] * size_y + other[1]))
    return pairs


def plain_filter_grad(bordered, upstream, span_x, span_y, depth):
    padded = jnp.pad(bordered, ((0, 0), (0, 0), (1, 1), (0, 0)))
    blocks = []
    for first in range(3):
        for second in range(3):
            for third in range(3):
                piece = padded[
                    first : first + span_x, second : second + span_y, third : third + depth
                ].reshape(upstream.shape)
                blocks.append(
                    jnp.dot(
                        piece.T,
                        upstream,
                        precision=lax.Precision.HIGHEST,
                        preferred_element_type=F32,
                    )
                )
    term = jnp.concatenate(blocks, axis=0)
    row_sums = lax.psum_scatter(term, "gx", scatter_dimension=0, tiled=True)
    return lax.psum_scatter(row_sums, "gy", scatter_dimension=1, tiled=True)


def body(inputs, cotangent, weight, occupancy):
    span_x, span_y, depth, channels = inputs.shape
    count = span_x * span_y * depth
    size_x, size_y = lax.axis_size("gx"), lax.axis_size("gy")
    me_x, me_y = lax.axis_index("gx"), lax.axis_index("gy")
    filled = occupancy.astype(F32)[..., None]
    taps = weight.reshape(27, channels, channels)
    cot = cotangent.reshape(count, channels)

    def masked(x, y):
        return inputs[x, y] * filled[x, y]

    every = slice(None)
    last_x, last_y = span_x - 1, span_y - 1
    face, other_face = masked(slice(0, 1), every), masked(slice(last_x, span_x), every)
    before_x, after_x = halo_x(face, other_face)
    before_y, after_y = halo_y(masked(every, 0), masked(every, last_y), before_x, after_x)
    swap = jnp.stack([(me_y >> 1) & 1, me_y & 1]).astype(jnp.int32)
    upstream, turned, right = forward(
        swap,
        inputs,
        filled,
        before_x,
        after_x,
        before_y.reshape(span_x + 2, 1, depth, channels),
        after_y.reshape(span_x + 2, 1, depth, channels),
        cot,
        taps,
    )
    up = upstream.reshape(inputs.shape)

    def data_halo_x(*others):
        first, last = up[:1], up[last_x:]
        for other in others:
            first, last, _ = lax.optimization_barrier((first, last, other))
        return halo_x(first, last)

    def data_halo_y(sides, *others):
        first, last = up[:, 0], up[:, last_y]
        for other in others:
            first, last, _ = lax.optimization_barrier((first, last, other))
        return halo_y(first, last, *sides)

    def data_piece(turn, sides, ends, begin, end):
        return data_grad(turn, up, filled, *sides, *ends, taps, begin, end)

    middle = span_x // 2
    parts, groups = 2, channels // 16
    if channels // size_y != 64 or 27 * groups % (parts * size_x) or channels != 256:
        own = inputs * filled
        bordered = jnp.concatenate(
            [before_y, jnp.concatenate([before_x, own, after_x], axis=0), after_y], axis=1
        )
        weight_grad = plain_filter_grad(bordered, upstream, span_x, span_y, depth)
        sides = data_halo_x()
        result = data_piece(swap, sides, data_halo_y(sides), 0, span_x)
        return (result.reshape(inputs.shape), weight_grad)

    units = 27 * groups // size_x // parts
    rest = [("gx", b) for b in range(1, bits_of(size_x))]
    x_bit, y_bit = ("gx", 0), ("gy", 1)
    paths = [
        ([x_bit, y_bit] + rest, [y_bit, x_bit] + rest),
        ([y_bit, x_bit] + rest, rest + [x_bit, y_bit]),
    ]
    tiles = 2 * size_x * units
    core = [(i, i ^ 1) for i in range(size_y)]
    tables = []
    for part, (chunk, place) in enumerate(unit_tables(channels, size_x)):
        relative = jnp.asarray(chunk) ^ me_x
        ways = []
        for path in paths[part]:
            at, jump = jnp.zeros_like(relative), 0
            for position, (axis, bit) in enumerate(path):
                worth = 1 << (len(path) - 1 - position)
                if axis == "gx":
                    at = at + ((relative >> bit) & 1) * worth
                else:
                    jump = worth * units
            at = at * units + jnp.asarray(place)
            ways.append(jnp.concatenate([jnp.full((1,), jump, jnp.int32), at]))
        tables.append(jnp.where(me_y & 1, jnp.stack(ways[::-1]), jnp.stack(ways)))
    flips = [list(zip(*path)) for path in paths]
    stages = len(flips[0])

    def terms(part, table):
        keep, send = filter_terms(part, table, turned, right, tiles, span_y * depth)
        return keep, send, lax.ppermute(send, "gy", core)

    def stage(part, index, keep, got):
        half = keep.shape[0] // 2
        send, keep = keep[half:] + got[half:], keep[:half] + got[:half]
        pairs = flip_pairs(size_x, size_y, flips[part][index])
        return keep, send, lax.ppermute(send, ("gx", "gy"), pairs)

    keep_a, send_a, got_a = terms(0, tables[0])
    sides = data_halo_x(send_a)
    keep_a, send_a, got_a = stage(0, 0, keep_a, got_a)
    keep_b, send_b, got_b = terms(1, after(tables[1], send_a, *sides))
    ends = data_halo_y(sides, send_b)
    keep_b, send_b, got_b = stage(1, 0, keep_b, got_b)
    keep_a, send_a, got_a = stage(0, 1, keep_a, got_a)
    pieces = []
    for index in range(2, stages):
        if index < 4:
            begin, end = ((0, middle), (middle, span_x))[index - 2]
            pieces.append(data_piece(after(swap, send_a, send_b), sides, ends, begin, end))
            keep_a, keep_b = after(keep_a, pieces[-1]), after(keep_b, pieces[-1])
        keep_a, send_a, got_a = stage(0, index, keep_a, got_a)
        keep_b, send_b, got_b = stage(1, index - 1, keep_b, got_b)
    keep_b, send_b, got_b = stage(1, stages - 1, keep_b, got_b)
    sums = [keep_a + got_a, keep_b + got_b]
    both = jnp.stack([s.reshape(units, 8, 2, 64) for s in sums], axis=1)
    weight_grad = both.transpose(0, 1, 3, 2, 4).reshape(units * 32, 64)
    return (jnp.concatenate(pieces, axis=0).reshape(inputs.shape), weight_grad)


def solution(mesh):
    in_specs = (P("gx", "gy", None, None), P("gx", "gy", None, None), P(), P("gx", "gy", None))
    out_specs = (P("gx", "gy", None, None), P("gx", "gy"))
    return jax.shard_map(body, mesh=mesh, in_specs=in_specs, out_specs=out_specs, check_vma=False)
```

time: 354 us -> 124 us (0.35)
  matrix products: 222 us -> 0 us
  Pallas kernels: 0 us -> 46 us
  waiting for transfers between devices: 69.7 us -> 27 us
  starting transfers between devices: 20.8 us -> 38.4 us
  between operations: 14.8 us -> 0.94 us
  local copies, waits for them, and re-layouts: 17.5 us -> 4.8 us
    dot_general x81 -> x0, matrix products: 222 us -> none  [the longest x27 81.6 us: body(): jnp.dot(piece, weight[index * channels:(index + 1) * channels], precision...]
    reduce_scatter x1 -> x0, waiting for transfers between devices: 55.6 us -> none  [body(): row_sums = lax.psum_scatter(term, 'gx', scatter_dimension=0, tiled=True)]
    pallas_call x0 -> x5, Pallas kernels: none -> 46 us  [the longest x2 17.3 us: data_grad(): pl.pallas_call(kernel, grid=(9,), in_specs=[pl.BlockSpec(memory_space=plt...]
    ppermute x8 -> x18, waiting for transfers between devices: 5.85 us -> 27 us  [the longest x8 17.5 us: stage(): return (keep, send, lax.ppermute(send, ('gx', 'gy'), pairs))]
    ppermute x8 -> x18, starting transfers between devices: 20.3 us -> 38.4 us  [the longest x8 14.7 us: stage(): return (keep, send, lax.ppermute(send, ('gx', 'gy'), pairs))]
    slice x7 -> x2, local copies, waits for them, and re-layouts: 13.7 us -> 0.03 us  [the longest x1 0.02 us: data_halo_x(): first, last = (up[:1], up[last_x:])]
    unnamed x3 -> x0, waiting for transfers between devices: 8.28 us -> none
  transfers between devices with their start and end apart: 10 -> 18, of which waited for: 4 -> 9; matrix products, arithmetic and copies ran while one was open for 25% -> 4% of each run, Pallas kernels for 0% -> 14%
where the time goes in v2:
time: 124 us
  Pallas kernels  46 us (37%)
  starting transfers between devices  38.4 us (31%)
  waiting for transfers between devices  27 us (22%)
  other arithmetic  6.72 us (5%)
  local copies, waits for them, and re-layouts  4.8 us (4%)
    ppermute x8, waiting for transfers between devices, stage(): return (keep, send, lax.ppermute(send, ('gx', 'gy'), pairs))  17.5 us
    pallas_call x2, Pallas kernels, data_grad(): pl.pallas_call(kernel, grid=(9,), in_specs=[pl.BlockSpec(memory_space=plt...  17.3 us
    pallas_call x1, Pallas kernels, forward(): pl.pallas_call(forward_kernel, grid=(9,), in_specs=[pl.BlockSpec(memory_s...  15.5 us
    ppermute x8, starting transfers between devices, stage(): return (keep, send, lax.ppermute(send, ('gx', 'gy'), pairs))  14.7 us
    pallas_call x2, Pallas kernels, filter_terms(): pl.pallas_call(kernel, in_specs=[pl.BlockSpec(memory_space=pltpu.SMEM), W...  13.2 us
    ppermute x4, starting transfers between devices, halo_x(): return (lax.ppermute(last, 'gx', up), lax.ppermute(first, 'gx', down))  12 us
    ppermute x4, waiting for transfers between devices, halo_x(): return (lax.ppermute(last, 'gx', up), lax.ppermute(first, 'gx', down))  8.86 us
    ppermute x2, starting transfers between devices, halo_y(): lax.ppermute(high[:, None], 'gy', up)  6.47 us
  transfers between devices with their start and end apart: 18, of which 9 were waited for; matrix products, arithmetic and copies ran while one was open for 4% of the time, Pallas kernels for 14%

profile of v2, /device:TPU:0, one launch (start us, length us, event | category | flops | bytes accessed | tf_op | source)
XLA Modules:
  0.0 123.9 jit_solution(1455595134943528369)
XLA Ops:
  1.6 1.1 slice_multiply_fusion
  2.6 4.8 %collective-permute-start = (f32[1,8,16,256]{3,2,1,0:T(8,128)S(1)}, f32[1,8,16,256]{3,2,1,0:T(8,128)S(1)}, u32[]{:S(2)}, u32[]{:S(2)}) collective-permute-start(f32[1,8,16,256]{3,2,1,0:T(8,128)S(1)} %get-tuple-element.55), channel_id=1, source_target_pairs={{0,4},{4,8},{8,12},{12,16},{16,20},{20,24},{24,28},{1,5},{5,9},{9,... | collective-permute-start | bytes 393224 | tf_op jit(solution)/shard_map/ppermute | solution.py:332
  7.5 1.3 %collective-permute-start.1 = (f32[1,8,16,256]{3,2,1,0:T(8,128)S(1)}, f32[1,8,16,256]{3,2,1,0:T(8,128)S(1)}, u32[]{:S(2)}, u32[]{:S(2)}) collective-permute-start(f32[1,8,16,256]{3,2,1,0:T(8,128)S(1)} %get-tuple-element.54), channel_id=1, source_target_pairs={{4,0},{8,4},{12,8},{16,12},{20,16},{24,20},{28,24},{5,1},{9,5},{13... | collective-permute-start | bytes 393224 | tf_op jit(solution)/shard_map/ppermute | solution.py:332
  8.8 1.1 bitcast_multiply_fusion
  10.8 3.6 %collective-permute-done.1.after_x_ref = f32[1,8,16,256]{3,2,1,0:T(8,128)S(1)} collective-permute-done((f32[1,8,16,256]{3,2,1,0:T(8,128)S(1)}, f32[1,8,16,256]{3,2,1,0:T(8,128)S(1)}, u32[]{:S(2)}, u32[]{:S(2)}) %collective-permute-start.1) | collective-permute-done | bytes 131104 | tf_op jit(solution)/shard_map/ppermute | solution.py:332
  14.4 1.3 %collective-permute-start.3 = (f32[10,1,16,256]{3,2,1,0:T(8,128)S(1)}, f32[10,1,16,256]{3,2,1,0:T(8,128)S(1)}, u32[]{:S(2)}, u32[]{:S(2)}) collective-permute-start(f32[10,1,16,256]{3,2,1,0:T(8,128)S(1)} %maximum_bitcast_fusion.1), channel_id=1, source_target_pairs={{1,0},{2,1},{3,2},{5,4},{6,5},{7,6},{9,8},{10,9},{11,10},{13,12},{... | collective-permute-start | bytes 491528 | tf_op jit(solution)/shard_map/ppermute | solution.py:340
  16.4 3.0 %collective-permute-start.2 = (f32[10,1,16,256]{3,2,1,0:T(8,128)}, f32[10,1,16,256]{3,2,1,0:T(8,128)S(1)}, u32[]{:S(2)}, u32[]{:S(2)}) collective-permute-start(f32[10,1,16,256]{3,2,1,0:T(8,128)} %maximum_bitcast_fusion), channel_id=1, source_target_pairs={{0,1},{1,2},{2,3},{4,5},{5,6},{6,7},{8,9},{9,10},{10,11},{12,13},{... | collective-permute-start | bytes 491528 | tf_op jit(solution)/shard_map/ppermute | solution.py:340
  20.6 3.0 %copy-done.1 = f32[6912,256]{1,0:T(8,128)S(1)} copy-done((f32[6912,256]{1,0:T(8,128)S(1)}, f32[6912,256]{1,0:T(8,128)}, u32[]{:S(2)}) %copy-start.1) | copy-done | bytes 7077912
  23.6 15.5 %shard_map.95 = (f32[1024,256]{1,0:T(8,128)S(1)}, bf16[2,768,1280]{2,1,0:T(8,128)(2,1)S(1)}, bf16[3,2,1024,256]{3,2,1,0:T(8,128)(2,1)S(1)}) custom-call(s32[2]{0:T(128)S(1)} %pad_add_fusion.7.swap_ref.refs_0_, f32[8,8,16,256]{3,2,1,0:T(8,128)S(1)} %copy-done, f32[8,8,16,1]{3,2,1,0:T(8,128)S(1)} %copy.19.filled_ref.refs_2_, ...), custom_call_target="tpu_custom_call" | custom-call | flops 10871635968 | bytes 15466496 | tf_op jit(solution)/shard_map/pallas_call | solution.py:143
  39.2 6.6 %shard_map.96 = (f32[432,8,128]{2,1,0:T(8,128)S(1)}, f32[432,8,128]{2,1,0:T(8,128)S(1)}) custom-call(s32[2,217]{1,0:T(2,128)S(1)} %get-tuple-element.78.refs_0_, bf16[2,768,1280]{2,1,0:T(8,128)(2,1)S(1)} %get-tuple-element.20.refs_1_, bf16[3,2,1024,256]{3,2,1,0:T(8,128)(2,1)S(1)} %get-tuple-element.21.refs_2_), custom_call_target="tpu_custom_call" | custom-call | flops 5435817984 | bytes 10616832 | tf_op jit(solution)/shard_map/pallas_call | solution.py:208
  45.8 2.5 %collective-permute-start.4 = (f32[432,8,128]{2,1,0:T(8,128)S(1)}, f32[432,8,128]{2,1,0:T(8,128)S(1)}, u32[]{:S(2)}, u32[]{:S(2)}) collective-permute-start(f32[432,8,128]{2,1,0:T(8,128)S(1)} %get-tuple-element.23), channel_id=1, source_target_pairs={{0,1},{1,0},{2,3},{3,2},{4,5},{5,4},{6,7},{7,6},{8,9},{9,8},{10,11... | collective-permute-start | bytes 5308424 | tf_op jit(solution)/shard_map/ppermute | solution.py:463
  48.4 4.4 %collective-permute-start.6 = (f32[1,8,16,256]{3,2,1,0:T(8,128)S(1)}, f32[1,8,16,256]{3,2,1,0:T(8,128)S(1)}, u32[]{:S(2)}, u32[]{:S(2)}) collective-permute-start(f32[1,8,16,256]{3,2,1,0:T(8,128)S(1)} %bitcast.72), channel_id=1, source_target_pairs={{0,4},{4,8},{8,12},{12,16},{16,20},{20,24},{24,28},{1,5},{5,9},{9,... | collective-permute-start | bytes 393224 | tf_op jit(solution)/shard_map/ppermute | solution.py:332
  52.8 1.5 %collective-permute-start.7 = (f32[1,8,16,256]{3,2,1,0:T(8,128)S(1)}, f32[1,8,16,256]{3,2,1,0:T(8,128)S(1)}, u32[]{:S(2)}, u32[]{:S(2)}) collective-permute-start(f32[1,8,16,256]{3,2,1,0:T(8,128)S(1)} %bitcast.71), channel_id=1, source_target_pairs={{4,0},{8,4},{12,8},{16,12},{20,16},{24,20},{28,24},{5,1},{9,5},{13... | collective-permute-start | bytes 393224 | tf_op jit(solution)/shard_map/ppermute | solution.py:332
  54.5 1.1 collective-permute-done.6.refs_3_
  55.7 4.1 %collective-permute-done.7.refs_4_ = f32[1,8,16,256]{3,2,1,0:T(8,128)S(1)} collective-permute-done((f32[1,8,16,256]{3,2,1,0:T(8,128)S(1)}, f32[1,8,16,256]{3,2,1,0:T(8,128)S(1)}, u32[]{:S(2)}, u32[]{:S(2)}) %collective-permute-start.7) | collective-permute-done | bytes 131104 | tf_op jit(solution)/shard_map/ppermute | solution.py:332
  59.8 6.6 %shard_map.97 = (f32[432,8,128]{2,1,0:T(8,128)S(1)}, f32[432,8,128]{2,1,0:T(8,128)S(1)}) custom-call(s32[2,217]{1,0:T(2,128)S(1)} %get-tuple-element.27.refs_0_, bf16[2,768,1280]{2,1,0:T(8,128)(2,1)S(1)} %get-tuple-element.20.refs_1_, bf16[3,2,1024,256]{3,2,1,0:T(8,128)(2,1)S(1)} %get-tuple-element.21.refs_2_), custom_call_target="tpu_custom_call" | custom-call | flops 5435817984 | bytes 10616832 | tf_op jit(solution)/shard_map/pallas_call | solution.py:208
  66.5 2.1 %collective-permute-start.5 = (f32[216,8,128]{2,1,0:T(8,128)S(1)}, f32[216,8,128]{2,1,0:T(8,128)S(1)}, u32[]{:S(2)}, u32[]{:S(2)}) collective-permute-start(f32[216,8,128]{2,1,0:T(8,128)S(1)} %get-tuple-element.43), channel_id=1, source_target_pairs={{0,4},{1,3},{2,6},{3,1},{4,0},{5,7},{6,2},{7,5},{8,12},{9,11},{10,... | collective-permute-start | bytes 2654216 | tf_op jit(solution)/shard_map/ppermute | solution.py:469
  68.7 1.3 %collective-permute-start.10 = (f32[10,1,16,256]{3,2,1,0:T(8,128)S(1)}, f32[10,1,16,256]{3,2,1,0:T(8,128)S(1)}, u32[]{:S(2)}, u32[]{:S(2)}) collective-permute-start(f32[10,1,16,256]{3,2,1,0:T(8,128)S(1)} %maximum_bitcast_fusion.3), channel_id=1, source_target_pairs={{1,0},{2,1},{3,2},{5,4},{6,5},{7,6},{9,8},{10,9},{11,10},{13,12},{... | collective-permute-start | bytes 491528 | tf_op jit(solution)/shard_map/ppermute | solution.py:340
  70.0 3.4 %collective-permute-start.9 = (f32[10,1,16,256]{3,2,1,0:T(8,128)S(1)}, f32[10,1,16,256]{3,2,1,0:T(8,128)S(1)}, u32[]{:S(2)}, u32[]{:S(2)}) collective-permute-start(f32[10,1,16,256]{3,2,1,0:T(8,128)S(1)} %maximum_bitcast_fusion.2), channel_id=1, source_target_pairs={{0,1},{1,2},{2,3},{4,5},{5,6},{6,7},{8,9},{9,10},{10,11},{12,13},{... | collective-permute-start | bytes 491528 | tf_op jit(solution)/shard_map/ppermute | solution.py:340
  73.7 2.4 %collective-permute-start.12 = (f32[216,8,128]{2,1,0:T(8,128)S(1)}, f32[216,8,128]{2,1,0:T(8,128)S(1)}, u32[]{:S(2)}, u32[]{:S(2)}) collective-permute-start(f32[216,8,128]{2,1,0:T(8,128)S(1)} %get-tuple-element.41), channel_id=1, source_target_pairs={{0,2},{1,9},{2,0},{3,11},{4,6},{5,13},{6,4},{7,15},{8,10},{9,1},{1... | collective-permute-start | bytes 2654216 | tf_op jit(solution)/shard_map/ppermute | solution.py:469
  76.1 3.5 %collective-permute-done.5 = f32[216,8,128]{2,1,0:T(8,128)S(1)} collective-permute-done((f32[216,8,128]{2,1,0:T(8,128)S(1)}, f32[216,8,128]{2,1,0:T(8,128)S(1)}, u32[]{:S(2)}, u32[]{:S(2)}) %collective-permute-start.5) | collective-permute-done | bytes 884768 | tf_op jit(solution)/shard_map/ppermute | solution.py:469
  79.8 2.8 %collective-permute-start.11 = (f32[108,8,128]{2,1,0:T(8,128)S(1)}, f32[108,8,128]{2,1,0:T(8,128)S(1)}, u32[]{:S(2)}, u32[]{:S(2)}) collective-permute-start(f32[108,8,128]{2,1,0:T(8,128)S(1)} %get-tuple-element.47), channel_id=1, source_target_pairs={{0,2},{1,5},{2,0},{3,7},{4,6},{5,1},{6,4},{7,3},{8,10},{9,13},{10,... | collective-permute-start | bytes 1327112 | tf_op jit(solution)/shard_map/ppermute | solution.py:469
  82.6 8.6 %shard_map.98 = f32[512,256]{1,0:T(8,128)S(1)} custom-call(s32[2]{0:T(128)S(1)} %pad_add_fusion.7.swap_ref.refs_0_, f32[8,8,16,256]{3,2,1,0:T(8,128)S(1)} %bitcast.63, f32[8,8,16,1]{3,2,1,0:T(8,128)S(1)} %copy.19.filled_ref.refs_2_, f32[1,8,16,256]{3,2,1,0:T(8,128)S(1)} %collective-permute-done.6.refs_3_, ...), custom_call_target="tpu_custom_call" | custom-call | flops 5435817984 | bytes 8650752 | tf_op jit(solution)/shard_map/pallas_call | solution.py:297
  91.2 4.9 %collective-permute-done.11 = f32[108,8,128]{2,1,0:T(8,128)S(1)} collective-permute-done((f32[108,8,128]{2,1,0:T(8,128)S(1)}, f32[108,8,128]{2,1,0:T(8,128)S(1)}, u32[]{:S(2)}, u32[]{:S(2)}) %collective-permute-start.11) | collective-permute-done | bytes 442400 | tf_op jit(solution)/shard_map/ppermute | solution.py:469
  96.2 1.8 %collective-permute-start.13 = (f32[54,8,128]{2,1,0:T(8,128)S(1)}, f32[54,8,128]{2,1,0:T(8,128)S(1)}, u32[]{:S(2)}, u32[]{:S(2)}) collective-permute-start(f32[54,8,128]{2,1,0:T(8,128)S(1)} %get-tuple-element.57), channel_id=1, source_target_pairs={{0,8},{1,9},{2,10},{3,11},{4,12},{5,13},{6,14},{7,15},{8,0},{9,1},... | collective-permute-start | bytes 663560 | tf_op jit(solution)/shard_map/ppermute | solution.py:469
  98.1 2.0 %collective-permute-start.15 = (f32[108,8,128]{2,1,0:T(8,128)S(1)}, f32[108,8,128]{2,1,0:T(8,128)S(1)}, u32[]{:S(2)}, u32[]{:S(2)}) collective-permute-start(f32[108,8,128]{2,1,0:T(8,128)S(1)} %get-tuple-element.45), channel_id=1, source_target_pairs={{0,4},{1,17},{2,6},{3,19},{4,0},{5,21},{6,2},{7,23},{8,12},{9,25},... | collective-permute-start | bytes 1327112 | tf_op jit(solution)/shard_map/ppermute | solution.py:469
  100.1 8.6 %shard_map.99 = f32[512,256]{1,0:T(8,128)S(1)} custom-call(s32[2]{0:T(128)S(1)} %pad_add_fusion.7.swap_ref.refs_0_, f32[8,8,16,256]{3,2,1,0:T(8,128)S(1)} %bitcast.64, f32[8,8,16,1]{3,2,1,0:T(8,128)S(1)} %copy.19.filled_ref.refs_2_, f32[1,8,16,256]{3,2,1,0:T(8,128)S(1)} %collective-permute-done.6.refs_3_, ...), custom_call_target="tpu_custom_call" | custom-call | flops 5435817984 | bytes 8650752 | tf_op jit(solution)/shard_map/pallas_call | solution.py:297
  109.3 2.7 %collective-permute-start.14 = (f32[27,8,128]{2,1,0:T(8,128)S(1)}, f32[27,8,128]{2,1,0:T(8,128)S(1)}, u32[]{:S(2)}, u32[]{:S(2)}) collective-permute-start(f32[27,8,128]{2,1,0:T(8,128)S(1)} %slice_add_fusion.14), channel_id=1, source_target_pairs={{0,16},{1,17},{2,18},{3,19},{4,20},{5,21},{6,22},{7,23},{8,24},{9,... | collective-permute-start | bytes 331784 | tf_op jit(solution)/shard_map/ppermute | solution.py:469
  112.0 1.0 pad_maximum_fusion
  113.1 3.4 %collective-permute-done.16 = f32[54,8,128]{2,1,0:T(8,128)S(1)} collective-permute-done((f32[54,8,128]{2,1,0:T(8,128)S(1)}, f32[54,8,128]{2,1,0:T(8,128)S(1)}, u32[]{:S(2)}, u32[]{:S(2)}) %collective-permute-start.16) | collective-permute-done | bytes 221216 | tf_op jit(solution)/shard_map/ppermute | solution.py:469
  116.8 1.1 collective-permute-done.14
  118.1 4.6 %collective-permute-done.17 = f32[27,8,128]{2,1,0:T(8,128)S(1)} collective-permute-done((f32[27,8,128]{2,1,0:T(8,128)S(1)}, f32[27,8,128]{2,1,0:T(8,128)S(1)}, u32[]{:S(2)}, u32[]{:S(2)}) %collective-permute-start.17) | collective-permute-done | bytes 110624 | tf_op jit(solution)/shard_map/ppermute | solution.py:469
  (53 shorter events, 6.9 us)
Async XLA Ops:
  0.6 20.0 %copy-start = (f32[8,8,16,256]{3,2,1,0:T(8,128)S(1)}, f32[8,8,16,256]{3,2,1,0:T(8,128)}, u32[]{:S(2)}) copy-start(f32[8,8,16,256]{3,2,1,0:T(8,128)} %inputs_ref.1) | copy-start | bytes 3145732
  0.6 20.0 %copy-start.2 = (f32[8,8,16,256]{3,2,1,0:T(8,128)S(1)}, f32[8,8,16,256]{3,2,1,0:T(8,128)}, u32[]{:S(2)}) copy-start(f32[8,8,16,256]{3,2,1,0:T(8,128)} %param.9) | copy-start | bytes 3145732
  2.6 8.1 %collective-permute-start = (f32[1,8,16,256]{3,2,1,0:T(8,128)S(1)}, f32[1,8,16,256]{3,2,1,0:T(8,128)S(1)}, u32[]{:S(2)}, u32[]{:S(2)}) collective-permute-start(f32[1,8,16,256]{3,2,1,0:T(8,128)S(1)} %get-tuple-element.55), channel_id=1, source_target_pairs={{0,4},{4,8},{8,12},{12,16},{16,20},{20,24},{24,28},{1,5},{5,9},{9,... | collective-permute-start | bytes 393224 | tf_op jit(solution)/shard_map/ppermute | solution.py:332
  7.5 6.9 %collective-permute-start.1 = (f32[1,8,16,256]{3,2,1,0:T(8,128)S(1)}, f32[1,8,16,256]{3,2,1,0:T(8,128)S(1)}, u32[]{:S(2)}, u32[]{:S(2)}) collective-permute-start(f32[1,8,16,256]{3,2,1,0:T(8,128)S(1)} %get-tuple-element.54), channel_id=1, source_target_pairs={{4,0},{8,4},{12,8},{16,12},{20,16},{24,20},{28,24},{5,1},{9,5},{13... | collective-permute-start | bytes 393224 | tf_op jit(solution)/shard_map/ppermute | solution.py:332
  14.4 5.6 %collective-permute-start.3 = (f32[10,1,16,256]{3,2,1,0:T(8,128)S(1)}, f32[10,1,16,256]{3,2,1,0:T(8,128)S(1)}, u32[]{:S(2)}, u32[]{:S(2)}) collective-permute-start(f32[10,1,16,256]{3,2,1,0:T(8,128)S(1)} %maximum_bitcast_fusion.1), channel_id=1, source_target_pairs={{1,0},{2,1},{3,2},{5,4},{6,5},{7,6},{9,8},{10,9},{11,10},{13,12},{... | collective-permute-start | bytes 491528 | tf_op jit(solution)/shard_map/ppermute | solution.py:340
  16.4 4.2 %collective-permute-start.2 = (f32[10,1,16,256]{3,2,1,0:T(8,128)}, f32[10,1,16,256]{3,2,1,0:T(8,128)S(1)}, u32[]{:S(2)}, u32[]{:S(2)}) collective-permute-start(f32[10,1,16,256]{3,2,1,0:T(8,128)} %maximum_bitcast_fusion), channel_id=1, source_target_pairs={{0,1},{1,2},{2,3},{4,5},{5,6},{6,7},{8,9},{9,10},{10,11},{12,13},{... | collective-permute-start | bytes 491528 | tf_op jit(solution)/shard_map/ppermute | solution.py:340
  20.6 3.0 %copy-start.1 = (f32[6912,256]{1,0:T(8,128)S(1)}, f32[6912,256]{1,0:T(8,128)}, u32[]{:S(2)}) copy-start(f32[6912,256]{1,0:T(8,128)} %param.10) | copy-start | bytes 21233668
  45.8 8.4 %collective-permute-start.4 = (f32[432,8,128]{2,1,0:T(8,128)S(1)}, f32[432,8,128]{2,1,0:T(8,128)S(1)}, u32[]{:S(2)}, u32[]{:S(2)}) collective-permute-start(f32[432,8,128]{2,1,0:T(8,128)S(1)} %get-tuple-element.23), channel_id=1, source_target_pairs={{0,1},{1,0},{2,3},{3,2},{4,5},{5,4},{6,7},{7,6},{8,9},{9,8},{10,11... | collective-permute-start | bytes 5308424 | tf_op jit(solution)/shard_map/ppermute | solution.py:463
  48.4 7.3 %collective-permute-start.6 = (f32[1,8,16,256]{3,2,1,0:T(8,128)S(1)}, f32[1,8,16,256]{3,2,1,0:T(8,128)S(1)}, u32[]{:S(2)}, u32[]{:S(2)}) collective-permute-start(f32[1,8,16,256]{3,2,1,0:T(8,128)S(1)} %bitcast.72), channel_id=1, source_target_pairs={{0,4},{4,8},{8,12},{12,16},{16,20},{20,24},{24,28},{1,5},{5,9},{9,... | collective-permute-start | bytes 393224 | tf_op jit(solution)/shard_map/ppermute | solution.py:332
  52.8 7.0 %collective-permute-start.7 = (f32[1,8,16,256]{3,2,1,0:T(8,128)S(1)}, f32[1,8,16,256]{3,2,1,0:T(8,128)S(1)}, u32[]{:S(2)}, u32[]{:S(2)}) collective-permute-start(f32[1,8,16,256]{3,2,1,0:T(8,128)S(1)} %bitcast.71), channel_id=1, source_target_pairs={{4,0},{8,4},{12,8},{16,12},{20,16},{24,20},{28,24},{5,1},{9,5},{13... | collective-permute-start | bytes 393224 | tf_op jit(solution)/shard_map/ppermute | solution.py:332
  66.4 7.0 %collective-permute-start.8 = (f32[432,8,128]{2,1,0:T(8,128)S(1)}, f32[432,8,128]{2,1,0:T(8,128)S(1)}, u32[]{:S(2)}, u32[]{:S(2)}) collective-permute-start(f32[432,8,128]{2,1,0:T(8,128)S(1)} %get-tuple-element.29), channel_id=1, source_target_pairs={{0,1},{1,0},{2,3},{3,2},{4,5},{5,4},{6,7},{7,6},{8,9},{9,8},{10,11... | collective-permute-start | bytes 5308424 | tf_op jit(solution)/shard_map/ppermute | solution.py:463
  66.5 13.1 %collective-permute-start.5 = (f32[216,8,128]{2,1,0:T(8,128)S(1)}, f32[216,8,128]{2,1,0:T(8,128)S(1)}, u32[]{:S(2)}, u32[]{:S(2)}) collective-permute-start(f32[216,8,128]{2,1,0:T(8,128)S(1)} %get-tuple-element.43), channel_id=1, source_target_pairs={{0,4},{1,3},{2,6},{3,1},{4,0},{5,7},{6,2},{7,5},{8,12},{9,11},{10,... | collective-permute-start | bytes 2654216 | tf_op jit(solution)/shard_map/ppermute | solution.py:469
  68.7 13.9 %collective-permute-start.10 = (f32[10,1,16,256]{3,2,1,0:T(8,128)S(1)}, f32[10,1,16,256]{3,2,1,0:T(8,128)S(1)}, u32[]{:S(2)}, u32[]{:S(2)}) collective-permute-start(f32[10,1,16,256]{3,2,1,0:T(8,128)S(1)} %maximum_bitcast_fusion.3), channel_id=1, source_target_pairs={{1,0},{2,1},{3,2},{5,4},{6,5},{7,6},{9,8},{10,9},{11,10},{13,12},{... | collective-permute-start | bytes 491528 | tf_op jit(solution)/shard_map/ppermute | solution.py:340
  70.0 12.6 %collective-permute-start.9 = (f32[10,1,16,256]{3,2,1,0:T(8,128)S(1)}, f32[10,1,16,256]{3,2,1,0:T(8,128)S(1)}, u32[]{:S(2)}, u32[]{:S(2)}) collective-permute-start(f32[10,1,16,256]{3,2,1,0:T(8,128)S(1)} %maximum_bitcast_fusion.2), channel_id=1, source_target_pairs={{0,1},{1,2},{2,3},{4,5},{5,6},{6,7},{8,9},{9,10},{10,11},{12,13},{... | collective-permute-start | bytes 491528 | tf_op jit(solution)/shard_map/ppermute | solution.py:340
  73.7 24.3 %collective-permute-start.12 = (f32[216,8,128]{2,1,0:T(8,128)S(1)}, f32[216,8,128]{2,1,0:T(8,128)S(1)}, u32[]{:S(2)}, u32[]{:S(2)}) collective-permute-start(f32[216,8,128]{2,1,0:T(8,128)S(1)} %get-tuple-element.41), channel_id=1, source_target_pairs={{0,2},{1,9},{2,0},{3,11},{4,6},{5,13},{6,4},{7,15},{8,10},{9,1},{1... | collective-permute-start | bytes 2654216 | tf_op jit(solution)/shard_map/ppermute | solution.py:469
  79.8 16.4 %collective-permute-start.11 = (f32[108,8,128]{2,1,0:T(8,128)S(1)}, f32[108,8,128]{2,1,0:T(8,128)S(1)}, u32[]{:S(2)}, u32[]{:S(2)}) collective-permute-start(f32[108,8,128]{2,1,0:T(8,128)S(1)} %get-tuple-element.47), channel_id=1, source_target_pairs={{0,2},{1,5},{2,0},{3,7},{4,6},{5,1},{6,4},{7,3},{8,10},{9,13},{10,... | collective-permute-start | bytes 1327112 | tf_op jit(solution)/shard_map/ppermute | solution.py:469
  96.2 13.1 %collective-permute-start.13 = (f32[54,8,128]{2,1,0:T(8,128)S(1)}, f32[54,8,128]{2,1,0:T(8,128)S(1)}, u32[]{:S(2)}, u32[]{:S(2)}) collective-permute-start(f32[54,8,128]{2,1,0:T(8,128)S(1)} %get-tuple-element.57), channel_id=1, source_target_pairs={{0,8},{1,9},{2,10},{3,11},{4,12},{5,13},{6,14},{7,15},{8,0},{9,1},... | collective-permute-start | bytes 663560 | tf_op jit(solution)/shard_map/ppermute | solution.py:469
  98.1 10.6 %collective-permute-start.15 = (f32[108,8,128]{2,1,0:T(8,128)S(1)}, f32[108,8,128]{2,1,0:T(8,128)S(1)}, u32[]{:S(2)}, u32[]{:S(2)}) collective-permute-start(f32[108,8,128]{2,1,0:T(8,128)S(1)} %get-tuple-element.45), channel_id=1, source_target_pairs={{0,4},{1,17},{2,6},{3,19},{4,0},{5,21},{6,2},{7,23},{8,12},{9,25},... | collective-permute-start | bytes 1327112 | tf_op jit(solution)/shard_map/ppermute | solution.py:469
  108.8 7.6 %collective-permute-start.16 = (f32[54,8,128]{2,1,0:T(8,128)S(1)}, f32[54,8,128]{2,1,0:T(8,128)S(1)}, u32[]{:S(2)}, u32[]{:S(2)}) collective-permute-start(f32[54,8,128]{2,1,0:T(8,128)S(1)} %get-tuple-element.59), channel_id=1, source_target_pairs={{0,8},{1,5},{2,10},{3,7},{4,12},{5,1},{6,14},{7,3},{8,0},{9,13},{1... | collective-permute-start | bytes 663560 | tf_op jit(solution)/shard_map/ppermute | solution.py:469
  109.3 8.6 %collective-permute-start.14 = (f32[27,8,128]{2,1,0:T(8,128)S(1)}, f32[27,8,128]{2,1,0:T(8,128)S(1)}, u32[]{:S(2)}, u32[]{:S(2)}) collective-permute-start(f32[27,8,128]{2,1,0:T(8,128)S(1)} %slice_add_fusion.14), channel_id=1, source_target_pairs={{0,16},{1,17},{2,18},{3,19},{4,20},{5,21},{6,22},{7,23},{8,24},{9,... | collective-permute-start | bytes 331784 | tf_op jit(solution)/shard_map/ppermute | solution.py:469
  116.4 6.3 %collective-permute-start.17 = (f32[27,8,128]{2,1,0:T(8,128)S(1)}, f32[27,8,128]{2,1,0:T(8,128)S(1)}, u32[]{:S(2)}, u32[]{:S(2)}) collective-permute-start(f32[27,8,128]{2,1,0:T(8,128)S(1)} %slice_add_fusion.12), channel_id=1, source_target_pairs={{0,16},{1,3},{2,18},{3,1},{4,20},{5,7},{6,22},{7,5},{8,24},{9,11},... | collective-permute-start | bytes 331784 | tf_op jit(solution)/shard_map/ppermute | solution.py:469

commit v3 on v2

--- a/solution.py
+++ b/solution.py
@@ -95,25 +95,31 @@
             stack_ref[i] = stack_terms(slab)
         acc_ref[...] = jnp.zeros_like(acc_ref)
 
-    first, second = step // 3, step % 3
-    piece = stack_ref[pl.ds(first, span_x), pl.ds(second, span_y)].reshape(count, 2 * channels)
     for third in range(3):
-        acc_ref[third] += products(piece, *split(weight_ref[3 * step + third]), 0)
+        total = acc_ref[third]
+        for second in range(3):
+            piece = stack_ref[pl.ds(step, span_x), second : second + span_y]
+            total += products(
+                piece.reshape(count, 2 * channels),
+                *split(weight_ref[9 * step + 3 * second + third]),
+                0,
+            )
+        acc_ref[third] = total
 
     each = -(-(span_x + 2) // 3)
     groups = channels // 16
     for j in range(each):
-        i = jnp.minimum(first * each + j, span_x + 1)
-        turn = slab_ref[i, pl.ds(second, span_y)].reshape(side, channels).T
-        high, low = split(turn)
+        i = jnp.minimum(step * each + j, span_x + 1)
         lanes = pl.ds(pl.multiple_of(i * side, LANES), side)
-        for m in range(groups):
-            at = (m % 2) * 3 * (channels // 2) + 16 * (m // 2)
-            rows = pl.ds(pl.multiple_of(at + second * (channels // 2), 16), 16)
-            turned_ref[0, rows, lanes] = high[16 * m : 16 * m + 16]
-            turned_ref[1, rows, lanes] = low[16 * m : 16 * m + 16]
-
-    @pl.when(step == 8)
+        for second in range(3):
+            turn = slab_ref[i, second : second + span_y].reshape(side, channels).T
+            high, low = split(turn)
+            for m in range(groups):
+                at = ((m % 2) * 3 + second) * (channels // 2) + 16 * (m // 2)
+                turned_ref[0, at : at + 16, lanes] = high[16 * m : 16 * m + 16]
+                turned_ref[1, at : at + 16, lanes] = low[16 * m : 16 * m + 16]
+
+    @pl.when(step == 2)
     def _():
         preact = (
             acc_ref[1] + shift_rows(acc_ref[0], -1, depth) + shift_rows(acc_ref[2], 1, depth)
@@ -135,6 +141,27 @@
             right_ref[third, 1] = low
 
 
+def lines_kernel(inputs_ref, filled_ref, weight_ref, first_ref, last_ref):
+    first_ref[...] = inputs_ref[:, 0] * filled_ref[:, 0]
+    last = inputs_ref.shape[1] - 1
+    last_ref[...] = inputs_ref[:, last] * filled_ref[:, last]
+
+
+def edge_lines(inputs, filled, taps):
+    span_x, span_y, depth, channels = inputs.shape
+    line = jax.ShapeDtypeStruct((span_x, depth, channels), F32)
+    return pl.pallas_call(
+        lines_kernel,
+        in_specs=[WHOLE] * 3,
+        out_specs=[WHOLE] * 2,
+        out_shape=[line] * 2,
+        compiler_params=params(4),
+        cost_estimate=pl.CostEstimate(
+            flops=line.size, bytes_accessed=4 * line.size, transcendentals=0
+        ),
+    )(inputs, filled, taps)
+
+
 def forward(swap, inputs, filled, before_x, after_x, before_y, after_y, cot, taps):
     span_x, span_y, depth, channels = inputs.shape
     count = span_x * span_y * depth
@@ -142,7 +169,7 @@
     right = (3, 2, count, channels)
     return pl.pallas_call(
         forward_kernel,
-        grid=(9,),
+        grid=(3,),
         in_specs=[pl.BlockSpec(memory_space=pltpu.SMEM)]
         + [WHOLE] * 8,
         out_specs=[WHOLE] * 3,
@@ -158,8 +185,8 @@
         ],
         compiler_params=params(24),
         cost_estimate=pl.CostEstimate(
-            flops=2 * 81 * count * channels * channels,
-            bytes_accessed=4 * (8 * inputs.size + taps.size),
+            flops=count * channels,
+            bytes_accessed=inputs.size,
             transcendentals=count * channels,
         ),
     )(swap, inputs, filled, before_x, after_x, before_y, after_y, cot, taps)
@@ -213,8 +240,8 @@
         scratch_shapes=[pltpu.VMEM((3 * channels // 2, channels), F32)],
         compiler_params=params(12),
         cost_estimate=pl.CostEstimate(
-            flops=81 * count * channels * channels,
-            bytes_accessed=2 * (turned.size + right.size) + 8 * tiles * 8 * LANES,
+            flops=count * channels,
+            bytes_accessed=count * channels,
             transcendentals=0,
         ),
     )(place, turned, right)
@@ -273,14 +300,18 @@
             )
         acc_ref[...] = jnp.zeros_like(acc_ref)
 
-    first, second = step // 3, step % 3
-    piece = stack_ref[pl.ds(2 - first, width), pl.ds(2 - second, span_y)].reshape(
-        count, 2 * channels
-    )
     for third in range(3):
-        acc_ref[third] += products(piece, *split(weight_ref[3 * step + third]), 1)
-
-    @pl.when(step == 8)
+        total = acc_ref[third]
+        for second in range(3):
+            piece = stack_ref[pl.ds(2 - step, width), 2 - second : 2 - second + span_y]
+            total += products(
+                piece.reshape(count, 2 * channels),
+                *split(weight_ref[9 * step + 3 * second + third]),
+                1,
+            )
+        acc_ref[third] = total
+
+    @pl.when(step == 2)
     def _():
         total = acc_ref[1] + shift_rows(acc_ref[0], 1, depth) + shift_rows(acc_ref[2], -1, depth)
         out_ref[...] = total * filled_ref[begin:end].reshape(count, 1)
@@ -296,7 +327,7 @@
 
     return pl.pallas_call(
         kernel,
-        grid=(9,),
+        grid=(3,),
         in_specs=[pl.BlockSpec(memory_space=pltpu.SMEM)] + [WHOLE] * 7,
         out_specs=WHOLE,
         out_shape=jax.ShapeDtypeStruct((count, channels), F32),
@@ -306,8 +337,8 @@
         ],
         compiler_params=params(16),
         cost_estimate=pl.CostEstimate(
-            flops=2 * 81 * count * channels * channels,
-            bytes_accessed=4 * (3 * count * channels + taps.size),
+            flops=count * channels,
+            bytes_accessed=count * channels,
             transcendentals=0,
         ),
     )(turn, up, filled, before_x, after_x, before_y, after_y, taps)
@@ -389,7 +420,8 @@
     last_x, last_y = span_x - 1, span_y - 1
     face, other_face = masked(slice(0, 1), every), masked(slice(last_x, span_x), every)
     before_x, after_x = halo_x(face, other_face)
-    before_y, after_y = halo_y(masked(every, 0), masked(every, last_y), before_x, after_x)
+    taps = after(taps, face, other_face)
+    before_y, after_y = halo_y(*edge_lines(inputs, filled, taps), before_x, after_x)
     swap = jnp.stack([(me_y >> 1) & 1, me_y & 1]).astype(jnp.int32)
     upstream, turned, right = forward(
         swap,
@@ -406,15 +438,15 @@
 
     def data_halo_x(*others):
         first, last = up[:1], up[last_x:]
-        for other in others:
-            first, last, _ = lax.optimization_barrier((first, last, other))
-        return halo_x(first, last)
+        if others:
+            first, last, _ = lax.optimization_barrier((first, last, others))
+        return first, halo_x(first, last)
 
     def data_halo_y(sides, *others):
         first, last = up[:, 0], up[:, last_y]
-        for other in others:
-            first, last, _ = lax.optimization_barrier((first, last, other))
-        return halo_y(first, last, *sides)
+        if others:
+            first, last, _ = lax.optimization_barrier((first, last, others))
+        return first, halo_y(first, last, *sides)
 
     def data_piece(turn, sides, ends, begin, end):
         return data_grad(turn, up, filled, *sides, *ends, taps, begin, end)
@@ -427,8 +459,8 @@
             [before_y, jnp.concatenate([before_x, own, after_x], axis=0), after_y], axis=1
         )
         weight_grad = plain_filter_grad(bordered, upstream, span_x, span_y, depth)
-        sides = data_halo_x()
-        result = data_piece(swap, sides, data_halo_y(sides), 0, span_x)
+        sides = data_halo_x()[1]
+        result = data_piece(swap, sides, data_halo_y(sides)[1], 0, span_x)
         return (result.reshape(inputs.shape), weight_grad)
 
     units = 27 * groups // size_x // parts
@@ -469,21 +501,19 @@
         return keep, send, lax.ppermute(send, ("gx", "gy"), pairs)
 
     keep_a, send_a, got_a = terms(0, tables[0])
-    sides = data_halo_x(send_a)
-    keep_a, send_a, got_a = stage(0, 0, keep_a, got_a)
-    keep_b, send_b, got_b = terms(1, after(tables[1], send_a, *sides))
-    ends = data_halo_y(sides, send_b)
-    keep_b, send_b, got_b = stage(1, 0, keep_b, got_b)
-    keep_a, send_a, got_a = stage(0, 1, keep_a, got_a)
-    pieces = []
+    keep_b, send_b, got_b = terms(1, after(tables[1], send_a))
+    keep_a, send_a, got_a = stage(0, 0, after(keep_a, send_b), got_a)
+    face, sides = data_halo_x(send_a)
+    keep_b, send_b, got_b = stage(1, 0, after(keep_b, face), got_b)
+    keep_a, send_a, got_a = stage(0, 1, after(keep_a, send_b), got_a)
+    line, ends = data_halo_y(sides, send_a)
+    keep_b, send_b, got_b = stage(1, 1, after(keep_b, line), got_b)
+    pieces = [data_piece(after(swap, send_b), sides, ends, 0, middle)]
     for index in range(2, stages):
-        if index < 4:
-            begin, end = ((0, middle), (middle, span_x))[index - 2]
-            pieces.append(data_piece(after(swap, send_a, send_b), sides, ends, begin, end))
-            keep_a, keep_b = after(keep_a, pieces[-1]), after(keep_b, pieces[-1])
-        keep_a, send_a, got_a = stage(0, index, keep_a, got_a)
-        keep_b, send_b, got_b = stage(1, index - 1, keep_b, got_b)
-    keep_b, send_b, got_b = stage(1, stages - 1, keep_b, got_b)
+        keep_a, send_a, got_a = stage(0, index, after(keep_a, pieces[-1], send_b), got_a)
+        keep_b, send_b, got_b = stage(1, index, after(keep_b, send_a), got_b)
+        if index == 2:
+            pieces.append(data_piece(after(swap, send_b), sides, ends, middle, span_x))
     sums = [keep_a + got_a, keep_b + got_b]
     both = jnp.stack([s.reshape(units, 8, 2, 64) for s in sums], axis=1)
     weight_grad = both.transpose(0, 1, 3, 2, 4).reshape(units * 32, 64)

time: 124 us -> 114 us (0.919)
  waiting for transfers between devices: 27 us -> 20.6 us
  Pallas kernels: 46 us -> 41.6 us
  local copies, waits for them, and re-layouts: 4.8 us -> 7.82 us
  other arithmetic: 6.72 us -> 4.7 us
    ppermute x8, waiting for transfers between devices: 17.5 us -> 9.43 us  [stage(): return (keep, send, lax.ppermute(send, ('gx', 'gy'), pairs))]
    pallas_call x3 -> x4, Pallas kernels: 32.8 us -> 28.3 us  [the longest x2 14.1 us: data_grad(): pl.pallas_call(kernel, grid=(3,), in_specs=[pl.BlockSpec(memory_space=plt...]
    unnamed x7 -> x9, local copies, waits for them, and re-layouts: 3.92 us -> 6.95 us
    ppermute x4, starting transfers between devices: 12 us -> 9.36 us  [halo_x(): return (lax.ppermute(last, 'gx', up), lax.ppermute(first, 'gx', down))]
    ppermute x8, starting transfers between devices: 14.7 us -> 16.6 us  [stage(): return (keep, send, lax.ppermute(send, ('gx', 'gy'), pairs))]
  transfers between devices with their start and end apart: 18 -> 18, of which waited for: 9 -> 7; matrix products, arithmetic and copies ran while one was open for 4% -> 3% of each run, Pallas kernels for 14% -> 18%
where the time goes in v3:
time: 114 us
  Pallas kernels  41.6 us (36%)
  starting transfers between devices  38.2 us (34%)
  waiting for transfers between devices  20.6 us (18%)
  local copies, waits for them, and re-layouts  7.82 us (7%)
  other arithmetic  4.7 us (4%)
    ppermute x8, starting transfers between devices, stage(): return (keep, send, lax.ppermute(send, ('gx', 'gy'), pairs))  16.6 us
    pallas_call x2, Pallas kernels, data_grad(): pl.pallas_call(kernel, grid=(3,), in_specs=[pl.BlockSpec(memory_space=plt...  14.1 us
    pallas_call x1, Pallas kernels, forward(): pl.pallas_call(forward_kernel, grid=(3,), in_specs=[pl.BlockSpec(memory_s...  14.1 us
    pallas_call x2, Pallas kernels, filter_terms(): pl.pallas_call(kernel, in_specs=[pl.BlockSpec(memory_space=pltpu.SMEM), W...  13.2 us
    ppermute x8, waiting for transfers between devices, stage(): return (keep, send, lax.ppermute(send, ('gx', 'gy'), pairs))  9.43 us
    ppermute x4, starting transfers between devices, halo_x(): return (lax.ppermute(last, 'gx', up), lax.ppermute(first, 'gx', down))  9.36 us
    ppermute x4, waiting for transfers between devices, halo_x(): return (lax.ppermute(last, 'gx', up), lax.ppermute(first, 'gx', down))  9.29 us
    ppermute x2, starting transfers between devices, halo_y(): lax.ppermute(high[:, None], 'gy', up)  7.06 us
  transfers between devices with their start and end apart: 18, of which 7 were waited for; matrix products, arithmetic and copies ran while one was open for 3% of the time, Pallas kernels for 18%

profile of v3, /device:TPU:0, one launch (start us, length us, event | category | flops | bytes accessed | tf_op | source)
XLA Modules:
  0.0 113.8 jit_solution(17717432883170551111)
XLA Ops:
  1.5 1.1 slice_multiply_fusion
  2.6 4.8 %collective-permute-start = (f32[1,8,16,256]{3,2,1,0:T(8,128)S(1)}, f32[1,8,16,256]{3,2,1,0:T(8,128)S(1)}, u32[]{:S(2)}, u32[]{:S(2)}) collective-permute-start(f32[1,8,16,256]{3,2,1,0:T(8,128)S(1)} %get-tuple-element.67), channel_id=1, source_target_pairs={{0,4},{4,8},{8,12},{12,16},{16,20},{20,24},{24,28},{1,5},{5,9},{9,... | collective-permute-start | bytes 393224 | tf_op jit(solution)/shard_map/ppermute | solution.py:363
  7.4 1.3 %collective-permute-start.1 = (f32[1,8,16,256]{3,2,1,0:T(8,128)S(1)}, f32[1,8,16,256]{3,2,1,0:T(8,128)S(1)}, u32[]{:S(2)}, u32[]{:S(2)}) collective-permute-start(f32[1,8,16,256]{3,2,1,0:T(8,128)S(1)} %get-tuple-element.66), channel_id=1, source_target_pairs={{4,0},{8,4},{12,8},{16,12},{20,16},{24,20},{28,24},{5,1},{9,5},{13... | collective-permute-start | bytes 393224 | tf_op jit(solution)/shard_map/ppermute | solution.py:363
  10.0 3.0 %copy-done = f32[6912,256]{1,0:T(8,128)S(1)} copy-done((f32[6912,256]{1,0:T(8,128)S(1)}, f32[6912,256]{1,0:T(8,128)}, u32[]{:S(2)}) %copy-start) | copy-done | bytes 7077912
  13.2 1.1 collective-permute-done.1.after_x_ref
  14.3 1.3 %collective-permute-start.3 = (f32[10,1,16,256]{3,2,1,0:T(8,128)S(1)}, f32[10,1,16,256]{3,2,1,0:T(8,128)S(1)}, u32[]{:S(2)}, u32[]{:S(2)}) collective-permute-start(f32[10,1,16,256]{3,2,1,0:T(8,128)S(1)} %maximum_bitcast_fusion.1), channel_id=1, source_target_pairs={{1,0},{2,1},{3,2},{5,4},{6,5},{7,6},{9,8},{10,9},{11,10},{13,12},{... | collective-permute-start | bytes 491528 | tf_op jit(solution)/shard_map/ppermute | solution.py:371
  15.6 3.0 %collective-permute-start.2 = (f32[10,1,16,256]{3,2,1,0:T(8,128)S(1)}, f32[10,1,16,256]{3,2,1,0:T(8,128)S(1)}, u32[]{:S(2)}, u32[]{:S(2)}) collective-permute-start(f32[10,1,16,256]{3,2,1,0:T(8,128)S(1)} %maximum_bitcast_fusion), channel_id=1, source_target_pairs={{0,1},{1,2},{2,3},{4,5},{5,6},{6,7},{8,9},{9,10},{10,11},{12,13},{... | collective-permute-start | bytes 491528 | tf_op jit(solution)/shard_map/ppermute | solution.py:371
  18.8 0.9 collective-permute-done.2.before_y_ref
  19.7 3.0 %copy-done.1 = f32[6912,256]{1,0:T(8,128)S(1)} copy-done((f32[6912,256]{1,0:T(8,128)S(1)}, f32[6912,256]{1,0:T(8,128)}, u32[]{:S(2)}) %copy-start.1) | copy-done | bytes 7077912
  22.7 14.1 %shard_map.96 = (f32[1024,256]{1,0:T(8,128)S(1)}, bf16[2,768,1280]{2,1,0:T(8,128)(2,1)S(1)}, bf16[3,2,1024,256]{3,2,1,0:T(8,128)(2,1)S(1)}) custom-call(s32[2]{0:T(128)S(1)} %pad_add_fusion.7.swap_ref.refs_0_, f32[8,8,16,256]{3,2,1,0:T(8,128)S(1)} %copy-done.2, f32[8,8,16,1]{3,2,1,0:T(8,128)S(1)} %copy.16.filled_ref.refs_2_, ...), custom_call_target="tpu_custom_call" | custom-call | flops 262144 | bytes 262144 | tf_op jit(solution)/shard_map/pallas_call | solution.py:170
  36.8 6.6 %shard_map.97 = (f32[432,8,128]{2,1,0:T(8,128)S(1)}, f32[432,8,128]{2,1,0:T(8,128)S(1)}) custom-call(s32[2,217]{1,0:T(2,128)S(1)} %get-tuple-element.87.refs_0_, bf16[2,768,1280]{2,1,0:T(8,128)(2,1)S(1)} %get-tuple-element.30.refs_1_, bf16[3,2,1024,256]{3,2,1,0:T(8,128)(2,1)S(1)} %get-tuple-element.31.refs_2_), custom_call_target="tpu_custom_call" | custom-call | flops 262144 | bytes 262144 | tf_op jit(solution)/shard_map/pallas_call | solution.py:235
  43.5 2.4 %collective-permute-start.4 = (f32[432,8,128]{2,1,0:T(8,128)S(1)}, f32[432,8,128]{2,1,0:T(8,128)S(1)}, u32[]{:S(2)}, u32[]{:S(2)}) collective-permute-start(f32[432,8,128]{2,1,0:T(8,128)S(1)} %get-tuple-element.32), channel_id=1, source_target_pairs={{0,1},{1,0},{2,3},{3,2},{4,5},{5,4},{6,7},{7,6},{8,9},{9,8},{10,11... | collective-permute-start | bytes 5308424 | tf_op jit(solution)/shard_map/ppermute | solution.py:495
  45.9 6.6 %shard_map.98 = (f32[432,8,128]{2,1,0:T(8,128)S(1)}, f32[432,8,128]{2,1,0:T(8,128)S(1)}) custom-call(s32[2,217]{1,0:T(2,128)S(1)} %get-tuple-element.33.refs_0_, bf16[2,768,1280]{2,1,0:T(8,128)(2,1)S(1)} %get-tuple-element.30.refs_1_, bf16[3,2,1024,256]{3,2,1,0:T(8,128)(2,1)S(1)} %get-tuple-element.31.refs_2_), custom_call_target="tpu_custom_call" | custom-call | flops 262144 | bytes 262144 | tf_op jit(solution)/shard_map/pallas_call | solution.py:235
  52.8 2.5 %collective-permute-start.6 = (f32[216,8,128]{2,1,0:T(8,128)S(1)}, f32[216,8,128]{2,1,0:T(8,128)S(1)}, u32[]{:S(2)}, u32[]{:S(2)}) collective-permute-start(f32[216,8,128]{2,1,0:T(8,128)S(1)} %get-tuple-element.55), channel_id=1, source_target_pairs={{0,4},{1,3},{2,6},{3,1},{4,0},{5,7},{6,2},{7,5},{8,12},{9,11},{10,... | collective-permute-start | bytes 2654216 | tf_op jit(solution)/shard_map/ppermute | solution.py:501
  55.4 1.9 %collective-permute-start.8 = (f32[1,8,16,256]{3,2,1,0:T(8,128)S(1)}, f32[1,8,16,256]{3,2,1,0:T(8,128)S(1)}, u32[]{:S(2)}, u32[]{:S(2)}) collective-permute-start(f32[1,8,16,256]{3,2,1,0:T(8,128)S(1)} %bitcast.63), channel_id=1, source_target_pairs={{0,4},{4,8},{8,12},{12,16},{16,20},{20,24},{24,28},{1,5},{5,9},{9,... | collective-permute-start | bytes 393224 | tf_op jit(solution)/shard_map/ppermute | solution.py:363
  57.5 2.9 %collective-permute-start.7 = (f32[216,8,128]{2,1,0:T(8,128)S(1)}, f32[216,8,128]{2,1,0:T(8,128)S(1)}, u32[]{:S(2)}, u32[]{:S(2)}) collective-permute-start(f32[216,8,128]{2,1,0:T(8,128)S(1)} %get-tuple-element.57), channel_id=1, source_target_pairs={{0,2},{1,9},{2,0},{3,11},{4,6},{5,13},{6,4},{7,15},{8,10},{9,1},{1... | collective-permute-start | bytes 2654216 | tf_op jit(solution)/shard_map/ppermute | solution.py:501
  60.4 1.3 %collective-permute-start.9 = (f32[1,8,16,256]{3,2,1,0:T(8,128)S(1)}, f32[1,8,16,256]{3,2,1,0:T(8,128)S(1)}, u32[]{:S(2)}, u32[]{:S(2)}) collective-permute-start(f32[1,8,16,256]{3,2,1,0:T(8,128)S(1)} %bitcast.62), channel_id=1, source_target_pairs={{4,0},{8,4},{12,8},{16,12},{20,16},{24,20},{28,24},{5,1},{9,5},{13... | collective-permute-start | bytes 393224 | tf_op jit(solution)/shard_map/ppermute | solution.py:363
  61.7 8.2 %collective-permute-done.8.refs_3_ = f32[1,8,16,256]{3,2,1,0:T(8,128)S(1)} collective-permute-done((f32[1,8,16,256]{3,2,1,0:T(8,128)S(1)}, f32[1,8,16,256]{3,2,1,0:T(8,128)S(1)}, u32[]{:S(2)}, u32[]{:S(2)}) %collective-permute-start.8) | collective-permute-done | bytes 131104 | tf_op jit(solution)/shard_map/ppermute | solution.py:363
  70.0 3.2 %collective-permute-start.12 = (f32[108,8,128]{2,1,0:T(8,128)S(1)}, f32[108,8,128]{2,1,0:T(8,128)S(1)}, u32[]{:S(2)}, u32[]{:S(2)}) collective-permute-start(f32[108,8,128]{2,1,0:T(8,128)S(1)} %get-tuple-element.59), channel_id=1, source_target_pairs={{0,2},{1,5},{2,0},{3,7},{4,6},{5,1},{6,4},{7,3},{8,10},{9,13},{10,... | collective-permute-start | bytes 1327112 | tf_op jit(solution)/shard_map/ppermute | solution.py:501
  73.3 1.3 %collective-permute-start.11 = (f32[10,1,16,256]{3,2,1,0:T(8,128)S(1)}, f32[10,1,16,256]{3,2,1,0:T(8,128)S(1)}, u32[]{:S(2)}, u32[]{:S(2)}) collective-permute-start(f32[10,1,16,256]{3,2,1,0:T(8,128)S(1)} %maximum_bitcast_fusion.3), channel_id=1, source_target_pairs={{1,0},{2,1},{3,2},{5,4},{6,5},{7,6},{9,8},{10,9},{11,10},{13,12},{... | collective-permute-start | bytes 491528 | tf_op jit(solution)/shard_map/ppermute | solution.py:371
  74.6 1.0 collective-permute-done.7
  75.7 2.8 %collective-permute-start.13 = (f32[108,8,128]{2,1,0:T(8,128)S(1)}, f32[108,8,128]{2,1,0:T(8,128)S(1)}, u32[]{:S(2)}, u32[]{:S(2)}) collective-permute-start(f32[108,8,128]{2,1,0:T(8,128)S(1)} %get-tuple-element.61), channel_id=1, source_target_pairs={{0,4},{1,17},{2,6},{3,19},{4,0},{5,21},{6,2},{7,23},{8,12},{9,25},... | collective-permute-start | bytes 1327112 | tf_op jit(solution)/shard_map/ppermute | solution.py:501
  78.6 4.0 %collective-permute-start.10 = (f32[10,1,16,256]{3,2,1,0:T(8,128)S(1)}, f32[10,1,16,256]{3,2,1,0:T(8,128)S(1)}, u32[]{:S(2)}, u32[]{:S(2)}) collective-permute-start(f32[10,1,16,256]{3,2,1,0:T(8,128)S(1)} %maximum_bitcast_fusion.2), channel_id=1, source_target_pairs={{0,1},{1,2},{2,3},{4,5},{5,6},{6,7},{8,9},{9,10},{10,11},{12,13},{... | collective-permute-start | bytes 491528 | tf_op jit(solution)/shard_map/ppermute | solution.py:371
  82.6 1.0 collective-permute-done.10.refs_5_
  83.6 7.1 %shard_map.99 = f32[512,256]{1,0:T(8,128)S(1)} custom-call(s32[2]{0:T(128)S(1)} %pad_add_fusion.7.swap_ref.refs_0_, f32[8,8,16,256]{3,2,1,0:T(8,128)S(1)} %bitcast.57, f32[8,8,16,1]{3,2,1,0:T(8,128)S(1)} %copy.16.filled_ref.refs_2_, f32[1,8,16,256]{3,2,1,0:T(8,128)S(1)} %collective-permute-done.8.refs_3_, ...), custom_call_target="tpu_custom_call" | custom-call | flops 131072 | bytes 131072 | tf_op jit(solution)/shard_map/pallas_call | solution.py:328
  90.7 1.6 %collective-permute-start.14 = (f32[54,8,128]{2,1,0:T(8,128)S(1)}, f32[54,8,128]{2,1,0:T(8,128)S(1)}, u32[]{:S(2)}, u32[]{:S(2)}) collective-permute-start(f32[54,8,128]{2,1,0:T(8,128)S(1)} %get-tuple-element.69), channel_id=1, source_target_pairs={{0,8},{1,9},{2,10},{3,11},{4,12},{5,13},{6,14},{7,15},{8,0},{9,1},... | collective-permute-start | bytes 663560 | tf_op jit(solution)/shard_map/ppermute | solution.py:501
  92.9 7.1 %shard_map.100 = f32[512,256]{1,0:T(8,128)S(1)} custom-call(s32[2]{0:T(128)S(1)} %pad_add_fusion.7.swap_ref.refs_0_, f32[8,8,16,256]{3,2,1,0:T(8,128)S(1)} %bitcast.58, f32[8,8,16,1]{3,2,1,0:T(8,128)S(1)} %copy.16.filled_ref.refs_2_, f32[1,8,16,256]{3,2,1,0:T(8,128)S(1)} %collective-permute-done.8.refs_3_, ...), custom_call_target="tpu_custom_call" | custom-call | flops 131072 | bytes 131072 | tf_op jit(solution)/shard_map/pallas_call | solution.py:328
  100.0 1.0 pad_maximum_fusion
  101.5 2.7 %collective-permute-start.17 = (f32[27,8,128]{2,1,0:T(8,128)S(1)}, f32[27,8,128]{2,1,0:T(8,128)S(1)}, u32[]{:S(2)}, u32[]{:S(2)}) collective-permute-start(f32[27,8,128]{2,1,0:T(8,128)S(1)} %slice_add_fusion.12), channel_id=1, source_target_pairs={{0,16},{1,3},{2,18},{3,1},{4,20},{5,7},{6,22},{7,5},{8,24},{9,11},... | collective-permute-start | bytes 331784 | tf_op jit(solution)/shard_map/ppermute | solution.py:501
  104.1 7.3 %collective-permute-done.15 = f32[27,8,128]{2,1,0:T(8,128)S(1)} collective-permute-done((f32[27,8,128]{2,1,0:T(8,128)S(1)}, f32[27,8,128]{2,1,0:T(8,128)S(1)}, u32[]{:S(2)}, u32[]{:S(2)}) %collective-permute-start.15) | collective-permute-done | bytes 110624 | tf_op jit(solution)/shard_map/ppermute | solution.py:501
  111.7 1.0 collective-permute-done.17
  113.0 0.9 copy.23
  (54 shorter events, 4.6 us)
Async XLA Ops:
  0.6 9.3 %copy-start.2 = (f32[8,8,16,256]{3,2,1,0:T(8,128)S(1)}, f32[8,8,16,256]{3,2,1,0:T(8,128)}, u32[]{:S(2)}) copy-start(f32[8,8,16,256]{3,2,1,0:T(8,128)} %inputs_ref.3) | copy-start | bytes 3145732
  2.6 10.6 %collective-permute-start = (f32[1,8,16,256]{3,2,1,0:T(8,128)S(1)}, f32[1,8,16,256]{3,2,1,0:T(8,128)S(1)}, u32[]{:S(2)}, u32[]{:S(2)}) collective-permute-start(f32[1,8,16,256]{3,2,1,0:T(8,128)S(1)} %get-tuple-element.67), channel_id=1, source_target_pairs={{0,4},{4,8},{8,12},{12,16},{16,20},{20,24},{24,28},{1,5},{5,9},{9,... | collective-permute-start | bytes 393224 | tf_op jit(solution)/shard_map/ppermute | solution.py:363
  7.4 6.9 %collective-permute-start.1 = (f32[1,8,16,256]{3,2,1,0:T(8,128)S(1)}, f32[1,8,16,256]{3,2,1,0:T(8,128)S(1)}, u32[]{:S(2)}, u32[]{:S(2)}) collective-permute-start(f32[1,8,16,256]{3,2,1,0:T(8,128)S(1)} %get-tuple-element.66), channel_id=1, source_target_pairs={{4,0},{8,4},{12,8},{16,12},{20,16},{24,20},{28,24},{5,1},{9,5},{13... | collective-permute-start | bytes 393224 | tf_op jit(solution)/shard_map/ppermute | solution.py:363
  10.0 3.0 %copy-start = (f32[6912,256]{1,0:T(8,128)S(1)}, f32[6912,256]{1,0:T(8,128)}, u32[]{:S(2)}) copy-start(f32[6912,256]{1,0:T(8,128)} %param.10) | copy-start | bytes 21233668
  13.0 6.7 %copy-start.3 = (f32[8,8,16,256]{3,2,1,0:T(8,128)S(1)}, f32[8,8,16,256]{3,2,1,0:T(8,128)}, u32[]{:S(2)}) copy-start(f32[8,8,16,256]{3,2,1,0:T(8,128)} %param.9) | copy-start | bytes 3145732
  14.3 4.5 %collective-permute-start.3 = (f32[10,1,16,256]{3,2,1,0:T(8,128)S(1)}, f32[10,1,16,256]{3,2,1,0:T(8,128)S(1)}, u32[]{:S(2)}, u32[]{:S(2)}) collective-permute-start(f32[10,1,16,256]{3,2,1,0:T(8,128)S(1)} %maximum_bitcast_fusion.1), channel_id=1, source_target_pairs={{1,0},{2,1},{3,2},{5,4},{6,5},{7,6},{9,8},{10,9},{11,10},{13,12},{... | collective-permute-start | bytes 491528 | tf_op jit(solution)/shard_map/ppermute | solution.py:371
  15.6 4.0 %collective-permute-start.2 = (f32[10,1,16,256]{3,2,1,0:T(8,128)S(1)}, f32[10,1,16,256]{3,2,1,0:T(8,128)S(1)}, u32[]{:S(2)}, u32[]{:S(2)}) collective-permute-start(f32[10,1,16,256]{3,2,1,0:T(8,128)S(1)} %maximum_bitcast_fusion), channel_id=1, source_target_pairs={{0,1},{1,2},{2,3},{4,5},{5,6},{6,7},{8,9},{9,10},{10,11},{12,13},{... | collective-permute-start | bytes 491528 | tf_op jit(solution)/shard_map/ppermute | solution.py:371
  19.7 3.0 %copy-start.1 = (f32[6912,256]{1,0:T(8,128)S(1)}, f32[6912,256]{1,0:T(8,128)}, u32[]{:S(2)}) copy-start(f32[6912,256]{1,0:T(8,128)} %param.10) | copy-start | bytes 21233668
  43.5 9.2 %collective-permute-start.4 = (f32[432,8,128]{2,1,0:T(8,128)S(1)}, f32[432,8,128]{2,1,0:T(8,128)S(1)}, u32[]{:S(2)}, u32[]{:S(2)}) collective-permute-start(f32[432,8,128]{2,1,0:T(8,128)S(1)} %get-tuple-element.32), channel_id=1, source_target_pairs={{0,1},{1,0},{2,3},{3,2},{4,5},{5,4},{6,7},{7,6},{8,9},{9,8},{10,11... | collective-permute-start | bytes 5308424 | tf_op jit(solution)/shard_map/ppermute | solution.py:495
  52.5 4.7 %collective-permute-start.5 = (f32[432,8,128]{2,1,0:T(8,128)S(1)}, f32[432,8,128]{2,1,0:T(8,128)S(1)}, u32[]{:S(2)}, u32[]{:S(2)}) collective-permute-start(f32[432,8,128]{2,1,0:T(8,128)S(1)} %get-tuple-element.37), channel_id=1, source_target_pairs={{0,1},{1,0},{2,3},{3,2},{4,5},{5,4},{6,7},{7,6},{8,9},{9,8},{10,11... | collective-permute-start | bytes 5308424 | tf_op jit(solution)/shard_map/ppermute | solution.py:495
  52.8 17.1 %collective-permute-start.6 = (f32[216,8,128]{2,1,0:T(8,128)S(1)}, f32[216,8,128]{2,1,0:T(8,128)S(1)}, u32[]{:S(2)}, u32[]{:S(2)}) collective-permute-start(f32[216,8,128]{2,1,0:T(8,128)S(1)} %get-tuple-element.55), channel_id=1, source_target_pairs={{0,4},{1,3},{2,6},{3,1},{4,0},{5,7},{6,2},{7,5},{8,12},{9,11},{10,... | collective-permute-start | bytes 2654216 | tf_op jit(solution)/shard_map/ppermute | solution.py:501
  55.4 14.6 %collective-permute-start.8 = (f32[1,8,16,256]{3,2,1,0:T(8,128)S(1)}, f32[1,8,16,256]{3,2,1,0:T(8,128)S(1)}, u32[]{:S(2)}, u32[]{:S(2)}) collective-permute-start(f32[1,8,16,256]{3,2,1,0:T(8,128)S(1)} %bitcast.63), channel_id=1, source_target_pairs={{0,4},{4,8},{8,12},{12,16},{16,20},{20,24},{24,28},{1,5},{5,9},{9,... | collective-permute-start | bytes 393224 | tf_op jit(solution)/shard_map/ppermute | solution.py:363
  57.5 18.1 %collective-permute-start.7 = (f32[216,8,128]{2,1,0:T(8,128)S(1)}, f32[216,8,128]{2,1,0:T(8,128)S(1)}, u32[]{:S(2)}, u32[]{:S(2)}) collective-permute-start(f32[216,8,128]{2,1,0:T(8,128)S(1)} %get-tuple-element.57), channel_id=1, source_target_pairs={{0,2},{1,9},{2,0},{3,11},{4,6},{5,13},{6,4},{7,15},{8,10},{9,1},{1... | collective-permute-start | bytes 2654216 | tf_op jit(solution)/shard_map/ppermute | solution.py:501
  60.4 9.5 %collective-permute-start.9 = (f32[1,8,16,256]{3,2,1,0:T(8,128)S(1)}, f32[1,8,16,256]{3,2,1,0:T(8,128)S(1)}, u32[]{:S(2)}, u32[]{:S(2)}) collective-permute-start(f32[1,8,16,256]{3,2,1,0:T(8,128)S(1)} %bitcast.62), channel_id=1, source_target_pairs={{4,0},{8,4},{12,8},{16,12},{20,16},{24,20},{28,24},{5,1},{9,5},{13... | collective-permute-start | bytes 393224 | tf_op jit(solution)/shard_map/ppermute | solution.py:363
  70.0 20.6 %collective-permute-start.12 = (f32[108,8,128]{2,1,0:T(8,128)S(1)}, f32[108,8,128]{2,1,0:T(8,128)S(1)}, u32[]{:S(2)}, u32[]{:S(2)}) collective-permute-start(f32[108,8,128]{2,1,0:T(8,128)S(1)} %get-tuple-element.59), channel_id=1, source_target_pairs={{0,2},{1,5},{2,0},{3,7},{4,6},{5,1},{6,4},{7,3},{8,10},{9,13},{10,... | collective-permute-start | bytes 1327112 | tf_op jit(solution)/shard_map/ppermute | solution.py:501
  73.3 9.3 %collective-permute-start.11 = (f32[10,1,16,256]{3,2,1,0:T(8,128)S(1)}, f32[10,1,16,256]{3,2,1,0:T(8,128)S(1)}, u32[]{:S(2)}, u32[]{:S(2)}) collective-permute-start(f32[10,1,16,256]{3,2,1,0:T(8,128)S(1)} %maximum_bitcast_fusion.3), channel_id=1, source_target_pairs={{1,0},{2,1},{3,2},{5,4},{6,5},{7,6},{9,8},{10,9},{11,10},{13,12},{... | collective-permute-start | bytes 491528 | tf_op jit(solution)/shard_map/ppermute | solution.py:371
  75.7 16.7 %collective-permute-start.13 = (f32[108,8,128]{2,1,0:T(8,128)S(1)}, f32[108,8,128]{2,1,0:T(8,128)S(1)}, u32[]{:S(2)}, u32[]{:S(2)}) collective-permute-start(f32[108,8,128]{2,1,0:T(8,128)S(1)} %get-tuple-element.61), channel_id=1, source_target_pairs={{0,4},{1,17},{2,6},{3,19},{4,0},{5,21},{6,2},{7,23},{8,12},{9,25},... | collective-permute-start | bytes 1327112 | tf_op jit(solution)/shard_map/ppermute | solution.py:501
  78.6 5.0 %collective-permute-start.10 = (f32[10,1,16,256]{3,2,1,0:T(8,128)S(1)}, f32[10,1,16,256]{3,2,1,0:T(8,128)S(1)}, u32[]{:S(2)}, u32[]{:S(2)}) collective-permute-start(f32[10,1,16,256]{3,2,1,0:T(8,128)S(1)} %maximum_bitcast_fusion.2), channel_id=1, source_target_pairs={{0,1},{1,2},{2,3},{4,5},{5,6},{6,7},{8,9},{9,10},{10,11},{12,13},{... | collective-permute-start | bytes 491528 | tf_op jit(solution)/shard_map/ppermute | solution.py:371
  90.7 10.3 %collective-permute-start.14 = (f32[54,8,128]{2,1,0:T(8,128)S(1)}, f32[54,8,128]{2,1,0:T(8,128)S(1)}, u32[]{:S(2)}, u32[]{:S(2)}) collective-permute-start(f32[54,8,128]{2,1,0:T(8,128)S(1)} %get-tuple-element.69), channel_id=1, source_target_pairs={{0,8},{1,9},{2,10},{3,11},{4,12},{5,13},{6,14},{7,15},{8,0},{9,1},... | collective-permute-start | bytes 663560 | tf_op jit(solution)/shard_map/ppermute | solution.py:501
  92.4 9.0 %collective-permute-start.16 = (f32[54,8,128]{2,1,0:T(8,128)S(1)}, f32[54,8,128]{2,1,0:T(8,128)S(1)}, u32[]{:S(2)}, u32[]{:S(2)}) collective-permute-start(f32[54,8,128]{2,1,0:T(8,128)S(1)} %get-tuple-element.71), channel_id=1, source_target_pairs={{0,8},{1,5},{2,10},{3,7},{4,12},{5,1},{6,14},{7,3},{8,0},{9,13},{1... | collective-permute-start | bytes 663560 | tf_op jit(solution)/shard_map/ppermute | solution.py:501
  101.1 10.4 %collective-permute-start.15 = (f32[27,8,128]{2,1,0:T(8,128)S(1)}, f32[27,8,128]{2,1,0:T(8,128)S(1)}, u32[]{:S(2)}, u32[]{:S(2)}) collective-permute-start(f32[27,8,128]{2,1,0:T(8,128)S(1)} %slice_add_fusion.14), channel_id=1, source_target_pairs={{0,16},{1,17},{2,18},{3,19},{4,20},{5,21},{6,22},{7,23},{8,24},{9,... | collective-permute-start | bytes 331784 | tf_op jit(solution)/shard_map/ppermute | solution.py:501
  101.5 11.2 %collective-permute-start.17 = (f32[27,8,128]{2,1,0:T(8,128)S(1)}, f32[27,8,128]{2,1,0:T(8,128)S(1)}, u32[]{:S(2)}, u32[]{:S(2)}) collective-permute-start(f32[27,8,128]{2,1,0:T(8,128)S(1)} %slice_add_fusion.12), channel_id=1, source_target_pairs={{0,16},{1,3},{2,18},{3,1},{4,20},{5,7},{6,22},{7,5},{8,24},{9,11},... | collective-permute-start | bytes 331784 | tf_op jit(solution)/shard_map/ppermute | solution.py:501

commit v4 on v3

--- a/solution.py
+++ b/solution.py
@@ -451,9 +451,11 @@
     def data_piece(turn, sides, ends, begin, end):
         return data_grad(turn, up, filled, *sides, *ends, taps, begin, end)
 
-    middle = span_x // 2
+    third = -(-span_x // 3)
+    cuts = (third, 2 * third, span_x)
     parts, groups = 2, channels // 16
-    if channels // size_y != 64 or 27 * groups % (parts * size_x) or channels != 256:
+    tiled = channels == 256 and size_y == 4 and 27 * groups % (parts * size_x) == 0
+    if not tiled or size_x < 8 or size_x & (size_x - 1):
         own = inputs * filled
         bordered = jnp.concatenate(
             [before_y, jnp.concatenate([before_x, own, after_x], axis=0), after_y], axis=1
@@ -508,13 +510,14 @@
     keep_a, send_a, got_a = stage(0, 1, after(keep_a, send_b), got_a)
     line, ends = data_halo_y(sides, send_a)
     keep_b, send_b, got_b = stage(1, 1, after(keep_b, line), got_b)
-    pieces = [data_piece(after(swap, send_b), sides, ends, 0, middle)]
+    pieces = [data_piece(after(swap, send_b), sides, ends, 0, cuts[0])]
     for index in range(2, stages):
         keep_a, send_a, got_a = stage(0, index, after(keep_a, pieces[-1], send_b), got_a)
         keep_b, send_b, got_b = stage(1, index, after(keep_b, send_a), got_b)
-        if index == 2:
-            pieces.append(data_piece(after(swap, send_b), sides, ends, middle, span_x))
-    sums = [keep_a + got_a, keep_b + got_b]
+        if index < 4:
+            begin, end = cuts[index - 2 : index]
+            pieces.append(data_piece(after(swap, send_b), sides, ends, begin, end))
+    sums = [after(keep_a, pieces[-1]) + got_a, after(keep_b, pieces[-1]) + got_b]
     both = jnp.stack([s.reshape(units, 8, 2, 64) for s in sums], axis=1)
     weight_grad = both.transpose(0, 1, 3, 2, 4).reshape(units * 32, 64)
     return (jnp.concatenate(pieces, axis=0).reshape(inputs.shape), weight_grad)

time: 114 us -> 110 us (0.965)
  waiting for transfers between devices: 20.6 us -> 17.9 us
  starting transfers between devices: 38.2 us -> 35.7 us
  Pallas kernels: 41.6 us -> 42.8 us
    ppermute x8, waiting for transfers between devices: 9.43 us -> 6.69 us  [stage(): return (keep, send, lax.ppermute(send, ('gx', 'gy'), pairs))]
    ppermute x8, starting transfers between devices: 16.6 us -> 14.2 us  [stage(): return (keep, send, lax.ppermute(send, ('gx', 'gy'), pairs))]
    pallas_call x2 -> x3, Pallas kernels: 14.1 us -> 15.4 us  [data_grad(): pl.pallas_call(kernel, grid=(3,), in_specs=[pl.BlockSpec(memory_space=plt...]
  transfers between devices with their start and end apart: 18 -> 18, of which waited for: 7 -> 9; matrix products, arithmetic and copies ran while one was open for 3% -> 3% of each run, Pallas kernels for 18% -> 20%
where the time goes in v4:
time: 110 us
  Pallas kernels  42.8 us (39%)
  starting transfers between devices  35.7 us (32%)
  waiting for transfers between devices  17.9 us (16%)
  local copies, waits for them, and re-layouts  7.82 us (7%)
  other arithmetic  4.75 us (4%)
    pallas_call x3, Pallas kernels, data_grad(): pl.pallas_call(kernel, grid=(3,), in_specs=[pl.BlockSpec(memory_space=plt...  15.4 us
    ppermute x8, starting transfers between devices, stage(): return (keep, send, lax.ppermute(send, ('gx', 'gy'), pairs))  14.2 us
    pallas_call x1, Pallas kernels, forward(): pl.pallas_call(forward_kernel, grid=(3,), in_specs=[pl.BlockSpec(memory_s...  14.1 us
    pallas_call x2, Pallas kernels, filter_terms(): pl.pallas_call(kernel, in_specs=[pl.BlockSpec(memory_space=pltpu.SMEM), W...  13.2 us
    ppermute x4, starting transfers between devices, halo_x(): return (lax.ppermute(last, 'gx', up), lax.ppermute(first, 'gx', down))  9.36 us
    ppermute x4, waiting for transfers between devices, halo_x(): return (lax.ppermute(last, 'gx', up), lax.ppermute(first, 'gx', down))  9.29 us
    ppermute x2, starting transfers between devices, halo_y(): lax.ppermute(high[:, None], 'gy', up)  7.06 us
    unnamed x9, local copies, waits for them, and re-layouts  6.95 us
  transfers between devices with their start and end apart: 18, of which 9 were waited for; matrix products, arithmetic and copies ran while one was open for 3% of the time, Pallas kernels for 20%

profile of v4, /device:TPU:0, one launch (start us, length us, event | category | flops | bytes accessed | tf_op | source)
XLA Modules:
  0.0 109.9 jit_solution(16110790415133416545)
XLA Ops:
  1.5 1.1 slice_multiply_fusion
  2.6 4.8 %collective-permute-start = (f32[1,8,16,256]{3,2,1,0:T(8,128)S(1)}, f32[1,8,16,256]{3,2,1,0:T(8,128)S(1)}, u32[]{:S(2)}, u32[]{:S(2)}) collective-permute-start(f32[1,8,16,256]{3,2,1,0:T(8,128)S(1)} %get-tuple-element.73), channel_id=1, source_target_pairs={{0,4},{4,8},{8,12},{12,16},{16,20},{20,24},{24,28},{1,5},{5,9},{9,... | collective-permute-start | bytes 393224 | tf_op jit(solution)/shard_map/ppermute | solution.py:363
  7.4 1.3 %collective-permute-start.1 = (f32[1,8,16,256]{3,2,1,0:T(8,128)S(1)}, f32[1,8,16,256]{3,2,1,0:T(8,128)S(1)}, u32[]{:S(2)}, u32[]{:S(2)}) collective-permute-start(f32[1,8,16,256]{3,2,1,0:T(8,128)S(1)} %get-tuple-element.72), channel_id=1, source_target_pairs={{4,0},{8,4},{12,8},{16,12},{20,16},{24,20},{28,24},{5,1},{9,5},{13... | collective-permute-start | bytes 393224 | tf_op jit(solution)/shard_map/ppermute | solution.py:363
  10.0 3.0 %copy-done = f32[6912,256]{1,0:T(8,128)S(1)} copy-done((f32[6912,256]{1,0:T(8,128)S(1)}, f32[6912,256]{1,0:T(8,128)}, u32[]{:S(2)}) %copy-start) | copy-done | bytes 7077912
  13.2 1.1 collective-permute-done.1.after_x_ref
  14.3 1.3 %collective-permute-start.3 = (f32[10,1,16,256]{3,2,1,0:T(8,128)S(1)}, f32[10,1,16,256]{3,2,1,0:T(8,128)S(1)}, u32[]{:S(2)}, u32[]{:S(2)}) collective-permute-start(f32[10,1,16,256]{3,2,1,0:T(8,128)S(1)} %maximum_bitcast_fusion.1), channel_id=1, source_target_pairs={{1,0},{2,1},{3,2},{5,4},{6,5},{7,6},{9,8},{10,9},{11,10},{13,12},{... | collective-permute-start | bytes 491528 | tf_op jit(solution)/shard_map/ppermute | solution.py:371
  15.6 3.0 %collective-permute-start.2 = (f32[10,1,16,256]{3,2,1,0:T(8,128)S(1)}, f32[10,1,16,256]{3,2,1,0:T(8,128)S(1)}, u32[]{:S(2)}, u32[]{:S(2)}) collective-permute-start(f32[10,1,16,256]{3,2,1,0:T(8,128)S(1)} %maximum_bitcast_fusion), channel_id=1, source_target_pairs={{0,1},{1,2},{2,3},{4,5},{5,6},{6,7},{8,9},{9,10},{10,11},{12,13},{... | collective-permute-start | bytes 491528 | tf_op jit(solution)/shard_map/ppermute | solution.py:371
  18.8 0.9 collective-permute-done.2.before_y_ref
  19.7 3.0 %copy-done.1 = f32[6912,256]{1,0:T(8,128)S(1)} copy-done((f32[6912,256]{1,0:T(8,128)S(1)}, f32[6912,256]{1,0:T(8,128)}, u32[]{:S(2)}) %copy-start.1) | copy-done | bytes 7077912
  22.7 14.1 %shard_map.96 = (f32[1024,256]{1,0:T(8,128)S(1)}, bf16[2,768,1280]{2,1,0:T(8,128)(2,1)S(1)}, bf16[3,2,1024,256]{3,2,1,0:T(8,128)(2,1)S(1)}) custom-call(s32[2]{0:T(128)S(1)} %pad_add_fusion.7.swap_ref.refs_0_, f32[8,8,16,256]{3,2,1,0:T(8,128)S(1)} %copy-done.2, f32[8,8,16,1]{3,2,1,0:T(8,128)S(1)} %copy.18.filled_ref.refs_2_, ...), custom_call_target="tpu_custom_call" | custom-call | flops 262144 | bytes 262144 | tf_op jit(solution)/shard_map/pallas_call | solution.py:170
  36.8 6.6 %shard_map.97 = (f32[432,8,128]{2,1,0:T(8,128)S(1)}, f32[432,8,128]{2,1,0:T(8,128)S(1)}) custom-call(s32[2,217]{1,0:T(2,128)S(1)} %get-tuple-element.97.refs_0_, bf16[2,768,1280]{2,1,0:T(8,128)(2,1)S(1)} %get-tuple-element.33.refs_1_, bf16[3,2,1024,256]{3,2,1,0:T(8,128)(2,1)S(1)} %get-tuple-element.34.refs_2_), custom_call_target="tpu_custom_call" | custom-call | flops 262144 | bytes 262144 | tf_op jit(solution)/shard_map/pallas_call | solution.py:235
  43.5 2.4 %collective-permute-start.4 = (f32[432,8,128]{2,1,0:T(8,128)S(1)}, f32[432,8,128]{2,1,0:T(8,128)S(1)}, u32[]{:S(2)}, u32[]{:S(2)}) collective-permute-start(f32[432,8,128]{2,1,0:T(8,128)S(1)} %get-tuple-element.35), channel_id=1, source_target_pairs={{0,1},{1,0},{2,3},{3,2},{4,5},{5,4},{6,7},{7,6},{8,9},{9,8},{10,11... | collective-permute-start | bytes 5308424 | tf_op jit(solution)/shard_map/ppermute | solution.py:497
  45.9 6.6 %shard_map.98 = (f32[432,8,128]{2,1,0:T(8,128)S(1)}, f32[432,8,128]{2,1,0:T(8,128)S(1)}) custom-call(s32[2,217]{1,0:T(2,128)S(1)} %get-tuple-element.36.refs_0_, bf16[2,768,1280]{2,1,0:T(8,128)(2,1)S(1)} %get-tuple-element.33.refs_1_, bf16[3,2,1024,256]{3,2,1,0:T(8,128)(2,1)S(1)} %get-tuple-element.34.refs_2_), custom_call_target="tpu_custom_call" | custom-call | flops 262144 | bytes 262144 | tf_op jit(solution)/shard_map/pallas_call | solution.py:235
  52.8 2.5 %collective-permute-start.6 = (f32[216,8,128]{2,1,0:T(8,128)S(1)}, f32[216,8,128]{2,1,0:T(8,128)S(1)}, u32[]{:S(2)}, u32[]{:S(2)}) collective-permute-start(f32[216,8,128]{2,1,0:T(8,128)S(1)} %get-tuple-element.61), channel_id=1, source_target_pairs={{0,4},{1,3},{2,6},{3,1},{4,0},{5,7},{6,2},{7,5},{8,12},{9,11},{10,... | collective-permute-start | bytes 2654216 | tf_op jit(solution)/shard_map/ppermute | solution.py:503
  55.4 1.9 %collective-permute-start.8 = (f32[1,8,16,256]{3,2,1,0:T(8,128)S(1)}, f32[1,8,16,256]{3,2,1,0:T(8,128)S(1)}, u32[]{:S(2)}, u32[]{:S(2)}) collective-permute-start(f32[1,8,16,256]{3,2,1,0:T(8,128)S(1)} %bitcast.65), channel_id=1, source_target_pairs={{0,4},{4,8},{8,12},{12,16},{16,20},{20,24},{24,28},{1,5},{5,9},{9,... | collective-permute-start | bytes 393224 | tf_op jit(solution)/shard_map/ppermute | solution.py:363
  57.5 2.9 %collective-permute-start.7 = (f32[216,8,128]{2,1,0:T(8,128)S(1)}, f32[216,8,128]{2,1,0:T(8,128)S(1)}, u32[]{:S(2)}, u32[]{:S(2)}) collective-permute-start(f32[216,8,128]{2,1,0:T(8,128)S(1)} %get-tuple-element.63), channel_id=1, source_target_pairs={{0,2},{1,9},{2,0},{3,11},{4,6},{5,13},{6,4},{7,15},{8,10},{9,1},{1... | collective-permute-start | bytes 2654216 | tf_op jit(solution)/shard_map/ppermute | solution.py:503
  60.4 1.3 %collective-permute-start.9 = (f32[1,8,16,256]{3,2,1,0:T(8,128)S(1)}, f32[1,8,16,256]{3,2,1,0:T(8,128)S(1)}, u32[]{:S(2)}, u32[]{:S(2)}) collective-permute-start(f32[1,8,16,256]{3,2,1,0:T(8,128)S(1)} %bitcast.64), channel_id=1, source_target_pairs={{4,0},{8,4},{12,8},{16,12},{20,16},{24,20},{28,24},{5,1},{9,5},{13... | collective-permute-start | bytes 393224 | tf_op jit(solution)/shard_map/ppermute | solution.py:363
  61.7 8.2 %collective-permute-done.8.refs_3_ = f32[1,8,16,256]{3,2,1,0:T(8,128)S(1)} collective-permute-done((f32[1,8,16,256]{3,2,1,0:T(8,128)S(1)}, f32[1,8,16,256]{3,2,1,0:T(8,128)S(1)}, u32[]{:S(2)}, u32[]{:S(2)}) %collective-permute-start.8) | collective-permute-done | bytes 131104 | tf_op jit(solution)/shard_map/ppermute | solution.py:363
  70.0 3.2 %collective-permute-start.12 = (f32[108,8,128]{2,1,0:T(8,128)S(1)}, f32[108,8,128]{2,1,0:T(8,128)S(1)}, u32[]{:S(2)}, u32[]{:S(2)}) collective-permute-start(f32[108,8,128]{2,1,0:T(8,128)S(1)} %get-tuple-element.65), channel_id=1, source_target_pairs={{0,2},{1,5},{2,0},{3,7},{4,6},{5,1},{6,4},{7,3},{8,10},{9,13},{10,... | collective-permute-start | bytes 1327112 | tf_op jit(solution)/shard_map/ppermute | solution.py:503
  73.3 1.3 %collective-permute-start.11 = (f32[10,1,16,256]{3,2,1,0:T(8,128)S(1)}, f32[10,1,16,256]{3,2,1,0:T(8,128)S(1)}, u32[]{:S(2)}, u32[]{:S(2)}) collective-permute-start(f32[10,1,16,256]{3,2,1,0:T(8,128)S(1)} %maximum_bitcast_fusion.3), channel_id=1, source_target_pairs={{1,0},{2,1},{3,2},{5,4},{6,5},{7,6},{9,8},{10,9},{11,10},{13,12},{... | collective-permute-start | bytes 491528 | tf_op jit(solution)/shard_map/ppermute | solution.py:371
  74.6 1.0 collective-permute-done.7
  75.7 2.8 %collective-permute-start.13 = (f32[108,8,128]{2,1,0:T(8,128)S(1)}, f32[108,8,128]{2,1,0:T(8,128)S(1)}, u32[]{:S(2)}, u32[]{:S(2)}) collective-permute-start(f32[108,8,128]{2,1,0:T(8,128)S(1)} %get-tuple-element.67), channel_id=1, source_target_pairs={{0,4},{1,17},{2,6},{3,19},{4,0},{5,21},{6,2},{7,23},{8,12},{9,25},... | collective-permute-start | bytes 1327112 | tf_op jit(solution)/shard_map/ppermute | solution.py:503
  78.6 4.0 %collective-permute-start.10 = (f32[10,1,16,256]{3,2,1,0:T(8,128)S(1)}, f32[10,1,16,256]{3,2,1,0:T(8,128)S(1)}, u32[]{:S(2)}, u32[]{:S(2)}) collective-permute-start(f32[10,1,16,256]{3,2,1,0:T(8,128)S(1)} %maximum_bitcast_fusion.2), channel_id=1, source_target_pairs={{0,1},{1,2},{2,3},{4,5},{5,6},{6,7},{8,9},{9,10},{10,11},{12,13},{... | collective-permute-start | bytes 491528 | tf_op jit(solution)/shard_map/ppermute | solution.py:371
  82.6 1.0 collective-permute-done.10.refs_5_
  83.6 5.6 %shard_map.99 = f32[384,256]{1,0:T(8,128)S(1)} custom-call(s32[2]{0:T(128)S(1)} %pad_add_fusion.7.swap_ref.refs_0_, f32[8,8,16,256]{3,2,1,0:T(8,128)S(1)} %bitcast.58, f32[8,8,16,1]{3,2,1,0:T(8,128)S(1)} %copy.18.filled_ref.refs_2_, f32[1,8,16,256]{3,2,1,0:T(8,128)S(1)} %collective-permute-done.8.refs_3_, ...), custom_call_target="tpu_custom_call" | custom-call | flops 98304 | bytes 98304 | tf_op jit(solution)/shard_map/pallas_call | solution.py:328
  89.3 1.6 %collective-permute-start.14 = (f32[54,8,128]{2,1,0:T(8,128)S(1)}, f32[54,8,128]{2,1,0:T(8,128)S(1)}, u32[]{:S(2)}, u32[]{:S(2)}) collective-permute-start(f32[54,8,128]{2,1,0:T(8,128)S(1)} %get-tuple-element.75), channel_id=1, source_target_pairs={{0,8},{1,9},{2,10},{3,11},{4,12},{5,13},{6,14},{7,15},{8,0},{9,1},... | collective-permute-start | bytes 663560 | tf_op jit(solution)/shard_map/ppermute | solution.py:503
  91.5 5.6 %shard_map.100 = f32[384,256]{1,0:T(8,128)S(1)} custom-call(s32[2]{0:T(128)S(1)} %pad_add_fusion.7.swap_ref.refs_0_, f32[8,8,16,256]{3,2,1,0:T(8,128)S(1)} %bitcast.59, f32[8,8,16,1]{3,2,1,0:T(8,128)S(1)} %copy.18.filled_ref.refs_2_, f32[1,8,16,256]{3,2,1,0:T(8,128)S(1)} %collective-permute-done.8.refs_3_, ...), custom_call_target="tpu_custom_call" | custom-call | flops 98304 | bytes 98304 | tf_op jit(solution)/shard_map/pallas_call | solution.py:328
  97.5 2.5 %collective-permute-done.15 = f32[54,8,128]{2,1,0:T(8,128)S(1)} collective-permute-done((f32[54,8,128]{2,1,0:T(8,128)S(1)}, f32[54,8,128]{2,1,0:T(8,128)S(1)}, u32[]{:S(2)}, u32[]{:S(2)}) %collective-permute-start.15) | collective-permute-done | bytes 221216 | tf_op jit(solution)/shard_map/ppermute | solution.py:503
  100.5 4.2 %shard_map.101 = f32[256,256]{1,0:T(8,128)S(1)} custom-call(s32[2]{0:T(128)S(1)} %pad_add_fusion.7.swap_ref.refs_0_, f32[8,8,16,256]{3,2,1,0:T(8,128)S(1)} %bitcast.60, f32[8,8,16,1]{3,2,1,0:T(8,128)S(1)} %copy.18.filled_ref.refs_2_, f32[1,8,16,256]{3,2,1,0:T(8,128)S(1)} %collective-permute-done.8.refs_3_, ...), custom_call_target="tpu_custom_call" | custom-call | flops 65536 | bytes 65536 | tf_op jit(solution)/shard_map/pallas_call | solution.py:328
  104.7 1.0 pad_maximum_fusion
  105.7 1.9 %collective-permute-done.16 = f32[27,8,128]{2,1,0:T(8,128)S(1)} collective-permute-done((f32[27,8,128]{2,1,0:T(8,128)S(1)}, f32[27,8,128]{2,1,0:T(8,128)S(1)}, u32[]{:S(2)}, u32[]{:S(2)}) %collective-permute-start.16) | collective-permute-done | bytes 110624 | tf_op jit(solution)/shard_map/ppermute | solution.py:503
  107.8 1.0 collective-permute-done.17
  (55 shorter events, 6.0 us)
Async XLA Ops:
  0.6 9.3 %copy-start.2 = (f32[8,8,16,256]{3,2,1,0:T(8,128)S(1)}, f32[8,8,16,256]{3,2,1,0:T(8,128)}, u32[]{:S(2)}) copy-start(f32[8,8,16,256]{3,2,1,0:T(8,128)} %inputs_ref.3) | copy-start | bytes 3145732
  2.6 10.6 %collective-permute-start = (f32[1,8,16,256]{3,2,1,0:T(8,128)S(1)}, f32[1,8,16,256]{3,2,1,0:T(8,128)S(1)}, u32[]{:S(2)}, u32[]{:S(2)}) collective-permute-start(f32[1,8,16,256]{3,2,1,0:T(8,128)S(1)} %get-tuple-element.73), channel_id=1, source_target_pairs={{0,4},{4,8},{8,12},{12,16},{16,20},{20,24},{24,28},{1,5},{5,9},{9,... | collective-permute-start | bytes 393224 | tf_op jit(solution)/shard_map/ppermute | solution.py:363
  7.4 6.9 %collective-permute-start.1 = (f32[1,8,16,256]{3,2,1,0:T(8,128)S(1)}, f32[1,8,16,256]{3,2,1,0:T(8,128)S(1)}, u32[]{:S(2)}, u32[]{:S(2)}) collective-permute-start(f32[1,8,16,256]{3,2,1,0:T(8,128)S(1)} %get-tuple-element.72), channel_id=1, source_target_pairs={{4,0},{8,4},{12,8},{16,12},{20,16},{24,20},{28,24},{5,1},{9,5},{13... | collective-permute-start | bytes 393224 | tf_op jit(solution)/shard_map/ppermute | solution.py:363
  10.0 3.0 %copy-start = (f32[6912,256]{1,0:T(8,128)S(1)}, f32[6912,256]{1,0:T(8,128)}, u32[]{:S(2)}) copy-start(f32[6912,256]{1,0:T(8,128)} %param.10) | copy-start | bytes 21233668
  13.0 6.7 %copy-start.3 = (f32[8,8,16,256]{3,2,1,0:T(8,128)S(1)}, f32[8,8,16,256]{3,2,1,0:T(8,128)}, u32[]{:S(2)}) copy-start(f32[8,8,16,256]{3,2,1,0:T(8,128)} %param.9) | copy-start | bytes 3145732
  14.3 4.5 %collective-permute-start.3 = (f32[10,1,16,256]{3,2,1,0:T(8,128)S(1)}, f32[10,1,16,256]{3,2,1,0:T(8,128)S(1)}, u32[]{:S(2)}, u32[]{:S(2)}) collective-permute-start(f32[10,1,16,256]{3,2,1,0:T(8,128)S(1)} %maximum_bitcast_fusion.1), channel_id=1, source_target_pairs={{1,0},{2,1},{3,2},{5,4},{6,5},{7,6},{9,8},{10,9},{11,10},{13,12},{... | collective-permute-start | bytes 491528 | tf_op jit(solution)/shard_map/ppermute | solution.py:371
  15.6 4.0 %collective-permute-start.2 = (f32[10,1,16,256]{3,2,1,0:T(8,128)S(1)}, f32[10,1,16,256]{3,2,1,0:T(8,128)S(1)}, u32[]{:S(2)}, u32[]{:S(2)}) collective-permute-start(f32[10,1,16,256]{3,2,1,0:T(8,128)S(1)} %maximum_bitcast_fusion), channel_id=1, source_target_pairs={{0,1},{1,2},{2,3},{4,5},{5,6},{6,7},{8,9},{9,10},{10,11},{12,13},{... | collective-permute-start | bytes 491528 | tf_op jit(solution)/shard_map/ppermute | solution.py:371
  19.7 3.0 %copy-start.1 = (f32[6912,256]{1,0:T(8,128)S(1)}, f32[6912,256]{1,0:T(8,128)}, u32[]{:S(2)}) copy-start(f32[6912,256]{1,0:T(8,128)} %param.10) | copy-start | bytes 21233668
  43.5 9.2 %collective-permute-start.4 = (f32[432,8,128]{2,1,0:T(8,128)S(1)}, f32[432,8,128]{2,1,0:T(8,128)S(1)}, u32[]{:S(2)}, u32[]{:S(2)}) collective-permute-start(f32[432,8,128]{2,1,0:T(8,128)S(1)} %get-tuple-element.35), channel_id=1, source_target_pairs={{0,1},{1,0},{2,3},{3,2},{4,5},{5,4},{6,7},{7,6},{8,9},{9,8},{10,11... | collective-permute-start | bytes 5308424 | tf_op jit(solution)/shard_map/ppermute | solution.py:497
  52.5 4.7 %collective-permute-start.5 = (f32[432,8,128]{2,1,0:T(8,128)S(1)}, f32[432,8,128]{2,1,0:T(8,128)S(1)}, u32[]{:S(2)}, u32[]{:S(2)}) collective-permute-start(f32[432,8,128]{2,1,0:T(8,128)S(1)} %get-tuple-element.40), channel_id=1, source_target_pairs={{0,1},{1,0},{2,3},{3,2},{4,5},{5,4},{6,7},{7,6},{8,9},{9,8},{10,11... | collective-permute-start | bytes 5308424 | tf_op jit(solution)/shard_map/ppermute | solution.py:497
  52.8 17.1 %collective-permute-start.6 = (f32[216,8,128]{2,1,0:T(8,128)S(1)}, f32[216,8,128]{2,1,0:T(8,128)S(1)}, u32[]{:S(2)}, u32[]{:S(2)}) collective-permute-start(f32[216,8,128]{2,1,0:T(8,128)S(1)} %get-tuple-element.61), channel_id=1, source_target_pairs={{0,4},{1,3},{2,6},{3,1},{4,0},{5,7},{6,2},{7,5},{8,12},{9,11},{10,... | collective-permute-start | bytes 2654216 | tf_op jit(solution)/shard_map/ppermute | solution.py:503
  55.4 14.6 %collective-permute-start.8 = (f32[1,8,16,256]{3,2,1,0:T(8,128)S(1)}, f32[1,8,16,256]{3,2,1,0:T(8,128)S(1)}, u32[]{:S(2)}, u32[]{:S(2)}) collective-permute-start(f32[1,8,16,256]{3,2,1,0:T(8,128)S(1)} %bitcast.65), channel_id=1, source_target_pairs={{0,4},{4,8},{8,12},{12,16},{16,20},{20,24},{24,28},{1,5},{5,9},{9,... | collective-permute-start | bytes 393224 | tf_op jit(solution)/shard_map/ppermute | solution.py:363
  57.5 18.1 %collective-permute-start.7 = (f32[216,8,128]{2,1,0:T(8,128)S(1)}, f32[216,8,128]{2,1,0:T(8,128)S(1)}, u32[]{:S(2)}, u32[]{:S(2)}) collective-permute-start(f32[216,8,128]{2,1,0:T(8,128)S(1)} %get-tuple-element.63), channel_id=1, source_target_pairs={{0,2},{1,9},{2,0},{3,11},{4,6},{5,13},{6,4},{7,15},{8,10},{9,1},{1... | collective-permute-start | bytes 2654216 | tf_op jit(solution)/shard_map/ppermute | solution.py:503
  60.4 9.5 %collective-permute-start.9 = (f32[1,8,16,256]{3,2,1,0:T(8,128)S(1)}, f32[1,8,16,256]{3,2,1,0:T(8,128)S(1)}, u32[]{:S(2)}, u32[]{:S(2)}) collective-permute-start(f32[1,8,16,256]{3,2,1,0:T(8,128)S(1)} %bitcast.64), channel_id=1, source_target_pairs={{4,0},{8,4},{12,8},{16,12},{20,16},{24,20},{28,24},{5,1},{9,5},{13... | collective-permute-start | bytes 393224 | tf_op jit(solution)/shard_map/ppermute | solution.py:363
  70.0 19.2 %collective-permute-start.12 = (f32[108,8,128]{2,1,0:T(8,128)S(1)}, f32[108,8,128]{2,1,0:T(8,128)S(1)}, u32[]{:S(2)}, u32[]{:S(2)}) collective-permute-start(f32[108,8,128]{2,1,0:T(8,128)S(1)} %get-tuple-element.65), channel_id=1, source_target_pairs={{0,2},{1,5},{2,0},{3,7},{4,6},{5,1},{6,4},{7,3},{8,10},{9,13},{10,... | collective-permute-start | bytes 1327112 | tf_op jit(solution)/shard_map/ppermute | solution.py:503
  73.3 9.3 %collective-permute-start.11 = (f32[10,1,16,256]{3,2,1,0:T(8,128)S(1)}, f32[10,1,16,256]{3,2,1,0:T(8,128)S(1)}, u32[]{:S(2)}, u32[]{:S(2)}) collective-permute-start(f32[10,1,16,256]{3,2,1,0:T(8,128)S(1)} %maximum_bitcast_fusion.3), channel_id=1, source_target_pairs={{1,0},{2,1},{3,2},{5,4},{6,5},{7,6},{9,8},{10,9},{11,10},{13,12},{... | collective-permute-start | bytes 491528 | tf_op jit(solution)/shard_map/ppermute | solution.py:371
  75.7 15.2 %collective-permute-start.13 = (f32[108,8,128]{2,1,0:T(8,128)S(1)}, f32[108,8,128]{2,1,0:T(8,128)S(1)}, u32[]{:S(2)}, u32[]{:S(2)}) collective-permute-start(f32[108,8,128]{2,1,0:T(8,128)S(1)} %get-tuple-element.67), channel_id=1, source_target_pairs={{0,4},{1,17},{2,6},{3,19},{4,0},{5,21},{6,2},{7,23},{8,12},{9,25},... | collective-permute-start | bytes 1327112 | tf_op jit(solution)/shard_map/ppermute | solution.py:503
  78.6 5.0 %collective-permute-start.10 = (f32[10,1,16,256]{3,2,1,0:T(8,128)S(1)}, f32[10,1,16,256]{3,2,1,0:T(8,128)S(1)}, u32[]{:S(2)}, u32[]{:S(2)}) collective-permute-start(f32[10,1,16,256]{3,2,1,0:T(8,128)S(1)} %maximum_bitcast_fusion.2), channel_id=1, source_target_pairs={{0,1},{1,2},{2,3},{4,5},{5,6},{6,7},{8,9},{9,10},{10,11},{12,13},{... | collective-permute-start | bytes 491528 | tf_op jit(solution)/shard_map/ppermute | solution.py:371
  89.3 8.1 %collective-permute-start.14 = (f32[54,8,128]{2,1,0:T(8,128)S(1)}, f32[54,8,128]{2,1,0:T(8,128)S(1)}, u32[]{:S(2)}, u32[]{:S(2)}) collective-permute-start(f32[54,8,128]{2,1,0:T(8,128)S(1)} %get-tuple-element.75), channel_id=1, source_target_pairs={{0,8},{1,9},{2,10},{3,11},{4,12},{5,13},{6,14},{7,15},{8,0},{9,1},... | collective-permute-start | bytes 663560 | tf_op jit(solution)/shard_map/ppermute | solution.py:503
  91.0 9.0 %collective-permute-start.15 = (f32[54,8,128]{2,1,0:T(8,128)S(1)}, f32[54,8,128]{2,1,0:T(8,128)S(1)}, u32[]{:S(2)}, u32[]{:S(2)}) collective-permute-start(f32[54,8,128]{2,1,0:T(8,128)S(1)} %get-tuple-element.77), channel_id=1, source_target_pairs={{0,8},{1,5},{2,10},{3,7},{4,12},{5,1},{6,14},{7,3},{8,0},{9,13},{1... | collective-permute-start | bytes 663560 | tf_op jit(solution)/shard_map/ppermute | solution.py:503
  97.4 10.2 %collective-permute-start.16 = (f32[27,8,128]{2,1,0:T(8,128)S(1)}, f32[27,8,128]{2,1,0:T(8,128)S(1)}, u32[]{:S(2)}, u32[]{:S(2)}) collective-permute-start(f32[27,8,128]{2,1,0:T(8,128)S(1)} %get-tuple-element.79), channel_id=1, source_target_pairs={{0,16},{1,17},{2,18},{3,19},{4,20},{5,21},{6,22},{7,23},{8,24},{9,... | collective-permute-start | bytes 331784 | tf_op jit(solution)/shard_map/ppermute | solution.py:503
  100.1 8.8 %collective-permute-start.17 = (f32[27,8,128]{2,1,0:T(8,128)S(1)}, f32[27,8,128]{2,1,0:T(8,128)S(1)}, u32[]{:S(2)}, u32[]{:S(2)}) collective-permute-start(f32[27,8,128]{2,1,0:T(8,128)S(1)} %get-tuple-element.81), channel_id=1, source_target_pairs={{0,16},{1,3},{2,18},{3,1},{4,20},{5,7},{6,22},{7,5},{8,24},{9,11},... | collective-permute-start | bytes 331784 | tf_op jit(solution)/shard_map/ppermute | solution.py:503

commit v5 on v4

--- a/solution.py
+++ b/solution.py
@@ -503,14 +503,14 @@
         return keep, send, lax.ppermute(send, ("gx", "gy"), pairs)
 
     keep_a, send_a, got_a = terms(0, tables[0])
-    keep_b, send_b, got_b = terms(1, after(tables[1], send_a))
-    keep_a, send_a, got_a = stage(0, 0, after(keep_a, send_b), got_a)
+    keep_a, send_a, got_a = stage(0, 0, keep_a, got_a)
     face, sides = data_halo_x(send_a)
-    keep_b, send_b, got_b = stage(1, 0, after(keep_b, face), got_b)
+    keep_b, send_b, got_b = terms(1, after(tables[1], send_a, face))
     keep_a, send_a, got_a = stage(0, 1, after(keep_a, send_b), got_a)
-    line, ends = data_halo_y(sides, send_a)
-    keep_b, send_b, got_b = stage(1, 1, after(keep_b, line), got_b)
+    keep_b, send_b, got_b = stage(1, 0, after(keep_b, send_a), got_b)
+    _, ends = data_halo_y(sides, send_b)
     pieces = [data_piece(after(swap, send_b), sides, ends, 0, cuts[0])]
+    keep_b, send_b, got_b = stage(1, 1, after(keep_b, pieces[0]), got_b)
     for index in range(2, stages):
         keep_a, send_a, got_a = stage(0, index, after(keep_a, pieces[-1], send_b), got_a)
         keep_b, send_b, got_b = stage(1, index, after(keep_b, send_a), got_b)

time: 110 us -> 127 us (1.15)
  the two profiles are of different devices: /device:TPU:0 before, /device:TPU:1 now
where the time goes in v5:
time: 127 us; the launch traced here: 126 us
  starting transfers between devices  43.6 us (34%)
  Pallas kernels  42.9 us (34%)
  waiting for transfers between devices  25.9 us (20%)
  local copies, waits for them, and re-layouts  7.82 us (6%)
  other arithmetic  4.92 us (4%)
    ppermute x8, starting transfers between devices, stage(): return (keep, send, lax.ppermute(send, ('gx', 'gy'), pairs))  18.8 us
    pallas_call x3, Pallas kernels, data_grad(): pl.pallas_call(kernel, grid=(3,), in_specs=[pl.BlockSpec(memory_space=plt...  15.4 us
    ppermute x8, waiting for transfers between devices, stage(): return (keep, send, lax.ppermute(send, ('gx', 'gy'), pairs))  15.4 us
    pallas_call x1, Pallas kernels, forward(): pl.pallas_call(forward_kernel, grid=(3,), in_specs=[pl.BlockSpec(memory_s...  14.1 us
    pallas_call x2, Pallas kernels, filter_terms(): pl.pallas_call(kernel, in_specs=[pl.BlockSpec(memory_space=pltpu.SMEM), W...  13.2 us
    ppermute x4, starting transfers between devices, halo_x(): return (lax.ppermute(last, 'gx', up), lax.ppermute(first, 'gx', down))  10.6 us
    ppermute x2, starting transfers between devices, halo_y(): lax.ppermute(low[:, None], 'gy', down)  8.82 us
    unnamed x9, local copies, waits for them, and re-layouts  6.95 us
  transfers between devices with their start and end apart: 18, of which 6 were waited for; matrix products, arithmetic and copies ran while one was open for 3% of the time, Pallas kernels for 12%

profile of v5, /device:TPU:1, one launch (start us, length us, event | category | flops | bytes accessed | tf_op | source)
XLA Modules:
  0.0 126.2 jit_solution(5076211970968480432)
XLA Ops:
  0.6 0.9 fusion.7
  1.5 1.1 slice_multiply_fusion
  2.6 4.0 %collective-permute-start = (f32[1,8,16,256]{3,2,1,0:T(8,128)S(1)}, f32[1,8,16,256]{3,2,1,0:T(8,128)S(1)}, u32[]{:S(2)}, u32[]{:S(2)}) collective-permute-start(f32[1,8,16,256]{3,2,1,0:T(8,128)S(1)} %get-tuple-element.71), channel_id=1, source_target_pairs={{0,4},{4,8},{8,12},{12,16},{16,20},{20,24},{24,28},{1,5},{5,9},{9,... | collective-permute-start | bytes 393224 | tf_op jit(solution)/shard_map/ppermute | solution.py:363
  6.5 1.3 %collective-permute-start.1 = (f32[1,8,16,256]{3,2,1,0:T(8,128)S(1)}, f32[1,8,16,256]{3,2,1,0:T(8,128)S(1)}, u32[]{:S(2)}, u32[]{:S(2)}) collective-permute-start(f32[1,8,16,256]{3,2,1,0:T(8,128)S(1)} %get-tuple-element.70), channel_id=1, source_target_pairs={{4,0},{8,4},{12,8},{16,12},{20,16},{24,20},{28,24},{5,1},{9,5},{13... | collective-permute-start | bytes 393224 | tf_op jit(solution)/shard_map/ppermute | solution.py:363
  9.1 3.0 %copy-done = f32[6912,256]{1,0:T(8,128)S(1)} copy-done((f32[6912,256]{1,0:T(8,128)S(1)}, f32[6912,256]{1,0:T(8,128)}, u32[]{:S(2)}) %copy-start) | copy-done | bytes 7077912
  12.4 3.9 %collective-permute-start.3 = (f32[10,1,16,256]{3,2,1,0:T(8,128)S(1)}, f32[10,1,16,256]{3,2,1,0:T(8,128)S(1)}, u32[]{:S(2)}, u32[]{:S(2)}) collective-permute-start(f32[10,1,16,256]{3,2,1,0:T(8,128)S(1)} %maximum_bitcast_fusion.1), channel_id=1, source_target_pairs={{1,0},{2,1},{3,2},{5,4},{6,5},{7,6},{9,8},{10,9},{11,10},{13,12},{... | collective-permute-start | bytes 491528 | tf_op jit(solution)/shard_map/ppermute | solution.py:371
  16.3 3.0 %collective-permute-start.2 = (f32[10,1,16,256]{3,2,1,0:T(8,128)S(1)}, f32[10,1,16,256]{3,2,1,0:T(8,128)S(1)}, u32[]{:S(2)}, u32[]{:S(2)}) collective-permute-start(f32[10,1,16,256]{3,2,1,0:T(8,128)S(1)} %maximum_bitcast_fusion), channel_id=1, source_target_pairs={{0,1},{1,2},{2,3},{4,5},{5,6},{6,7},{8,9},{9,10},{10,11},{12,13},{... | collective-permute-start | bytes 491528 | tf_op jit(solution)/shard_map/ppermute | solution.py:371
  19.5 0.9 collective-permute-done.3.after_y_ref
  20.4 1.2 collective-permute-done.2.before_y_ref
  21.6 3.0 %copy-done.1 = f32[6912,256]{1,0:T(8,128)S(1)} copy-done((f32[6912,256]{1,0:T(8,128)S(1)}, f32[6912,256]{1,0:T(8,128)}, u32[]{:S(2)}) %copy-start.1) | copy-done | bytes 7077912
  24.6 14.1 %shard_map.96 = (f32[1024,256]{1,0:T(8,128)S(1)}, bf16[2,768,1280]{2,1,0:T(8,128)(2,1)S(1)}, bf16[3,2,1024,256]{3,2,1,0:T(8,128)(2,1)S(1)}) custom-call(s32[2]{0:T(128)S(1)} %pad_add_fusion.7.swap_ref.refs_0_, f32[8,8,16,256]{3,2,1,0:T(8,128)S(1)} %copy-done.2, f32[8,8,16,1]{3,2,1,0:T(8,128)S(1)} %copy.18.filled_ref.refs_2_, ...), custom_call_target="tpu_custom_call" | custom-call | flops 262144 | bytes 262144 | tf_op jit(solution)/shard_map/pallas_call | solution.py:170
  38.8 6.6 %shard_map.97 = (f32[432,8,128]{2,1,0:T(8,128)S(1)}, f32[432,8,128]{2,1,0:T(8,128)S(1)}) custom-call(s32[2,217]{1,0:T(2,128)S(1)} %get-tuple-element.95.refs_0_, bf16[2,768,1280]{2,1,0:T(8,128)(2,1)S(1)} %get-tuple-element.32.refs_1_, bf16[3,2,1024,256]{3,2,1,0:T(8,128)(2,1)S(1)} %get-tuple-element.33.refs_2_), custom_call_target="tpu_custom_call" | custom-call | flops 262144 | bytes 262144 | tf_op jit(solution)/shard_map/pallas_call | solution.py:235
  45.5 3.7 %collective-permute-done.4 = f32[432,8,128]{2,1,0:T(8,128)S(1)} collective-permute-done((f32[432,8,128]{2,1,0:T(8,128)S(1)}, f32[432,8,128]{2,1,0:T(8,128)S(1)}, u32[]{:S(2)}, u32[]{:S(2)}) %collective-permute-start.4) | collective-permute-done | bytes 1769504 | tf_op jit(solution)/shard_map/ppermute | solution.py:497
  49.4 6.6 %shard_map.98 = (f32[432,8,128]{2,1,0:T(8,128)S(1)}, f32[432,8,128]{2,1,0:T(8,128)S(1)}) custom-call(s32[2,217]{1,0:T(2,128)S(1)} %get-tuple-element.38.refs_0_, bf16[2,768,1280]{2,1,0:T(8,128)(2,1)S(1)} %get-tuple-element.32.refs_1_, bf16[3,2,1024,256]{3,2,1,0:T(8,128)(2,1)S(1)} %get-tuple-element.33.refs_2_), custom_call_target="tpu_custom_call" | custom-call | flops 262144 | bytes 262144 | tf_op jit(solution)/shard_map/pallas_call | solution.py:235
  56.3 2.5 %collective-permute-start.5 = (f32[216,8,128]{2,1,0:T(8,128)S(1)}, f32[216,8,128]{2,1,0:T(8,128)S(1)}, u32[]{:S(2)}, u32[]{:S(2)}) collective-permute-start(f32[216,8,128]{2,1,0:T(8,128)S(1)} %get-tuple-element.61), channel_id=1, source_target_pairs={{0,4},{1,3},{2,6},{3,1},{4,0},{5,7},{6,2},{7,5},{8,12},{9,11},{10,... | collective-permute-start | bytes 2654216 | tf_op jit(solution)/shard_map/ppermute | solution.py:503
  58.7 4.1 %collective-permute-start.7 = (f32[1,8,16,256]{3,2,1,0:T(8,128)S(1)}, f32[1,8,16,256]{3,2,1,0:T(8,128)S(1)}, u32[]{:S(2)}, u32[]{:S(2)}) collective-permute-start(f32[1,8,16,256]{3,2,1,0:T(8,128)S(1)} %bitcast.65), channel_id=1, source_target_pairs={{0,4},{4,8},{8,12},{12,16},{16,20},{20,24},{24,28},{1,5},{5,9},{9,... | collective-permute-start | bytes 393224 | tf_op jit(solution)/shard_map/ppermute | solution.py:363
  62.8 6.7 %collective-permute-done.5 = f32[216,8,128]{2,1,0:T(8,128)S(1)} collective-permute-done((f32[216,8,128]{2,1,0:T(8,128)S(1)}, f32[216,8,128]{2,1,0:T(8,128)S(1)}, u32[]{:S(2)}, u32[]{:S(2)}) %collective-permute-start.5) | collective-permute-done | bytes 884768 | tf_op jit(solution)/shard_map/ppermute | solution.py:503
  69.8 2.5 %collective-permute-start.11 = (f32[216,8,128]{2,1,0:T(8,128)S(1)}, f32[216,8,128]{2,1,0:T(8,128)S(1)}, u32[]{:S(2)}, u32[]{:S(2)}) collective-permute-start(f32[216,8,128]{2,1,0:T(8,128)S(1)} %get-tuple-element.59), channel_id=1, source_target_pairs={{0,2},{1,9},{2,0},{3,11},{4,6},{5,13},{6,4},{7,15},{8,10},{9,1},{1... | collective-permute-start | bytes 2654216 | tf_op jit(solution)/shard_map/ppermute | solution.py:503
  72.3 1.3 %collective-permute-start.8 = (f32[1,8,16,256]{3,2,1,0:T(8,128)S(1)}, f32[1,8,16,256]{3,2,1,0:T(8,128)S(1)}, u32[]{:S(2)}, u32[]{:S(2)}) collective-permute-start(f32[1,8,16,256]{3,2,1,0:T(8,128)S(1)} %bitcast.64), channel_id=1, source_target_pairs={{4,0},{8,4},{12,8},{16,12},{20,16},{24,20},{28,24},{5,1},{9,5},{13... | collective-permute-start | bytes 393224 | tf_op jit(solution)/shard_map/ppermute | solution.py:363
  73.7 4.7 %collective-permute-done.8.refs_4_ = f32[1,8,16,256]{3,2,1,0:T(8,128)S(1)} collective-permute-done((f32[1,8,16,256]{3,2,1,0:T(8,128)S(1)}, f32[1,8,16,256]{3,2,1,0:T(8,128)S(1)}, u32[]{:S(2)}, u32[]{:S(2)}) %collective-permute-start.8) | collective-permute-done | bytes 131104 | tf_op jit(solution)/shard_map/ppermute | solution.py:363
  78.4 4.9 %collective-permute-start.10 = (f32[10,1,16,256]{3,2,1,0:T(8,128)S(1)}, f32[10,1,16,256]{3,2,1,0:T(8,128)S(1)}, u32[]{:S(2)}, u32[]{:S(2)}) collective-permute-start(f32[10,1,16,256]{3,2,1,0:T(8,128)S(1)} %maximum_bitcast_fusion.3), channel_id=1, source_target_pairs={{1,0},{2,1},{3,2},{5,4},{6,5},{7,6},{9,8},{10,9},{11,10},{13,12},{... | collective-permute-start | bytes 491528 | tf_op jit(solution)/shard_map/ppermute | solution.py:371
  83.3 2.1 %collective-permute-start.9 = (f32[10,1,16,256]{3,2,1,0:T(8,128)S(1)}, f32[10,1,16,256]{3,2,1,0:T(8,128)S(1)}, u32[]{:S(2)}, u32[]{:S(2)}) collective-permute-start(f32[10,1,16,256]{3,2,1,0:T(8,128)S(1)} %maximum_bitcast_fusion.2), channel_id=1, source_target_pairs={{0,1},{1,2},{2,3},{4,5},{5,6},{6,7},{8,9},{9,10},{10,11},{12,13},{... | collective-permute-start | bytes 491528 | tf_op jit(solution)/shard_map/ppermute | solution.py:371
  85.4 7.0 %collective-permute-start.12 = (f32[108,8,128]{2,1,0:T(8,128)S(1)}, f32[108,8,128]{2,1,0:T(8,128)S(1)}, u32[]{:S(2)}, u32[]{:S(2)}) collective-permute-start(f32[108,8,128]{2,1,0:T(8,128)S(1)} %get-tuple-element.63), channel_id=1, source_target_pairs={{0,2},{1,5},{2,0},{3,7},{4,6},{5,1},{6,4},{7,3},{8,10},{9,13},{10,... | collective-permute-start | bytes 1327112 | tf_op jit(solution)/shard_map/ppermute | solution.py:503
  92.4 5.6 %shard_map.99 = f32[384,256]{1,0:T(8,128)S(1)} custom-call(s32[2]{0:T(128)S(1)} %pad_add_fusion.7.swap_ref.refs_0_, f32[8,8,16,256]{3,2,1,0:T(8,128)S(1)} %bitcast.58, f32[8,8,16,1]{3,2,1,0:T(8,128)S(1)} %copy.18.filled_ref.refs_2_, f32[1,8,16,256]{3,2,1,0:T(8,128)S(1)} %collective-permute-done.7.refs_3_, ...), custom_call_target="tpu_custom_call" | custom-call | flops 98304 | bytes 98304 | tf_op jit(solution)/shard_map/pallas_call | solution.py:328
  98.2 2.5 %collective-permute-start.13 = (f32[108,8,128]{2,1,0:T(8,128)S(1)}, f32[108,8,128]{2,1,0:T(8,128)S(1)}, u32[]{:S(2)}, u32[]{:S(2)}) collective-permute-start(f32[108,8,128]{2,1,0:T(8,128)S(1)} %get-tuple-element.65), channel_id=1, source_target_pairs={{0,4},{1,17},{2,6},{3,19},{4,0},{5,21},{6,2},{7,23},{8,12},{9,25},... | collective-permute-start | bytes 1327112 | tf_op jit(solution)/shard_map/ppermute | solution.py:503
  100.8 1.7 %collective-permute-start.14 = (f32[54,8,128]{2,1,0:T(8,128)S(1)}, f32[54,8,128]{2,1,0:T(8,128)S(1)}, u32[]{:S(2)}, u32[]{:S(2)}) collective-permute-start(f32[54,8,128]{2,1,0:T(8,128)S(1)} %get-tuple-element.73), channel_id=1, source_target_pairs={{0,8},{1,9},{2,10},{3,11},{4,12},{5,13},{6,14},{7,15},{8,0},{9,1},... | collective-permute-start | bytes 663560 | tf_op jit(solution)/shard_map/ppermute | solution.py:503
  102.5 8.7 %collective-permute-done.13 = f32[108,8,128]{2,1,0:T(8,128)S(1)} collective-permute-done((f32[108,8,128]{2,1,0:T(8,128)S(1)}, f32[108,8,128]{2,1,0:T(8,128)S(1)}, u32[]{:S(2)}, u32[]{:S(2)}) %collective-permute-start.13) | collective-permute-done | bytes 442400 | tf_op jit(solution)/shard_map/ppermute | solution.py:503
  111.4 5.6 %shard_map.100 = f32[384,256]{1,0:T(8,128)S(1)} custom-call(s32[2]{0:T(128)S(1)} %pad_add_fusion.7.swap_ref.refs_0_, f32[8,8,16,256]{3,2,1,0:T(8,128)S(1)} %bitcast.59, f32[8,8,16,1]{3,2,1,0:T(8,128)S(1)} %copy.18.filled_ref.refs_2_, f32[1,8,16,256]{3,2,1,0:T(8,128)S(1)} %collective-permute-done.7.refs_3_, ...), custom_call_target="tpu_custom_call" | custom-call | flops 98304 | bytes 98304 | tf_op jit(solution)/shard_map/pallas_call | solution.py:328
  117.1 2.4 %collective-permute-start.16 = (f32[27,8,128]{2,1,0:T(8,128)S(1)}, f32[27,8,128]{2,1,0:T(8,128)S(1)}, u32[]{:S(2)}, u32[]{:S(2)}) collective-permute-start(f32[27,8,128]{2,1,0:T(8,128)S(1)} %get-tuple-element.77), channel_id=1, source_target_pairs={{0,16},{1,17},{2,18},{3,19},{4,20},{5,21},{6,22},{7,23},{8,24},{9,... | collective-permute-start | bytes 331784 | tf_op jit(solution)/shard_map/ppermute | solution.py:503
  119.6 4.2 %shard_map.101 = f32[256,256]{1,0:T(8,128)S(1)} custom-call(s32[2]{0:T(128)S(1)} %pad_add_fusion.7.swap_ref.refs_0_, f32[8,8,16,256]{3,2,1,0:T(8,128)S(1)} %bitcast.60, f32[8,8,16,1]{3,2,1,0:T(8,128)S(1)} %copy.18.filled_ref.refs_2_, f32[1,8,16,256]{3,2,1,0:T(8,128)S(1)} %collective-permute-done.7.refs_3_, ...), custom_call_target="tpu_custom_call" | custom-call | flops 65536 | bytes 65536 | tf_op jit(solution)/shard_map/pallas_call | solution.py:328
  124.0 1.0 pad_maximum_fusion
  125.3 0.9 copy.26
  (55 shorter events, 3.4 us)
Async XLA Ops:
  0.6 8.4 %copy-start.2 = (f32[8,8,16,256]{3,2,1,0:T(8,128)S(1)}, f32[8,8,16,256]{3,2,1,0:T(8,128)}, u32[]{:S(2)}) copy-start(f32[8,8,16,256]{3,2,1,0:T(8,128)} %inputs_ref.3) | copy-start | bytes 3145732
  2.6 9.7 %collective-permute-start = (f32[1,8,16,256]{3,2,1,0:T(8,128)S(1)}, f32[1,8,16,256]{3,2,1,0:T(8,128)S(1)}, u32[]{:S(2)}, u32[]{:S(2)}) collective-permute-start(f32[1,8,16,256]{3,2,1,0:T(8,128)S(1)} %get-tuple-element.71), channel_id=1, source_target_pairs={{0,4},{4,8},{8,12},{12,16},{16,20},{20,24},{24,28},{1,5},{5,9},{9,... | collective-permute-start | bytes 393224 | tf_op jit(solution)/shard_map/ppermute | solution.py:363
  6.5 5.8 %collective-permute-start.1 = (f32[1,8,16,256]{3,2,1,0:T(8,128)S(1)}, f32[1,8,16,256]{3,2,1,0:T(8,128)S(1)}, u32[]{:S(2)}, u32[]{:S(2)}) collective-permute-start(f32[1,8,16,256]{3,2,1,0:T(8,128)S(1)} %get-tuple-element.70), channel_id=1, source_target_pairs={{4,0},{8,4},{12,8},{16,12},{20,16},{24,20},{28,24},{5,1},{9,5},{13... | collective-permute-start | bytes 393224 | tf_op jit(solution)/shard_map/ppermute | solution.py:363
  9.1 3.0 %copy-start = (f32[6912,256]{1,0:T(8,128)S(1)}, f32[6912,256]{1,0:T(8,128)}, u32[]{:S(2)}) copy-start(f32[6912,256]{1,0:T(8,128)} %param.10) | copy-start | bytes 21233668
  12.1 9.5 %copy-start.3 = (f32[8,8,16,256]{3,2,1,0:T(8,128)S(1)}, f32[8,8,16,256]{3,2,1,0:T(8,128)}, u32[]{:S(2)}) copy-start(f32[8,8,16,256]{3,2,1,0:T(8,128)} %param.9) | copy-start | bytes 3145732
  12.4 8.0 %collective-permute-start.3 = (f32[10,1,16,256]{3,2,1,0:T(8,128)S(1)}, f32[10,1,16,256]{3,2,1,0:T(8,128)S(1)}, u32[]{:S(2)}, u32[]{:S(2)}) collective-permute-start(f32[10,1,16,256]{3,2,1,0:T(8,128)S(1)} %maximum_bitcast_fusion.1), channel_id=1, source_target_pairs={{1,0},{2,1},{3,2},{5,4},{6,5},{7,6},{9,8},{10,9},{11,10},{13,12},{... | collective-permute-start | bytes 491528 | tf_op jit(solution)/shard_map/ppermute | solution.py:371
  16.3 5.3 %collective-permute-start.2 = (f32[10,1,16,256]{3,2,1,0:T(8,128)S(1)}, f32[10,1,16,256]{3,2,1,0:T(8,128)S(1)}, u32[]{:S(2)}, u32[]{:S(2)}) collective-permute-start(f32[10,1,16,256]{3,2,1,0:T(8,128)S(1)} %maximum_bitcast_fusion), channel_id=1, source_target_pairs={{0,1},{1,2},{2,3},{4,5},{5,6},{6,7},{8,9},{9,10},{10,11},{12,13},{... | collective-permute-start | bytes 491528 | tf_op jit(solution)/shard_map/ppermute | solution.py:371
  21.6 3.0 %copy-start.1 = (f32[6912,256]{1,0:T(8,128)S(1)}, f32[6912,256]{1,0:T(8,128)}, u32[]{:S(2)}) copy-start(f32[6912,256]{1,0:T(8,128)} %param.10) | copy-start | bytes 21233668
  45.4 3.8 %collective-permute-start.4 = (f32[432,8,128]{2,1,0:T(8,128)S(1)}, f32[432,8,128]{2,1,0:T(8,128)S(1)}, u32[]{:S(2)}, u32[]{:S(2)}) collective-permute-start(f32[432,8,128]{2,1,0:T(8,128)S(1)} %get-tuple-element.35), channel_id=1, source_target_pairs={{0,1},{1,0},{2,3},{3,2},{4,5},{5,4},{6,7},{7,6},{8,9},{9,8},{10,11... | collective-permute-start | bytes 5308424 | tf_op jit(solution)/shard_map/ppermute | solution.py:497
  56.1 13.5 %collective-permute-start.6 = (f32[432,8,128]{2,1,0:T(8,128)S(1)}, f32[432,8,128]{2,1,0:T(8,128)S(1)}, u32[]{:S(2)}, u32[]{:S(2)}) collective-permute-start(f32[432,8,128]{2,1,0:T(8,128)S(1)} %get-tuple-element.40), channel_id=1, source_target_pairs={{0,1},{1,0},{2,3},{3,2},{4,5},{5,4},{6,7},{7,6},{8,9},{9,8},{10,11... | collective-permute-start | bytes 5308424 | tf_op jit(solution)/shard_map/ppermute | solution.py:497
  56.3 13.2 %collective-permute-start.5 = (f32[216,8,128]{2,1,0:T(8,128)S(1)}, f32[216,8,128]{2,1,0:T(8,128)S(1)}, u32[]{:S(2)}, u32[]{:S(2)}) collective-permute-start(f32[216,8,128]{2,1,0:T(8,128)S(1)} %get-tuple-element.61), channel_id=1, source_target_pairs={{0,4},{1,3},{2,6},{3,1},{4,0},{5,7},{6,2},{7,5},{8,12},{9,11},{10,... | collective-permute-start | bytes 2654216 | tf_op jit(solution)/shard_map/ppermute | solution.py:503
  58.7 14.9 %collective-permute-start.7 = (f32[1,8,16,256]{3,2,1,0:T(8,128)S(1)}, f32[1,8,16,256]{3,2,1,0:T(8,128)S(1)}, u32[]{:S(2)}, u32[]{:S(2)}) collective-permute-start(f32[1,8,16,256]{3,2,1,0:T(8,128)S(1)} %bitcast.65), channel_id=1, source_target_pairs={{0,4},{4,8},{8,12},{12,16},{16,20},{20,24},{24,28},{1,5},{5,9},{9,... | collective-permute-start | bytes 393224 | tf_op jit(solution)/shard_map/ppermute | solution.py:363
  69.8 28.2 %collective-permute-start.11 = (f32[216,8,128]{2,1,0:T(8,128)S(1)}, f32[216,8,128]{2,1,0:T(8,128)S(1)}, u32[]{:S(2)}, u32[]{:S(2)}) collective-permute-start(f32[216,8,128]{2,1,0:T(8,128)S(1)} %get-tuple-element.59), channel_id=1, source_target_pairs={{0,2},{1,9},{2,0},{3,11},{4,6},{5,13},{6,4},{7,15},{8,10},{9,1},{1... | collective-permute-start | bytes 2654216 | tf_op jit(solution)/shard_map/ppermute | solution.py:503
  72.3 6.0 %collective-permute-start.8 = (f32[1,8,16,256]{3,2,1,0:T(8,128)S(1)}, f32[1,8,16,256]{3,2,1,0:T(8,128)S(1)}, u32[]{:S(2)}, u32[]{:S(2)}) collective-permute-start(f32[1,8,16,256]{3,2,1,0:T(8,128)S(1)} %bitcast.64), channel_id=1, source_target_pairs={{4,0},{8,4},{12,8},{16,12},{20,16},{24,20},{28,24},{5,1},{9,5},{13... | collective-permute-start | bytes 393224 | tf_op jit(solution)/shard_map/ppermute | solution.py:363
  78.4 14.1 %collective-permute-start.10 = (f32[10,1,16,256]{3,2,1,0:T(8,128)S(1)}, f32[10,1,16,256]{3,2,1,0:T(8,128)S(1)}, u32[]{:S(2)}, u32[]{:S(2)}) collective-permute-start(f32[10,1,16,256]{3,2,1,0:T(8,128)S(1)} %maximum_bitcast_fusion.3), channel_id=1, source_target_pairs={{1,0},{2,1},{3,2},{5,4},{6,5},{7,6},{9,8},{10,9},{11,10},{13,12},{... | collective-permute-start | bytes 491528 | tf_op jit(solution)/shard_map/ppermute | solution.py:371
  83.3 9.1 %collective-permute-start.9 = (f32[10,1,16,256]{3,2,1,0:T(8,128)S(1)}, f32[10,1,16,256]{3,2,1,0:T(8,128)S(1)}, u32[]{:S(2)}, u32[]{:S(2)}) collective-permute-start(f32[10,1,16,256]{3,2,1,0:T(8,128)S(1)} %maximum_bitcast_fusion.2), channel_id=1, source_target_pairs={{0,1},{1,2},{2,3},{4,5},{5,6},{6,7},{8,9},{9,10},{10,11},{12,13},{... | collective-permute-start | bytes 491528 | tf_op jit(solution)/shard_map/ppermute | solution.py:371
  85.4 15.3 %collective-permute-start.12 = (f32[108,8,128]{2,1,0:T(8,128)S(1)}, f32[108,8,128]{2,1,0:T(8,128)S(1)}, u32[]{:S(2)}, u32[]{:S(2)}) collective-permute-start(f32[108,8,128]{2,1,0:T(8,128)S(1)} %get-tuple-element.63), channel_id=1, source_target_pairs={{0,2},{1,5},{2,0},{3,7},{4,6},{5,1},{6,4},{7,3},{8,10},{9,13},{10,... | collective-permute-start | bytes 1327112 | tf_op jit(solution)/shard_map/ppermute | solution.py:503
  98.2 13.1 %collective-permute-start.13 = (f32[108,8,128]{2,1,0:T(8,128)S(1)}, f32[108,8,128]{2,1,0:T(8,128)S(1)}, u32[]{:S(2)}, u32[]{:S(2)}) collective-permute-start(f32[108,8,128]{2,1,0:T(8,128)S(1)} %get-tuple-element.65), channel_id=1, source_target_pairs={{0,4},{1,17},{2,6},{3,19},{4,0},{5,21},{6,2},{7,23},{8,12},{9,25},... | collective-permute-start | bytes 1327112 | tf_op jit(solution)/shard_map/ppermute | solution.py:503
  100.8 16.2 %collective-permute-start.14 = (f32[54,8,128]{2,1,0:T(8,128)S(1)}, f32[54,8,128]{2,1,0:T(8,128)S(1)}, u32[]{:S(2)}, u32[]{:S(2)}) collective-permute-start(f32[54,8,128]{2,1,0:T(8,128)S(1)} %get-tuple-element.73), channel_id=1, source_target_pairs={{0,8},{1,9},{2,10},{3,11},{4,12},{5,13},{6,14},{7,15},{8,0},{9,1},... | collective-permute-start | bytes 663560 | tf_op jit(solution)/shard_map/ppermute | solution.py:503
  111.3 8.1 %collective-permute-start.15 = (f32[54,8,128]{2,1,0:T(8,128)S(1)}, f32[54,8,128]{2,1,0:T(8,128)S(1)}, u32[]{:S(2)}, u32[]{:S(2)}) collective-permute-start(f32[54,8,128]{2,1,0:T(8,128)S(1)} %get-tuple-element.75), channel_id=1, source_target_pairs={{0,8},{1,5},{2,10},{3,7},{4,12},{5,1},{6,14},{7,3},{8,0},{9,13},{1... | collective-permute-start | bytes 663560 | tf_op jit(solution)/shard_map/ppermute | solution.py:503
  117.1 6.7 %collective-permute-start.16 = (f32[27,8,128]{2,1,0:T(8,128)S(1)}, f32[27,8,128]{2,1,0:T(8,128)S(1)}, u32[]{:S(2)}, u32[]{:S(2)}) collective-permute-start(f32[27,8,128]{2,1,0:T(8,128)S(1)} %get-tuple-element.77), channel_id=1, source_target_pairs={{0,16},{1,17},{2,18},{3,19},{4,20},{5,21},{6,22},{7,23},{8,24},{9,... | collective-permute-start | bytes 331784 | tf_op jit(solution)/shard_map/ppermute | solution.py:503
  119.5 5.6 %collective-permute-start.17 = (f32[27,8,128]{2,1,0:T(8,128)S(1)}, f32[27,8,128]{2,1,0:T(8,128)S(1)}, u32[]{:S(2)}, u32[]{:S(2)}) collective-permute-start(f32[27,8,128]{2,1,0:T(8,128)S(1)} %get-tuple-element.79), channel_id=1, source_target_pairs={{0,16},{1,3},{2,18},{3,1},{4,20},{5,7},{6,22},{7,5},{8,24},{9,11},... | collective-permute-start | bytes 331784 | tf_op jit(solution)/shard_map/ppermute | solution.py:503
